TPU v7x, 32 devices: a whole 2x2x4 slice. The times are simulated.
32 devices in a mesh: dp: 16 (over z, y, x), group: 2 (over core).
Axes of the slice: x: 2, y: 2, z: 4, core: 2. Of those that a mesh axis runs over, the one named last changes fastest.
Arguments:
- tokens: bfloat16 [32, 512, 768], P('group', 'dp'), may hold values from -6 to 6
- memory: bfloat16 [32, 512, 768], P('group', 'dp'), may hold values from -6 to 6
- segments: int32 [32, 512], P('group', 'dp'), may hold values from 0 to 3, never falling along the last dimension, each value on 1 to 256 neighbouring positions
- memory_segments: int32 [32, 512], P('group', 'dp'), may hold values from 0 to 3, never falling along the last dimension, each value on 1 to 256 neighbouring positions
- row_source: int32 [32], replicated, may hold values from 0 to 31, as said below
- denoiser_modes: int32 [32], replicated, may hold values from 0 to 2, as said below
- sentinel: int32 [32, 512], P(('dp', 'group')), may hold values 0 or 1
- cotangent: bfloat16 [32, 512, 768], P(('dp', 'group')), may hold values from -6 to 6
- w_in: float32 [768, 8704], P(None, ('dp', 'group')), may hold values from -0.21875 to 0.21875
- w_out: float32 [3584, 768], P(('dp', 'group')), may hold values from -0.625 to 0.625
- norm_gains: float32 [3, 768], replicated, may hold values from 0.5 to 1.5
- rel_bias: float32 [3, 32, 12], replicated, may hold values from -4 to 4
- rows_in: float32 [3, 768], replicated, may hold values from 1024 to 16384
- cols_in: float32 [8704], P(('dp', 'group')), may hold values from 1024 to 16384
- rows_out: float32 [3584], P(('dp', 'group')), may hold values from 1024 to 16384
- cols_out: float32 [3, 768], replicated, may hold values from 1024 to 16384
- sq_gains: float32 [3, 768], replicated, may hold values from 1024 to 16384
- sq_rel: float32 [3, 32, 12], replicated, may hold values from 1024 to 16384
Outputs:
- mixed: bfloat16 [32, 512, 768], P(('dp', 'group'))
- d_tokens: bfloat16 [32, 512, 768], P('group', 'dp')
- d_memory: bfloat16 [32, 512, 768], P('group', 'dp')
- grad_in: float32 [768, 8704], P(None, ('dp', 'group'))
- grad_out: float32 [3584, 768], P(('dp', 'group'))
- grad_gains: float32 [3, 768], replicated
- grad_rel: float32 [3, 32, 12], replicated
- new_in: float32 [768, 8704], P(None, ('dp', 'group'))
- new_out: float32 [3584, 768], P(('dp', 'group'))
- new_gains: float32 [3, 768], replicated
- new_rel: float32 [3, 32, 12], replicated
- rows_in_new: float32 [3, 768], replicated
- cols_in_new: float32 [8704], P(('dp', 'group'))
- rows_out_new: float32 [3584], P(('dp', 'group'))
- cols_out_new: float32 [3, 768], replicated
- sq_gains_new: float32 [3, 768], replicated
- sq_rel_new: float32 [3, 32, 12], replicated
Inputs may be any that keep to these rules, and one draw needn't show every extreme that they name: row_source is a permutation of the rows; its entry at q = (i * 2 + g) + k, for index i of dp, g of group and k below 1, is a row of half g, from g * 16 to (g + 1) * 16 - 1. `denoiser_modes`: the rows that row_source places at one index i of dp, for both indices of group, share one mode. `segments`: every row holds each number 0 to 3, never falling along the row. `memory_segments`: every row holds each number 0 to 3, never falling along the row.
All inputs are finite; a program needn't handle non-finite values. No bound on the sum of `sentinel` on one device may be relied on, other than what follows from the above.
Results may differ from a plain program's by a relative error of at most 0.02.
Values may be sent and summed in bfloat16 or wider, within the bound.
A program may use at most 320 MiB of HBM per device.

v0:
```python
import jax
import jax.numpy as jnp
import numpy as np
from jax import lax
from jax.sharding import PartitionSpec as P

HEADS = 12
HSIZE = 64
FF = 2048
BUCKETS = 32
MODES = 3
SEQ = 512


EPSILON = 1e-06
MASKED = -1e30
DECAY_RATE = 0.9
STEP_SIZE = 0.01
PLAIN_STEP = 0.15
PRECISE = lax.Precision.HIGHEST


def bucket_table(length, buckets):
    exact_span = buckets // 2
    distances = np.arange(length)
    safe_spans = np.maximum(distances, 1)
    logged = np.floor(
        np.log(safe_spans / exact_span) / np.log(128.0 / exact_span) * (buckets - exact_span)
    )
    far_bucket = np.minimum(exact_span + logged, buckets - 1)
    return np.where(distances < exact_span, distances, far_bucket).astype(np.int32)


def rms_norm(values, gain_vec):
    return (
        values * lax.rsqrt(jnp.mean(values * values, axis=-1, keepdims=True) + EPSILON) * gain_vec
    )


def gelu_tanh(values):
    return jax.nn.gelu(values, approximate=True)


def project(values, matrix):
    return jnp.einsum("rlk,kn->rln", values, matrix, preferred_element_type=jnp.float32)


def project_back(grad_rows, matrix):
    return jnp.einsum("rln,kn->rlk", grad_rows, matrix, preferred_element_type=jnp.float32)


def weight_grad(values, grad_rows):
    return jnp.einsum("rlk,rln->kn", values, grad_rows, preferred_element_type=jnp.float32)


def spread_bias(by_dist):
    length = by_dist.shape[0]
    heads = by_dist.shape[1]
    reversed_rows = jnp.concatenate(
        [by_dist[::-1].T, jnp.zeros((heads, length), jnp.float32)], axis=1
    )
    repeated = jnp.tile(reversed_rows, (1, length))
    window = repeated[:, length - 1 : length - 1 + length * (2 * length - 1)]
    return window.reshape(heads, length, 2 * length - 1)[:, :, :length]


def collect_bias(d_scores):
    heads = d_scores.shape[0]
    length = d_scores.shape[1]
    widened = jnp.concatenate(
        [d_scores, jnp.zeros((heads, length, length - 1), jnp.float32)], axis=2
    )
    flat = widened.reshape(heads, length * (2 * length - 1))
    flat = jnp.concatenate(
        [jnp.zeros((heads, length - 1), jnp.float32), flat, jnp.zeros((heads, 1), jnp.float32)],
        axis=1,
    )
    summed = jnp.sum(flat.reshape(heads, length, 2 * length), axis=1)
    return summed[:, :length][:, ::-1].T


def scores_of(query, key_part, allowed, bias_rows):
    scores = (
        jnp.einsum("qhe,khe->hqk", query, key_part, preferred_element_type=jnp.float32)
        * HSIZE ** (-0.5)
        + bias_rows
    )
    return jnp.where(allowed[None], scores, MASKED)


def attend_forward(query, key_part, value_part, allowed, bias_rows):
    scores = scores_of(query, key_part, allowed, bias_rows)
    row_top = jnp.max(scores, axis=-1, keepdims=True)
    raised = jnp.exp(scores - row_top)
    row_total = jnp.sum(raised, axis=-1, keepdims=True)
    weights = (raised / row_total).astype(jnp.bfloat16)
    result = jnp.einsum("hqk,khe->qhe", weights, value_part, preferred_element_type=jnp.float32)
    return (result, row_top + jnp.log(row_total))


def attend_backward(query, key_part, value_part, allowed, bias_rows, log_total, grad_out):
    scores = scores_of(query, key_part, allowed, bias_rows)
    weights_f = jnp.exp(scores - log_total)
    d_value = jnp.einsum(
        "hqk,qhe->khe", weights_f.astype(jnp.bfloat16), grad_out, preferred_element_type=jnp.float32
    )
    d_weights = jnp.einsum("qhe,khe->hqk", grad_out, value_part, preferred_element_type=jnp.float32)
    d_scores = weights_f * (d_weights - jnp.sum(weights_f * d_weights, axis=-1, keepdims=True))
    d_scores = d_scores.astype(jnp.bfloat16)
    inv_root = HSIZE ** (-0.5)
    d_query = (
        jnp.einsum("hqk,khe->qhe", d_scores, key_part, preferred_element_type=jnp.float32)
        * inv_root
    )
    d_key = (
        jnp.einsum("hqk,qhe->khe", d_scores, query, preferred_element_type=jnp.float32) * inv_root
    )
    return (d_query, d_key, d_value, d_scores)


def body(
    tokens,
    memory,
    segments,
    memory_segments,
    row_source,
    denoiser_modes,
    sentinel,
    cotangent,
    w_in,
    w_out,
    norm_gains,
    rel_bias,
    rows_in,
    cols_in,
    rows_out,
    cols_out,
    sq_gains,
    sq_rel,
):
    head_cols = HEADS * HSIZE
    n_index = lax.axis_size("dp")
    n_group = lax.axis_size("group")
    my_group = lax.axis_index("group")
    my_place = lax.axis_index(("dp", "group"))
    half_rows = tokens.shape[0]
    rows_dev = cotangent.shape[0]
    width = tokens.shape[2]
    slot_table = row_source.reshape(n_index, n_group, rows_dev)
    sources = (
        lax.dynamic_index_in_dim(slot_table, my_group, 1, keepdims=False).reshape(-1)
        - my_group * half_rows
    )
    own_rows = lax.dynamic_index_in_dim(
        row_source.reshape(n_index * n_group, rows_dev), my_place, 0, keepdims=False
    )
    own_modes = jnp.take(denoiser_modes, own_rows, axis=0)
    sending = (tokens[sources], memory[sources], segments[sources], memory_segments[sources])
    tok_rows, mem_rows, seg_rows, mseg_rows = (
        lax.all_to_all(sending[0], "dp", split_axis=0, concat_axis=1, tiled=True),
        lax.all_to_all(sending[1], "dp", split_axis=0, concat_axis=1, tiled=True),
        lax.all_to_all(sending[2], "dp", split_axis=0, concat_axis=1, tiled=True),
        lax.all_to_all(sending[3], "dp", split_axis=0, concat_axis=1, tiled=True),
    )
    w_in_all, w_out_all = (
        lax.all_gather(w_in.astype(jnp.bfloat16), ("dp", "group"), axis=1, tiled=True),
        lax.all_gather(w_out.astype(jnp.bfloat16), ("dp", "group"), axis=0, tiled=True),
    )
    bucket_hot = jnp.asarray(
        (bucket_table(SEQ, BUCKETS)[:, None] == np.arange(BUCKETS)[None, :]).astype(np.float32)
    )
    causal = jnp.asarray(np.tril(np.ones((SEQ, SEQ), dtype=bool)))
    mode_hot = (own_modes[:, None] == jnp.arange(MODES)[None, :]).astype(jnp.float32)
    rel_rows = jnp.einsum("rm,mbh->rbh", mode_hot, rel_bias, precision=PRECISE)

    def bias_of(rel_row):
        return spread_bias(jnp.dot(bucket_hot, rel_row, precision=PRECISE))

    x_zero = tok_rows.astype(jnp.float32)
    a_one = rms_norm(x_zero, norm_gains[0]).astype(jnp.bfloat16)
    qkv_rows = (
        project(a_one, w_in_all[:, : 3 * head_cols])
        .astype(jnp.bfloat16)
        .reshape(rows_dev, SEQ, 3, HEADS, HSIZE)
    )

    def self_forward(packed):
        qkv_row, seg_row, rel_row = packed
        allowed = causal & (seg_row[:, None] == seg_row[None, :])
        result, log_total = attend_forward(
            qkv_row[:, 0], qkv_row[:, 1], qkv_row[:, 2], allowed, bias_of(rel_row)
        )
        return (result.reshape(SEQ, head_cols).astype(jnp.bfloat16), log_total)

    att_one, lse_one = lax.map(self_forward, (qkv_rows, seg_rows, rel_rows))
    x_one = x_zero + project(att_one, w_out_all[:head_cols])
    a_two = rms_norm(x_one, norm_gains[1]).astype(jnp.bfloat16)
    q_cross = (
        project(a_two, w_in_all[:, 3 * head_cols : 4 * head_cols])
        .astype(jnp.bfloat16)
        .reshape(rows_dev, SEQ, HEADS, HSIZE)
    )
    kv_cross = (
        project(mem_rows, w_in_all[:, 4 * head_cols : 6 * head_cols])
        .astype(jnp.bfloat16)
        .reshape(rows_dev, SEQ, 2, HEADS, HSIZE)
    )

    def cross_forward(packed):
        query, kv_row, seg_row, mseg_row = packed
        allowed = seg_row[:, None] == mseg_row[None, :]
        result, log_total = attend_forward(query, kv_row[:, 0], kv_row[:, 1], allowed, 0.0)
        return (result.reshape(SEQ, head_cols).astype(jnp.bfloat16), log_total)

    att_two, lse_two = lax.map(cross_forward, (q_cross, kv_cross, seg_rows, mseg_rows))
    x_two = x_one + project(att_two, w_out_all[head_cols : 2 * head_cols])
    a_three = rms_norm(x_two, norm_gains[2]).astype(jnp.bfloat16)
    gate_up = project(a_three, w_in_all[:, 6 * head_cols :])
    gate_part = gate_up[..., :FF]
    up_part = gate_up[..., FF:]
    gelu_gate, gelu_pull = jax.vjp(gelu_tanh, gate_part)
    hidden = (gelu_gate * up_part).astype(jnp.bfloat16)
    mixed = (x_two + project(hidden, w_out_all[2 * head_cols :])).astype(jnp.bfloat16)
    kept = (1 - sentinel).astype(jnp.float32)
    grad_res = cotangent.astype(jnp.float32) * kept[:, :, None]
    grad_low = grad_res.astype(jnp.bfloat16)
    g_down = weight_grad(hidden, grad_low)
    d_hidden = project_back(grad_low, w_out_all[2 * head_cols :])
    d_gate = gelu_pull(d_hidden * up_part)[0]
    d_gate_up = jnp.concatenate([d_gate, d_hidden * gelu_gate], axis=-1).astype(jnp.bfloat16)
    g_gate_up = weight_grad(a_three, d_gate_up)
    d_a_three = project_back(d_gate_up, w_in_all[:, 6 * head_cols :])
    _, norm_pull = jax.vjp(rms_norm, x_two, norm_gains[2])
    d_part, d_gain_three = norm_pull(d_a_three)
    grad_res = grad_res + d_part
    grad_low = grad_res.astype(jnp.bfloat16)
    g_out_cross = weight_grad(att_two, grad_low)
    d_att_two = (
        project_back(grad_low, w_out_all[head_cols : 2 * head_cols])
        .astype(jnp.bfloat16)
        .reshape(rows_dev, SEQ, HEADS, HSIZE)
    )

    def cross_backward(packed):
        query, kv_row, seg_row, mseg_row, log_total, grad_out = packed
        allowed = seg_row[:, None] == mseg_row[None, :]
        d_query, d_key, d_value, _ = attend_backward(
            query, kv_row[:, 0], kv_row[:, 1], allowed, 0.0, log_total, grad_out
        )
        return (
            d_query.reshape(SEQ, head_cols),
            jnp.stack([d_key, d_value], axis=1).reshape(SEQ, 2 * head_cols),
        )

    d_q_cross, d_kv_cross = lax.map(
        cross_backward, (q_cross, kv_cross, seg_rows, mseg_rows, lse_two, d_att_two)
    )
    d_q_cross = d_q_cross.astype(jnp.bfloat16)
    d_kv_cross = d_kv_cross.astype(jnp.bfloat16)
    g_q_cross = weight_grad(a_two, d_q_cross)
    g_kv_cross = weight_grad(mem_rows, d_kv_cross)
    d_memory = project_back(d_kv_cross, w_in_all[:, 4 * head_cols : 6 * head_cols]).astype(
        jnp.bfloat16
    )
    d_a_two = project_back(d_q_cross, w_in_all[:, 3 * head_cols : 4 * head_cols])
    _, norm_pull = jax.vjp(rms_norm, x_one, norm_gains[1])
    d_part, d_gain_two = norm_pull(d_a_two)
    grad_res = grad_res + d_part
    grad_low = grad_res.astype(jnp.bfloat16)
    g_out_self = weight_grad(att_one, grad_low)
    d_att_one = (
        project_back(grad_low, w_out_all[:head_cols])
        .astype(jnp.bfloat16)
        .reshape(rows_dev, SEQ, HEADS, HSIZE)
    )

    def self_backward(packed):
        qkv_row, seg_row, rel_row, log_total, grad_out = packed
        allowed = causal & (seg_row[:, None] == seg_row[None, :])
        d_query, d_key, d_value, d_scores = attend_backward(
            qkv_row[:, 0],
            qkv_row[:, 1],
            qkv_row[:, 2],
            allowed,
            bias_of(rel_row),
            log_total,
            grad_out,
        )
        by_dist = collect_bias(d_scores.astype(jnp.float32))
        d_rel_row = jnp.dot(bucket_hot.T, by_dist, precision=PRECISE)
        return (jnp.stack([d_query, d_key, d_value], axis=1).reshape(SEQ, 3 * head_cols), d_rel_row)

    d_qkv, d_rel_rows = lax.map(self_backward, (qkv_rows, seg_rows, rel_rows, lse_one, d_att_one))
    d_qkv = d_qkv.astype(jnp.bfloat16)
    g_qkv = weight_grad(a_one, d_qkv)
    d_a_one = project_back(d_qkv, w_in_all[:, : 3 * head_cols])
    _, norm_pull = jax.vjp(rms_norm, x_zero, norm_gains[0])
    d_part, d_gain_one = norm_pull(d_a_one)
    d_tokens = (grad_res + d_part).astype(jnp.bfloat16)
    d_rel = jnp.einsum("rm,rbh->mbh", mode_hot, d_rel_rows, precision=PRECISE)
    back_tok, back_mem = (
        lax.all_to_all(d_tokens, "dp", split_axis=1, concat_axis=0, tiled=True),
        lax.all_to_all(d_memory, "dp", split_axis=1, concat_axis=0, tiled=True),
    )
    inverse = jnp.argsort(sources)
    d_tokens_out = back_tok[inverse]
    d_memory_out = back_mem[inverse]
    g_in = jnp.concatenate([g_qkv, g_q_cross, g_kv_cross, g_gate_up], axis=1)
    g_out = jnp.concatenate([g_out_self, g_out_cross, g_down], axis=0)
    split_in = g_in.reshape(width, n_index, n_group, -1)
    split_out = g_out.reshape(n_index, n_group, -1, width)
    part_in, part_out = (
        lax.psum_scatter(
            split_in.astype(jnp.bfloat16), "group", scatter_dimension=2, tiled=True
        ).astype(jnp.float32),
        lax.psum_scatter(
            split_out.astype(jnp.bfloat16), "group", scatter_dimension=1, tiled=True
        ).astype(jnp.float32),
    )
    part_in, part_out = (
        lax.psum_scatter(part_in, "dp", scatter_dimension=1, tiled=True),
        lax.psum_scatter(part_out, "dp", scatter_dimension=0, tiled=True),
    )
    part_in = part_in.reshape(width, -1)
    part_out = part_out.reshape(-1, width)
    col_count = part_in.shape[1]
    col_ids = my_place * col_count + jnp.arange(col_count)
    col_hot = jnp.stack(
        [
            col_ids < 3 * head_cols,
            (col_ids >= 3 * head_cols) & (col_ids < 6 * head_cols),
            col_ids >= 6 * head_cols,
        ],
        axis=0,
    ).astype(jnp.float32)
    sq_in = part_in * part_in
    row_terms = jnp.einsum("mc,dc->md", col_hot, sq_in, precision=PRECISE)
    row_count = part_out.shape[0]
    row_ids = my_place * row_count + jnp.arange(row_count)
    row_hot = jnp.stack(
        [
            row_ids < head_cols,
            (row_ids >= head_cols) & (row_ids < 2 * head_cols),
            row_ids >= 2 * head_cols,
        ],
        axis=0,
    ).astype(jnp.float32)
    sq_out = part_out * part_out
    rows_out_new = DECAY_RATE * rows_out + (1 - DECAY_RATE) * jnp.mean(sq_out, axis=1)
    col_terms = jnp.einsum("mr,rd->md", row_hot, sq_out, precision=PRECISE)
    row_totals = jnp.dot(row_hot, rows_out_new, precision=PRECISE)
    gain_grads = jnp.stack([d_gain_one, d_gain_two, d_gain_three], axis=0)
    row_sums, col_sums, total_sums, g_gains, g_rel = lax.psum(
        (row_terms, col_terms, row_totals, gain_grads, d_rel), ("dp", "group")
    )
    in_counts = jnp.array([3 * head_cols, 3 * head_cols, 2 * FF], jnp.float32)
    out_counts = jnp.array([head_cols, head_cols, FF], jnp.float32)
    rows_in_new = DECAY_RATE * rows_in + (1 - DECAY_RATE) * row_sums / in_counts[:, None]
    cols_in_new = DECAY_RATE * cols_in + (1 - DECAY_RATE) * jnp.mean(sq_in, axis=0)
    row_scaled = rows_in_new / jnp.mean(rows_in_new, axis=1, keepdims=True)
    in_scale = (
        jnp.einsum("mc,md->dc", col_hot, row_scaled, precision=PRECISE) * cols_in_new[None, :]
    )
    new_in = w_in - STEP_SIZE * part_in * lax.rsqrt(in_scale)
    cols_out_new = DECAY_RATE * cols_out + (1 - DECAY_RATE) * col_sums / out_counts[:, None]
    row_mean = jnp.dot(row_hot.T, total_sums / out_counts, precision=PRECISE)
    col_pick = jnp.einsum("mr,md->rd", row_hot, cols_out_new, precision=PRECISE)
    new_out = w_out - STEP_SIZE * part_out * lax.rsqrt(
        (rows_out_new / row_mean)[:, None] * col_pick
    )
    sq_gains_new = DECAY_RATE * sq_gains + (1 - DECAY_RATE) * g_gains * g_gains
    new_gains = norm_gains - PLAIN_STEP * g_gains * lax.rsqrt(sq_gains_new)
    sq_rel_new = DECAY_RATE * sq_rel + (1 - DECAY_RATE) * g_rel * g_rel
    new_rel = rel_bias - PLAIN_STEP * g_rel * lax.rsqrt(sq_rel_new)
    return (
        mixed,
        d_tokens_out,
        d_memory_out,
        part_in,
        part_out,
        g_gains,
        g_rel,
        new_in,
        new_out,
        new_gains,
        new_rel,
        rows_in_new,
        cols_in_new,
        rows_out_new,
        cols_out_new,
        sq_gains_new,
        sq_rel_new,
    )


def solution(mesh):
    return jax.shard_map(
        body,
        mesh=mesh,
        in_specs=(
            P("group", "dp", None),
            P("group", "dp", None),
            P("group", "dp"),
            P("group", "dp"),
            P(),
            P(),
            P(("dp", "group"), None),
            P(("dp", "group"), None, None),
            P(None, ("dp", "group")),
            P(("dp", "group"), None),
            P(),
            P(),
            P(),
            P(("dp", "group")),
            P(("dp", "group")),
            P(),
            P(),
            P(),
        ),
        out_specs=(
            P(("dp", "group"), None, None),
            P("group", "dp", None),
            P("group", "dp", None),
            P(None, ("dp", "group")),
            P(("dp", "group"), None),
            P(),
            P(),
            P(None, ("dp", "group")),
            P(("dp", "group"), None),
            P(),
            P(),
            P(),
            P(("dp", "group")),
            P(("dp", "group")),
            P(),
            P(),
            P(),
        ),
        check_vma=False,
    )
```

profile of v0, /device:TPU:0, one launch (start us, length us, event | category | flops | bytes accessed | tf_op | source)
XLA Modules:
  0.0 941.6 jit_solution(8088391880958749174)
XLA Ops:
  13.9 8.3 all-to-all-start.1
  24.1 5.5 all-to-all-done.1
  34.5 5.7 all-to-all-done.3
  48.6 11.6 %tile.24 = f32[12,512,1024]{2,1,0:T(8,128)} broadcast(f32[12,1024]{1,0:T(8,128)S(1)} %concatenate.34), dimensions={0,2} | broadcast | bytes 25214976 | tf_op jit(solution)/shard_map/while/body/eval_jaxpr/tile | solution.py:62
  60.2 10.9 %pad.34 = f32[16,512,1024]{2,1,0:T(8,128)S(1)} pad(f32[12,512,1024]{2,1,0:T(8,128)} %tile.24, f32[]{:T(128)} %constant.112.clone.1), padding=0_4x0_0x0_0 | pad | bytes 58720260
  71.1 39.7 %copy.136 = f32[2,8,512,1024]{3,1,2,0:T(8,128)} copy(f32[2,8,512,1024]{3,2,1,0:T(8,128)S(1)} %bitcast.249) | data formatting | bytes 67108864
  110.8 26.0 %slice.136 = f32[12,523776]{1,0:T(8,128)} slice(f32[12,524288]{1,0:T(8,128)} %bitcast.250), slice={[0:12], [511:524287]} | slice | bytes 50282496 | tf_op jit(solution)/shard_map/while/body/eval_jaxpr/slice | solution.py:63
  136.8 54.7 %reshape.621 = f32[12,512,1023]{2,1,0:T(8,128)} reshape(f32[12,523776]{1,0:T(8,128)} %slice.136) | data formatting | bytes 50282496 | tf_op jit(solution)/shard_map/while/body/eval_jaxpr/reshape | solution.py:64
  191.4 11.1 %slice.137 = f32[12,512,512]{2,1,0:T(8,128)} slice(f32[12,512,1023]{2,1,0:T(8,128)} %reshape.621), slice={[0:12], [0:512], [0:512]} | slice | bytes 25165824 | tf_op jit(solution)/shard_map/while/body/eval_jaxpr/slice | solution.py:64
  202.5 12.8 %copy.135 = f32[12,512,512]{1,2,0:T(8,128)} copy(f32[12,512,512]{2,1,0:T(8,128)} %slice.137) | data formatting | bytes 25165824
  220.0 6.4 all-to-all-start.2
  228.1 5.4 convolution_convert_fusion.2
  236.4 6.3 fusion.135
  258.5 4.7 convolution_convert_fusion.5
  273.7 5.0 fusion.64
  281.3 6.2 convolution_bitcast_fusion
  287.5 5.8 fusion.33
  293.3 8.5 multiply_reduce_fusion.2
  306.6 11.6 %multiply_reduce_fusion.1 = (f32[12,512]{1,0:T(8,128)S(1)}, f32[12,512,512]{1,2,0:T(8,128)}) fusion(f32[12,512]{1,0:T(8,128)S(1)} %log_add_fusion.1, f32[12,512,512]{1,2,0:T(8,128)} %copy-done.3, pred[512,512]{0,1:T(8,128)(4,1)S(1)} %get-tuple-element.159, bf16[512,12,64]{0,2,1:T(8,128)(2,1)S(1)} %bitcast.281, bf16[512,2,12,64]{0,3,2,1:T(8,128)(2,1)} %bitcast.266), kind=kOutput, calls=%fused_computation.13 | convolution fusion | flops 418375680 | bytes 27049984 | tf_op jit(solution)/shard_map/while/body/eval_jaxpr/qhe,khe->hqk/dot_general | solution.py:107
  319.7 7.1 multiply_convert_fusion.1
  338.7 7.7 fusion.56
  346.4 9.0 multiply_reduce_fusion
  355.4 11.0 %multiply_convert_fusion = bf16[12,512,512]{1,2,0:T(8,128)(2,1)} fusion(f32[12,512,512]{1,2,0:T(8,128)} %get-tuple-element.174, f32[12,512,512]{1,2,0:T(8,128)S(1)} %bitcast.244, f32[12,512]{1,0:T(8,128)S(1)} %get-tuple-element.173, f32[12,512]{1,0:T(8,128)S(1)} %log_add_fusion), kind=kLoop, calls=%fused_computation.9 | loop fusion | flops 12582912 | bytes 31506432 | tf_op jit(solution)/shard_map/while/body/eval_jaxpr/convert_element_type | solution.py:109
  366.4 5.8 multiply_bitcast_fusion.1
  372.2 4.9 multiply_bitcast_fusion.2
  383.1 5.6 convolution_convert_fusion
  395.6 4.1 convolution_convert_fusion.4
  407.5 5.3 pad_maximum_fusion
  412.9 18.1 %copy.117 = bf16[768,8704]{0,1:T(8,128)(2,1)} copy(bf16[768,8704]{1,0:T(8,128)(2,1)} %pad_maximum_fusion) | data formatting | bytes 26738688 | tf_op jit(solution)/shard_map/concatenate | solution.py:308
  431.0 3.7 convolution_convert_fusion.3
  438.9 64.0 %all-reduce.8.cloned.1.call-done = (bf16[768,16,2,272]{0,3,2,1:T(8,128)(2,1)}, bf16[16,2,112,768]{3,2,1,0:T(8,128)(2,1)}) async-done(((bf16[768,16,2,272]{0,3,2,1:T(8,128)(2,1)}, bf16[16,2,112,768]{3,2,1,0:T(8,128)(2,1)}), (bf16[768,16,2,272]{0,3,2,1:T(8,128)(2,1)}, bf16[16,2,112,768]{3,2,1,0:T(8,128)(2,1)})) %all-reduce.8.cloned.1.call-update) | async-done | bytes 18874384
  502.9 5.3 dynamic-slice_convert_fusion.1
  508.3 9.6 %dynamic-slice_convert_fusion = f32[768,16,1,272]{0,3,2,1:T(8,128)} fusion(bf16[768,16,2,272]{0,3,2,1:T(8,128)(2,1)} %get-tuple-element.146, u32[]{:T(128)} %bitcast.88), kind=kLoop, calls=%fused_computation.26 | loop fusion | flops 3342336 | bytes 20054020 | tf_op jit(solution)/shard_map/convert_element_type | solution.py:315
  521.6 5.1 fusion.47
  528.9 5.4 reduce.37
  535.4 7.1 all-to-all-start.4
  542.6 3.7 fusion.69
  547.5 5.4 reduce.38
  554.0 14.7 %pad_convert_fusion = f32[12,512,1023]{1,2,0:T(8,128)} fusion(bf16[12,512,512]{1,2,0:T(8,128)(2,1)} %multiply_convert_fusion), kind=kLoop, calls=%fused_computation.8 | loop fusion | flops 6285312 | bytes 31432704 | tf_op jit(solution)/shard_map/while/body/eval_jaxpr/reshape | solution.py:73
  568.7 24.9 %copy.118 = f32[12,512,1023]{2,1,0:T(8,128)} copy(f32[12,512,1023]{1,2,0:T(8,128)} %pad_convert_fusion) | data formatting | bytes 50282496 | tf_op jit(solution)/shard_map/while/body/eval_jaxpr/reshape | solution.py:73
  593.6 38.7 %reshape.654 = f32[12,523776]{1,0:T(8,128)} reshape(f32[12,512,1023]{2,1,0:T(8,128)} %copy.118) | data formatting | bytes 50282496 | tf_op jit(solution)/shard_map/while/body/eval_jaxpr/reshape | solution.py:73
  632.3 90.7 %dynamic-update-slice.2 = f32[12,524288]{1,0:T(8,128)} dynamic-update-slice(f32[12,524288]{1,0:T(8,128)} %dynamic-update-slice.1, f32[12,523776]{1,0:T(8,128)} %reshape.654, s32[]{} %constant.271, s32[]{} %constant.272) | dynamic-update-slice | bytes 50282500
  724.3 32.3 %copy.137 = f32[2,8,512,1024]{3,2,1,0:T(8,128)} copy(f32[2,8,512,1024]{3,1,2,0:T(8,128)} %bitcast.255) | data formatting | bytes 67108864
  756.7 6.6 all-to-all-start.5
  763.3 9.7 %slice_reduce_fusion = f32[12,1024]{1,0:T(8,128)S(1)} fusion(f32[16,512,1024]{2,1,0:T(8,128)} %bitcast.251), kind=kLoop, calls=%fused_computation.6 | loop fusion | flops 6279168 | bytes 25214976 | tf_op jit(solution)/shard_map/while/body/eval_jaxpr/reduce_sum | solution.py:78
  773.7 5.3 fusion.72
  791.6 93.5 %reduce-scatter.9.cloned.1.call-done = f32[768,1,1,272]{0,3,2,1:T(8,128)} async-done(((f32[768,16,1,272]{0,3,2,1:T(8,128)}), f32[768,1,1,272]{0,3,2,1:T(8,128)}) %reduce-scatter.9.cloned.1.call-update) | async-done | bytes 835600 | tf_op jit(solution)/shard_map/reduce_scatter | solution.py:321
  886.8 41.3 %all-reduce.4 = (f32[3,768]{1,0:T(4,128)S(1)}, f32[3,32,12]{1,2,0:T(8,128)S(1)}, f32[3,768]{1,0:T(4,128)S(1)}, f32[3,768]{1,0:T(4,128)S(1)}, f32[3]{0:T(128)S(1)}) all-reduce(f32[3,768]{1,0:T(4,128)S(1)} %pad_maximum_fusion.5, f32[3,32,12]{1,2,0:T(8,128)S(1)} %broadcast_multiply_fusion, ...), channel_id=1, replica_groups=mesh['dp'=16,'group'=2] {'dp','group'}, use_global_device_ids=true, to_apply=%region_20.21 | all-reduce | flops 8067 | bytes 64536 | tf_op jit(solution)/shard_map/psum | solution.py:353
  (336 shorter events, 131.9 us)
Async XLA Ops:
  7.2 25.9 %copy-start = (bf16[16,32,768]{2,1,0:T(8,128)(2,1)S(1)}, bf16[16,32,768]{2,1,0:T(8,128)(2,1)}, u32[]{:S(2)}) copy-start(bf16[16,32,768]{2,1,0:T(8,128)(2,1)} %param.22) | copy-start | bytes 2359300
  7.2 40.7 %copy-start.40 = (f32[512,32]{1,0:T(8,128)S(1)}, f32[512,32]{1,0:T(8,128)}, u32[]{:S(2)}) copy-start(f32[512,32]{1,0:T(8,128)} %constant.215.clone) | copy-start | bytes 196612
  7.2 36.7 %copy-start.75 = (s32[32]{0:T(128)S(1)}, s32[32]{0:T(128)}, u32[]{:S(2)}) copy-start(s32[32]{0:T(128)} %param.26) | copy-start | bytes 388
  7.2 39.2 %copy-start.78 = (s32[32]{0:T(128)S(1)}, s32[32]{0:T(128)}, u32[]{:S(2)}) copy-start(s32[32]{0:T(128)} %param.27) | copy-start | bytes 388
  7.2 40.4 %copy-start.48 = (f32[3,32,12]{1,2,0:T(8,128)S(1)}, f32[3,32,12]{1,2,0:T(8,128)}, u32[]{:S(2)}) copy-start(f32[3,32,12]{1,2,0:T(8,128)} %param.33) | copy-start | bytes 13828
  7.3 220.9 %all-gather.3.cloned.1.call-start = ((), (), s32[]{:S(2)}) async-start(), calls=%async_computation.8 | async-start | bytes 13787136 | tf_op jit(solution)/shard_map/all_gather | solution.py:166
  9.4 241.1 %all-gather.5.cloned.1.call-start = ((), (), s32[]{:S(2)}) async-start(), calls=%async_computation.9 | async-start | bytes 5677056 | tf_op jit(solution)/shard_map/all_gather | solution.py:167
  12.0 35.6 %copy-start.76 = (s32[16]{0:T(128)}, s32[16]{0:T(128)S(1)}, u32[]{:S(2)}) copy-start(s32[16]{0:T(128)S(1)} %subtract_reduce_fusion) | copy-start | bytes 196
  13.9 15.7 %all-to-all-start.1 = ((s32[16,1,32]{2,1,0:T(1,128)}), s32[16,1,32]{2,1,0:T(1,128)S(1)}, u32[]{:S(2)}, u32[]{:S(2)}) async-start(s32[16,1,32]{2,1,0:T(1,128)} %bitcast.5), calls=%async_computation.1 | async-start | bytes 16384 | tf_op jit(solution)/shard_map/all_to_all | solution.py:162
  29.6 10.6 %all-to-all-start.3 = ((s32[16,1,32]{2,1,0:T(1,128)}), s32[16,1,32]{2,1,0:T(1,128)S(1)}, u32[]{:S(2)}, u32[]{:S(2)}) async-start(s32[16,1,32]{2,1,0:T(1,128)} %bitcast.19), calls=%async_computation.3 | async-start | bytes 16384 | tf_op jit(solution)/shard_map/all_to_all | solution.py:163
  40.2 179.7 %all-to-all-start = ((bf16[16,32,768]{2,1,0:T(8,128)(2,1)}), bf16[16,32,768]{2,1,0:T(8,128)(2,1)S(1)}, u32[]{:S(2)}, u32[]{:S(2)}) async-start(bf16[16,32,768]{2,1,0:T(8,128)(2,1)} %gather_fusion), calls=%async_computation | async-start | bytes 1572864 | tf_op jit(solution)/shard_map/all_to_all | solution.py:160
  202.5 12.8 %copy-start.45 = (bf16[16,32,768]{2,1,0:T(8,128)(2,1)S(1)}, bf16[16,32,768]{2,1,0:T(8,128)(2,1)}, u32[]{:S(2)}) copy-start(bf16[16,32,768]{2,1,0:T(8,128)(2,1)} %param.23) | copy-start | bytes 2359300
  202.5 14.2 %copy-start.54 = (f32[3,768]{1,0:T(4,128)S(1)}, f32[3,768]{1,0:T(4,128)}, u32[]{:S(2)}) copy-start(f32[3,768]{1,0:T(4,128)} %param.32) | copy-start | bytes 27652
  202.5 14.3 %copy-start.72 = (s32[1,512]{1,0:T(1,128)S(1)}, s32[1,512]{1,0:T(1,128)}, u32[]{:S(2)}) copy-start(s32[1,512]{1,0:T(1,128)} %param.28) | copy-start | bytes 6148
  202.5 16.3 %copy-start.47 = (pred[512,512]{0,1:T(32,128)(4,1)S(1)}, pred[512,512]{0,1:T(32,128)(4,1)}, u32[]{:S(2)}) copy-start(pred[512,512]{0,1:T(32,128)(4,1)} %constant.216.clone) | copy-start | bytes 786436
  216.8 16.7 %copy-start.50 = (f32[768]{0:T(1024)}, f32[768]{0:T(1024)S(1)}, u32[]{:S(2)}) copy-start(f32[768]{0:T(1024)S(1)} %get-tuple-element.140) | copy-start | bytes 9220
  220.0 30.5 %copy-start.5 = (bf16[16,32,768]{2,1,0:T(8,128)(2,1)}, bf16[16,32,768]{2,1,0:T(8,128)(2,1)S(1)}, u32[]{:S(2)}) copy-start(bf16[16,32,768]{2,1,0:T(8,128)(2,1)S(1)} %all-to-all-done) | copy-start | bytes 2359300
  220.0 38.5 %all-to-all-start.2 = ((bf16[16,32,768]{2,1,0:T(8,128)(2,1)}), bf16[16,32,768]{2,1,0:T(8,128)(2,1)}, u32[]{:S(2)}, u32[]{:S(2)}) async-start(bf16[16,32,768]{2,1,0:T(8,128)(2,1)} %gather_fusion.2), calls=%async_computation.2 | async-start | bytes 1572864 | tf_op jit(solution)/shard_map/all_to_all | solution.py:161
  226.4 276.5 %all-reduce.8.cloned.1.call-start = ((), (), s32[]{:S(2)}) async-start(), calls=%async_computation.12 | async-start | bytes 37748736
  281.2 20.6 %copy-start.16 = (f32[512,768]{1,0:T(8,128)}, f32[512,768]{1,0:T(8,128)S(1)}, u32[]{:S(2)}) copy-start(f32[512,768]{1,0:T(8,128)S(1)} %get-tuple-element.168) | copy-start | bytes 4718596
  306.6 11.7 %copy-start.28 = (bf16[512,768]{0,1:T(8,128)(2,1)}, bf16[512,768]{0,1:T(8,128)(2,1)S(1)}, u32[]{:S(2)}) copy-start(bf16[512,768]{0,1:T(8,128)(2,1)S(1)} %copy.106) | copy-start | bytes 2359300
  306.6 11.6 %slice-start.3 = ((s8[12582912]{0:T(1024)(128)(4,1)}), s8[4194304]{0:T(1024)(128)(4,1)S(1)}, s32[]{:S(2)}) async-start(s8[12582912]{0:T(1024)(128)(4,1)} %bitcast.245), calls=%async_computation.16 | async-start | bytes 8388608
  306.6 11.6 %slice-start.4 = ((s8[12582912]{0:T(1024)(128)(4,1)}), s8[4194304]{0:T(1024)(128)(4,1)S(1)}, s32[]{:S(2)}) async-start(s8[12582912]{0:T(1024)(128)(4,1)} %bitcast.245), calls=%async_computation.17 | async-start | bytes 8388608
  306.6 13.1 %slice-start.5 = ((s8[12582912]{0:T(1024)(128)(4,1)}), s8[4194304]{0:T(1024)(128)(4,1)S(1)}, s32[]{:S(2)}) async-start(s8[12582912]{0:T(1024)(128)(4,1)} %bitcast.245), calls=%async_computation.18 | async-start | bytes 8388608
  338.7 16.7 %slice-start = ((s8[12582912]{0:T(1024)(128)(4,1)}), s8[4194304]{0:T(1024)(128)(4,1)S(1)}, s32[]{:S(2)}) async-start(s8[12582912]{0:T(1024)(128)(4,1)} %bitcast.243), calls=%async_computation.13 | async-start | bytes 8388608
  338.7 16.6 %slice-start.1 = ((s8[12582912]{0:T(1024)(128)(4,1)}), s8[4194304]{0:T(1024)(128)(4,1)S(1)}, s32[]{:S(2)}) async-start(s8[12582912]{0:T(1024)(128)(4,1)} %bitcast.243), calls=%async_computation.14 | async-start | bytes 8388608
  355.4 21.8 %slice-start.6 = ((s8[12582912]{0:T(1024)(128)(4,1)}), s8[4194304]{0:T(1024)(128)(4,1)S(1)}, s32[]{:S(2)}) async-start(s8[12582912]{0:T(1024)(128)(4,1)} %bitcast.247), calls=%async_computation.19 | async-start | bytes 8388608
  355.4 21.8 %slice-start.7 = ((s8[12582912]{0:T(1024)(128)(4,1)}), s8[4194304]{0:T(1024)(128)(4,1)S(1)}, s32[]{:S(2)}) async-start(s8[12582912]{0:T(1024)(128)(4,1)} %bitcast.247), calls=%async_computation.20 | async-start | bytes 8388608
  366.4 10.8 %slice-start.8 = ((s8[12582912]{0:T(1024)(128)(4,1)}), s8[4194304]{0:T(1024)(128)(4,1)S(1)}, s32[]{:S(2)}) async-start(s8[12582912]{0:T(1024)(128)(4,1)} %bitcast.247), calls=%async_computation.21 | async-start | bytes 8388608
  412.9 18.1 %copy-start.43 = (bf16[1,512,768]{2,1,0:T(8,128)(2,1)S(1)}, bf16[1,512,768]{2,1,0:T(8,128)(2,1)}, u32[]{:S(2)}) copy-start(bf16[1,512,768]{2,1,0:T(8,128)(2,1)} %param.29) | copy-start | bytes 2359300
  437.7 351.4 %reduce-scatter.11.cloned.1.call-start = ((), (), s32[]{:S(2)}) async-start(), calls=%async_computation.11 | async-start | bytes 5849088 | tf_op jit(solution)/shard_map/reduce_scatter | solution.py:322
  508.2 376.9 %reduce-scatter.9.cloned.1.call-start = ((), (), s32[]{:S(2)}) async-start(), calls=%async_computation.10 | async-start | bytes 14204928 | tf_op jit(solution)/shard_map/reduce_scatter | solution.py:321
  535.4 221.3 %all-to-all-start.4 = ((bf16[16,2,12288]{2,1,0:T(2,128)(2,1)}), bf16[16,2,12288]{2,1,0:T(2,128)(2,1)S(1)}, u32[]{:S(2)}, u32[]{:S(2)}) async-start(bf16[16,2,12288]{2,1,0:T(2,128)(2,1)} %reshape.746), calls=%async_computation.4 | async-start | bytes 1572864 | tf_op jit(solution)/shard_map/all_to_all | solution.py:302
  756.7 26.5 %all-to-all-start.5 = ((bf16[16,2,12288]{2,1,0:T(2,128)(2,1)}), bf16[16,2,12288]{2,1,0:T(2,128)(2,1)S(1)}, u32[]{:S(2)}, u32[]{:S(2)}) async-start(bf16[16,2,12288]{2,1,0:T(2,128)(2,1)} %reshape.748), calls=%async_computation.5 | async-start | bytes 1572864 | tf_op jit(solution)/shard_map/all_to_all | solution.py:303
  763.3 10.5 %copy-start.18 = (f32[512,768]{1,0:T(8,128)S(1)}, f32[512,768]{1,0:T(8,128)}, u32[]{:S(2)}) copy-start(f32[512,768]{1,0:T(8,128)} %copy-done.16) | copy-start | bytes 4718596
  783.9 144.2 %copy-start.62 = (f32[3,768]{1,0:T(4,128)S(1)}, f32[3,768]{1,0:T(4,128)}, u32[]{:S(2)}) copy-start(f32[3,768]{1,0:T(4,128)} %param.34) | copy-start | bytes 27652
  783.9 144.2 %copy-start.74 = (f32[3]{0:T(128)S(1)}, f32[3]{0:T(128)}, u32[]{:S(2)}) copy-start(f32[3]{0:T(128)} %constant.241) | copy-start | bytes 40
  783.9 145.7 %copy-start.71 = (f32[272]{0:T(512)S(1)}, f32[272]{0:T(512)}, u32[]{:S(2)}) copy-start(f32[272]{0:T(512)} %param.35) | copy-start | bytes 3268
  783.9 145.7 %copy-start.73 = (f32[3]{0:T(128)S(1)}, f32[3]{0:T(128)}, u32[]{:S(2)}) copy-start(f32[3]{0:T(128)} %constant.242) | copy-start | bytes 40
  783.9 145.8 %copy-start.63 = (f32[3,768]{1,0:T(4,128)S(1)}, f32[3,768]{1,0:T(4,128)}, u32[]{:S(2)}) copy-start(f32[3,768]{1,0:T(4,128)} %param.37) | copy-start | bytes 27652
  784.9 147.1 %copy-start.55 = (f32[3,768]{1,0:T(4,128)S(1)}, f32[3,768]{1,0:T(4,128)}, u32[]{:S(2)}) copy-start(f32[3,768]{1,0:T(4,128)} %param.32) | copy-start | bytes 27652
  784.9 147.1 %copy-start.64 = (f32[3,768]{1,0:T(4,128)S(1)}, f32[3,768]{1,0:T(4,128)}, u32[]{:S(2)}) copy-start(f32[3,768]{1,0:T(4,128)} %param.38) | copy-start | bytes 27652
  784.9 147.7 %copy-start.49 = (f32[3,32,12]{1,2,0:T(8,128)S(1)}, f32[3,32,12]{1,2,0:T(8,128)}, u32[]{:S(2)}) copy-start(f32[3,32,12]{1,2,0:T(8,128)} %param.33) | copy-start | bytes 13828
  784.9 147.7 %copy-start.56 = (f32[3,32,12]{1,2,0:T(8,128)S(1)}, f32[3,32,12]{1,2,0:T(8,128)}, u32[]{:S(2)}) copy-start(f32[3,32,12]{1,2,0:T(8,128)} %param.39) | copy-start | bytes 13828
  784.9 148.3 %copy-start.27 = (f32[768,272]{0,1:T(8,128)S(1)}, f32[768,272]{0,1:T(8,128)}, u32[]{:S(2)}) copy-start(f32[768,272]{0,1:T(8,128)} %param.30) | copy-start | bytes 2506756
  786.4 148.4 %copy-start.1 = (bf16[16,32,768]{2,1,0:T(8,128)(2,1)S(1)}, bf16[16,32,768]{2,1,0:T(8,128)(2,1)}, u32[]{:S(2)}) copy-start(bf16[16,32,768]{2,1,0:T(8,128)(2,1)} %param.22) | copy-start | bytes 2359300
  790.3 144.6 %copy-start.81 = (f32[112]{0:T(128)}, f32[112]{0:T(128)S(1)}, u32[]{:S(2)}) copy-start(f32[112]{0:T(128)S(1)} %multiply_add_fusion.6) | copy-start | bytes 1348
  885.1 48.2 %copy-start.20 = (f32[768,1,1,272]{0,3,2,1:T(8,128)S(1)}, f32[768,1,1,272]{0,3,2,1:T(8,128)}, u32[]{:S(2)}) copy-start(f32[768,1,1,272]{0,3,2,1:T(8,128)} %reduce-scatter.9.cloned.1.call-done) | copy-start | bytes 2506756
  (60 other events, 299.3 us)
Sparse Core Ops, SparseCore 0:
  11.6 116.5 all-gather.2
  131.6 64.2 all-gather.4
  437.8 65.0 all-reduce.7
  509.4 151.2 reduce-scatter.10
  667.8 217.2 reduce-scatter.8
where the time goes:
time: 954 us; the launch traced here: 942 us
  local copies, waits for them, and re-layouts  425 us (45%)
  waiting for transfers between devices  172 us (18%)
  matrix products  152 us (16%)
  other arithmetic  97.5 us (10%)
  blocking collectives  41.3 us (4%)
  starting transfers between devices  35.7 us (4%)
  between operations  18.1 us (2%)
    unnamed x208, local copies, waits for them, and re-layouts  211 us
    reduce_scatter x1, waiting for transfers between devices, body(): lax.psum_scatter(part_in, 'dp', scatter_dimension=1, tiled=True)  93.5 us
    unnamed x6, waiting for transfers between devices  64.1 us
    reshape x2, local copies, waits for them, and re-layouts, collect_bias(): flat = widened.reshape(heads, length * (2 * length - 1))  63.6 us
    reshape x1, local copies, waits for them, and re-layouts, spread_bias(): return window.reshape(heads, length, 2 * length - 1)[:, :, :length]  54.7 us
    psum x1, blocking collectives, body(): lax.psum((row_terms, col_terms, row_totals, gain_grads, d_rel), ('dp', 'g...  41.3 us
    dot_general x7, matrix products, project_back(): jnp.einsum('rln,kn->rlk', grad_rows, matrix, preferred_element_type=jnp.f...  30.9 us
    dot_general x7, matrix products, project(): jnp.einsum('rlk,kn->rln', values, matrix, preferred_element_type=jnp.floa...  29.6 us
  transfers between devices with their start and end apart: 11, of which 5 were waited for; matrix products, arithmetic and copies ran while one was open for 50% of the time, Pallas kernels for 0%

commit v1 on v0

v1 whole, which is shorter than its diff:
```python
import functools

import jax
import jax.numpy as jnp
import numpy as np
from jax import lax
from jax.experimental import pallas as pl
from jax.experimental.pallas import tpu as pltpu
from jax.sharding import PartitionSpec as P

HEADS = 12
HSIZE = 64
FF = 2048
BUCKETS = 32
MODES = 3
SEGS = 4
SEQ = 512
WIDTH = 768
EPSILON = 1e-06
MASKED = -1e30
DECAY_RATE = 0.9
STEP_SIZE = 0.01
PLAIN_STEP = 0.15
GELU_SCALE = 0.7978845608028654
PRECISE = lax.Precision.HIGHEST
MESH = pl.DeviceIdType.MESH
VMEM_BYTES = 60 << 20


def bucket_table(length, buckets):
    exact_span = buckets // 2
    distances = np.arange(length)
    safe_spans = np.maximum(distances, 1)
    logged = np.floor(
        np.log(safe_spans / exact_span) / np.log(128.0 / exact_span) * (buckets - exact_span)
    )
    far_bucket = np.minimum(exact_span + logged, buckets - 1)
    return np.where(distances < exact_span, distances, far_bucket).astype(np.int32)


def nt(a, b):
    return lax.dot_general(a, b, (((1,), (1,)), ((), ())), preferred_element_type=jnp.float32)


def nn(a, b):
    return lax.dot_general(a, b, (((1,), (0,)), ((), ())), preferred_element_type=jnp.float32)


def tn(a, b):
    return lax.dot_general(a, b, (((0,), (0,)), ((), ())), preferred_element_type=jnp.float32)


def inv_rms(values):
    return lax.rsqrt(jnp.mean(values * values, axis=-1, keepdims=True) + EPSILON)


def rms_back(values, gain, grad):
    inv = inv_rms(values)
    scaled = grad * gain
    along = jnp.mean(scaled * values, axis=-1, keepdims=True)
    return inv * scaled - values * (inv * inv * inv * along), jnp.sum(
        grad * (values * inv), axis=0, keepdims=True
    )


def lane_of(shape):
    return lax.broadcasted_iota(jnp.int32, shape, 1)


def ext_masks(aux, first):
    lane = lane_of(aux.shape)
    spot = lane & 63
    documents = (spot >= first) & (spot < first + SEGS)
    hot = jnp.where(documents, aux.astype(jnp.float32), 0.0)
    against = jnp.where(documents, (1.0 - aux.astype(jnp.float32)) * MASKED, 0.0)
    return hot, against


def halves(tile, ext, even):
    lane = lane_of(tile.shape)
    return jnp.where((lane < HSIZE) if even else (lane >= HSIZE), tile, ext)


def pick(first, second, lane):
    return jnp.where(lane < HSIZE, first, second)


def tile_cols(p, base=0):
    return pl.ds(pl.multiple_of(p * 128 + base, 128), 128)


def attend_pair(p, q_tile, k_tile, v_tile, k_ext, q_ext, att_ref, lse_ref, bias_of):
    lane = lane_of((128, 128))
    ones = jnp.ones((SEQ, 128), jnp.bfloat16)
    sides = []
    for even in (True, False):
        sides.append(
            (
                halves(q_tile, q_ext, even),
                halves(k_tile, k_ext, even),
                halves(v_tile, ones, even),
                None if bias_of is None else bias_of(2 * p + (0 if even else 1)),
            )
        )
    for i in range(SEQ // 128):
        lo = 0 if bias_of is None else max(0, i - 2) * 128
        hi = SEQ if bias_of is None else (i + 1) * 128
        outs, tops = [], []
        for qe, ke, ve, bias in sides:
            s = nt(qe[i * 128 : (i + 1) * 128], ke[lo:hi])
            if bias is not None:
                near, far = bias
                parts = [near[:, 128:]] if i == 0 else [near] if i == 1 else [far, near]
                s = s + (parts[0] if len(parts) == 1 else jnp.concatenate(parts, axis=1))
            top = jnp.max(s, axis=1, keepdims=True)
            e = jnp.exp(s - top).astype(jnp.bfloat16)
            outs.append(nn(e, ve[lo:hi]))
            tops.append(top)
        att = pick(outs[0], outs[1], lane)
        total = pltpu.roll(pick(outs[1], outs[0], lane), HSIZE, 1)
        rows = pl.ds(i * 128, 128)
        att_ref[rows, tile_cols(p)] = (att / total).astype(jnp.bfloat16)
        lse = pick(tops[0], tops[1], lane) + jnp.log(total)
        kept = lse_ref[rows, :]
        first = jnp.sum(jnp.where(lane == 0, lse, 0.0), axis=1, keepdims=True)
        second = jnp.sum(jnp.where(lane == HSIZE, lse, 0.0), axis=1, keepdims=True)
        lse_ref[rows, :] = jnp.where(
            lane == 2 * p, first, jnp.where(lane == 2 * p + 1, second, kept)
        )


def forward_bias(table_ref):
    def bias_of(h):
        row = table_ref[pl.ds(h, 1), :]
        near = pltpu.roll(jnp.broadcast_to(row, (128, 256)), 0, 1, stride=1, stride_axis=0)
        lane = lax.broadcasted_iota(jnp.int32, (128, 256), 1)
        sub = lax.broadcasted_iota(jnp.int32, (128, 256), 0)
        near = jnp.where(lane - 128 > sub, MASKED, near)
        far = jnp.broadcast_to(row[:, :1], (128, 128))
        return near, far

    return bias_of


def back_bias(table_ref):
    def bias_of(h):
        row = table_ref[pl.ds(h, 1), :]
        near = pltpu.roll(jnp.broadcast_to(row, (128, 256)), 0, 1, stride=1, stride_axis=0)
        lane = lax.broadcasted_iota(jnp.int32, (128, 256), 1)
        sub = lax.broadcasted_iota(jnp.int32, (128, 256), 0)
        near = jnp.where(lane < sub, MASKED, near)
        far = jnp.broadcast_to(row[:, 128:129], (128, 128))
        return near, far

    return bias_of


def by_distance(near):
    rows = 64
    while rows >= 8:
        near = near[:rows] + pltpu.roll(near[rows:], 256 - rows, 1)
        rows //= 2
    sub = lax.broadcasted_iota(jnp.int32, (8, 256), 0)
    for bit in (4, 2, 1):
        near = jnp.where((sub & bit) != 0, pltpu.roll(near, 256 - bit, 1), near)
    return near


def split_cols(values, base, lane, count):
    rest, out = values, jnp.zeros((values.shape[0], 128), jnp.float32)
    for k in range(count):
        part = rest.astype(jnp.bfloat16).astype(jnp.float32)
        out = jnp.where((lane & 63) == base + k, part, out)
        rest = rest - part
    return out


def back_pair(
    p, q_tile, k_tile, v_tile, do_tile, att_tile, lse_all, hot, against, bias_of, dq_acc, rel_acc, dist_ref
):
    lane = lane_of((SEQ, 128))
    lane1 = lane_of((128, 128))
    spot = lane & 63
    ones3 = jnp.where((spot >= 8) & (spot < 11), 1.0, 0.0)
    k_ext = (hot + ones3).astype(jnp.bfloat16)
    v_ext = jnp.where((spot >= 0) & (spot < 2), 1.0, 0.0).astype(jnp.bfloat16)
    product = do_tile.astype(jnp.float32) * att_tile.astype(jnp.float32)
    sides = []
    for even in (True, False):
        h = 2 * p + (0 if even else 1)
        lse = jnp.sum(jnp.where(lane == h, lse_all, 0.0), axis=1, keepdims=True)
        own = (lane < HSIZE) if even else (lane >= HSIZE)
        delta = jnp.sum(jnp.where(own, product, 0.0), axis=1, keepdims=True)
        q_ext = (against + split_cols(-lse, 8, lane, 3)).astype(jnp.bfloat16)
        d_ext = split_cols(-delta, 0, lane, 2).astype(jnp.bfloat16)
        sides.append(
            (
                halves(q_tile, q_ext, even),
                halves(k_tile, k_ext, even),
                halves(v_tile, v_ext, even),
                halves(do_tile, d_ext, even),
                None if bias_of is None else bias_of(h),
            )
        )
    dks, dvs = [], []
    dq_acc[...] = jnp.zeros_like(dq_acc)
    if bias_of is not None:
        rel_acc[...] = jnp.zeros_like(rel_acc)
    for j in range(SEQ // 128):
        lo = 0 if bias_of is None else j * 128
        hi = SEQ if bias_of is None else min(SEQ, (j + 3) * 128)
        dk2, dv2 = [], []
        for n, (qe, ke, ve, de, bias) in enumerate(sides):
            s = nt(ke[j * 128 : (j + 1) * 128], qe[lo:hi])
            if bias is not None:
                near, far = bias
                s = s + (
                    near[:, :128] if hi - lo == 128 else near if hi - lo == 256
                    else jnp.concatenate([near, far], axis=1)
                )
            w = jnp.exp(s)
            dv2.append(nn(w.astype(jnp.bfloat16), do_tile[lo:hi]))
            ds = w * nt(ve[j * 128 : (j + 1) * 128], de[lo:hi])
            if bias is not None:
                rel_acc[n, :, : hi - lo] += ds
            ds = ds.astype(jnp.bfloat16)
            dk2.append(nn(ds, q_tile[lo:hi]))
            dq_acc[n, :, lo:hi] += tn(k_tile[j * 128 : (j + 1) * 128], ds)
        dks.append(pick(dk2[0], dk2[1], lane1))
        dvs.append(pick(dv2[0], dv2[1], lane1))
    if bias_of is not None:
        for n in range(2):
            near = by_distance(rel_acc[n, :, :256])
            dist_ref[pl.ds(2 * p + n, 1), :] = jnp.concatenate(
                [
                    jnp.sum(near, axis=0, keepdims=True),
                    jnp.sum(rel_acc[n, :, 256:], axis=0, keepdims=True),
                ],
                axis=1,
            )
    sub = lax.broadcasted_iota(jnp.int32, (128, SEQ), 0)
    dq = jnp.where(sub < HSIZE, dq_acc[0], dq_acc[1]).T * HSIZE**-0.5
    return dq, jnp.concatenate(dks, axis=0), jnp.concatenate(dvs, axis=0)


HEAD_COLS = HEADS * HSIZE


def attention_forward(
    tok, mem, aux, win, wout, gains, table, qkv, att1, lse1, x1, qc, kvc, att2, lse2, x2, step
):
    x0 = tok[...].astype(jnp.float32)
    a1 = (x0 * inv_rms(x0) * gains[0:1, :]).astype(jnp.bfloat16)
    for k in range(3):
        cols = slice(k * HEAD_COLS, (k + 1) * HEAD_COLS)
        got = nt(a1, win[cols, :])
        if k == 0:
            got = got.astype(jnp.bfloat16).astype(jnp.float32) * HSIZE**-0.5
        qkv[:, cols] = got.astype(jnp.bfloat16)
    lse1[...] = jnp.zeros_like(lse1)
    lse2[...] = jnp.zeros_like(lse2)

    @pl.loop(0, HEADS // 2)
    def _(p):
        hot, against = ext_masks(aux[...], 0)
        attend_pair(
            p, qkv[:, tile_cols(p)], qkv[:, tile_cols(p, HEAD_COLS)], qkv[:, tile_cols(p, 2 * HEAD_COLS)],
            hot.astype(jnp.bfloat16), against.astype(jnp.bfloat16), att1, lse1, forward_bias(table),
        )
        step("self", p)

    x1[...] = tok[...].astype(jnp.float32) + nn(att1[...], wout[0:HEAD_COLS, :])
    a2 = (x1[...] * inv_rms(x1[...]) * gains[1:2, :]).astype(jnp.bfloat16)
    got = nt(a2, win[3 * HEAD_COLS : 4 * HEAD_COLS, :])
    qc[...] = (got.astype(jnp.bfloat16).astype(jnp.float32) * HSIZE**-0.5).astype(jnp.bfloat16)
    for k in range(2):
        kvc[:, k * HEAD_COLS : (k + 1) * HEAD_COLS] = nt(
            mem[...], win[(4 + k) * HEAD_COLS : (5 + k) * HEAD_COLS, :]
        ).astype(jnp.bfloat16)

    @pl.loop(0, HEADS // 2)
    def _(p):
        _, against = ext_masks(aux[...], 0)
        hot = pltpu.roll(ext_masks(aux[...], SEGS)[0], 128 - SEGS, 1)
        attend_pair(
            p, qc[:, tile_cols(p)], kvc[:, tile_cols(p)], kvc[:, tile_cols(p, HEAD_COLS)],
            hot.astype(jnp.bfloat16), against.astype(jnp.bfloat16), att2, lse2, None,
        )
        step("cross", p)

    x2[...] = x1[...] + nn(att2[...], wout[HEAD_COLS : 2 * HEAD_COLS, :])


def ff_kernel(
    x2, cot, keep, gains, w_gate, w_up, w_down, mixed, g2, d_gain, g_win, g_wout, a3, e3, acc, da3, held, sem
):
    c = pl.program_id(0)
    slot = lax.rem(c, 2)
    rows = w_gate.shape[0]
    first = pl.multiple_of(c * rows, rows)
    puts = [
        pltpu.make_async_copy(held.at[slot, 0], g_win.at[pl.ds(6 * HEAD_COLS + first, rows)], sem.at[slot, 0]),
        pltpu.make_async_copy(held.at[slot, 1], g_win.at[pl.ds(6 * HEAD_COLS + FF + first, rows)], sem.at[slot, 1]),
        pltpu.make_async_copy(held.at[slot, 2], g_wout.at[pl.ds(2 * HEAD_COLS + first, rows)], sem.at[slot, 2]),
    ]

    @pl.when(c >= 2)
    def _():
        for put in puts:
            put.wait()

    @pl.when(c == 0)
    def _():
        a3[...] = (x2[...] * inv_rms(x2[...]) * gains[2:3, :]).astype(jnp.bfloat16)
        e3[...] = (cot[...].astype(jnp.float32) * keep[:, 0:1]).astype(jnp.bfloat16)
        acc[...] = x2[...]
        da3[...] = jnp.zeros_like(da3)

    gate = nt(a3[...], w_gate[...])
    up = nt(a3[...], w_up[...])
    dh = nt(e3[...], w_down[...])
    cube = 0.044715 * gate * gate
    inner = jnp.tanh(GELU_SCALE * gate * (1.0 + cube))
    half = 0.5 * (1.0 + inner)
    gelu = gate * half
    slope = half + 0.5 * gate * (1.0 - inner * inner) * (GELU_SCALE * (1.0 + 3.0 * cube))
    hidden = (gelu * up).astype(jnp.bfloat16)
    d_gate = (dh * up * slope).astype(jnp.bfloat16)
    d_up = (dh * gelu).astype(jnp.bfloat16)
    acc[...] += nn(hidden, w_down[...])
    held[slot, 0] = tn(d_gate, a3[...]).astype(jnp.bfloat16)
    held[slot, 1] = tn(d_up, a3[...]).astype(jnp.bfloat16)
    held[slot, 2] = tn(hidden, e3[...]).astype(jnp.bfloat16)
    for put in puts:
        put.start()
    da3[...] += nn(d_gate, w_gate[...]) + nn(d_up, w_up[...])

    @pl.when(c == pl.num_programs(0) - 1)
    def _():
        mixed[...] = acc[...].astype(jnp.bfloat16)
        part, gain = rms_back(x2[...], gains[2:3, :], da3[...])
        g2[...] = cot[...].astype(jnp.float32) * keep[:, 0:1] + part
        d_gain[...] = gain
        for k in range(3):
            for other in range(2):
                pltpu.make_async_copy(held.at[other, k], g_wout.at[0:rows], sem.at[other, k]).wait()


def attention_backward(
    tok, mem, aux, win, wout, gains, table, qkv, att1, lse1, x1, qc, kvc, att2, lse2, g2,
    d_mem, d_tok, d_gains, dist, do, dqkv, dq_acc, rel_acc, emit, step,
):
    e2 = g2[...].astype(jnp.bfloat16)
    do[...] = nt(e2, wout[HEAD_COLS : 2 * HEAD_COLS, :]).astype(jnp.bfloat16)
    emit(7, tn(att2[...], e2))

    @pl.loop(0, HEADS // 2)
    def _(p):
        _, against = ext_masks(aux[...], 0)
        hot = pltpu.roll(ext_masks(aux[...], SEGS)[0], 128 - SEGS, 1)
        dq, dk, dv = back_pair(
            p, qc[:, tile_cols(p)], kvc[:, tile_cols(p)], kvc[:, tile_cols(p, HEAD_COLS)], do[:, tile_cols(p)],
            att2[:, tile_cols(p)], lse2[...], hot, against, None, dq_acc, rel_acc, dist,
        )
        dqkv[:, tile_cols(p)] = dq.astype(jnp.bfloat16)
        dqkv[:, tile_cols(p, HEAD_COLS)] = dk.astype(jnp.bfloat16)
        dqkv[:, tile_cols(p, 2 * HEAD_COLS)] = dv.astype(jnp.bfloat16)
        step("cross", p)

    a2 = (x1[...] * inv_rms(x1[...]) * gains[1:2, :]).astype(jnp.bfloat16)
    for k in range(3):
        cols = slice(k * HEAD_COLS, (k + 1) * HEAD_COLS)
        emit(3 + k, tn(dqkv[:, cols], a2 if k == 0 else mem[...]))
    d_mem[...] = nn(
        dqkv[:, HEAD_COLS : 3 * HEAD_COLS], win[4 * HEAD_COLS : 6 * HEAD_COLS, :]
    ).astype(jnp.bfloat16)
    da2 = nn(dqkv[:, 0:HEAD_COLS], win[3 * HEAD_COLS : 4 * HEAD_COLS, :])
    part, gain = rms_back(x1[...], gains[1:2, :], da2)
    d_gains[1:2, :] = gain
    g2[...] += part
    e1 = g2[...].astype(jnp.bfloat16)
    do[...] = nt(e1, wout[0:HEAD_COLS, :]).astype(jnp.bfloat16)
    emit(6, tn(att1[...], e1))
    step("middle", 0)

    @pl.loop(0, HEADS // 2)
    def _(p):
        hot, against = ext_masks(aux[...], 0)
        dq, dk, dv = back_pair(
            p, qkv[:, tile_cols(p)], qkv[:, tile_cols(p, HEAD_COLS)], qkv[:, tile_cols(p, 2 * HEAD_COLS)],
            do[:, tile_cols(p)], att1[:, tile_cols(p)], lse1[...], hot, against, back_bias(table), dq_acc, rel_acc, dist,
        )
        dqkv[:, tile_cols(p)] = dq.astype(jnp.bfloat16)
        dqkv[:, tile_cols(p, HEAD_COLS)] = dk.astype(jnp.bfloat16)
        dqkv[:, tile_cols(p, 2 * HEAD_COLS)] = dv.astype(jnp.bfloat16)
        step("self", p)

    x0 = tok[...].astype(jnp.float32)
    a1 = (x0 * inv_rms(x0) * gains[0:1, :]).astype(jnp.bfloat16)
    for k in range(3):
        cols = slice(k * HEAD_COLS, (k + 1) * HEAD_COLS)
        emit(k, tn(dqkv[:, cols], a1))
    da1 = nn(dqkv[...], win[0 : 3 * HEAD_COLS, :])
    part, gain = rms_back(x0, gains[0:1, :], da1)
    d_gains[0:1, :] = gain
    d_tok[...] = (g2[...] + part).astype(jnp.bfloat16)


SHARE = {"i": 272, "o": 112}
PIECES = (
    ("i", 0, 64, 32), ("i", 64, 64, 32), ("i", 128, 64, 32), ("i", 192, 80, 48),
    ("o", 0, 64, 32), ("o", 64, 48, 16),
)


def place():
    dp = lax.axis_index("dp")
    return dp // 4, (dp // 2) % 2, dp % 2, lax.axis_index("group")


def dev(z, y, x, g):
    return ((z * 2 + y) * 2 + x, g)


def rows_of(ref, kind, zz, yy, xx, gg, lo, n):
    share = ((zz * 2 + yy) * 2 + xx) * 2 + gg
    return ref.at[pl.ds(pl.multiple_of(share * SHARE[kind] + lo, 16), n)]


class Links:
    def __init__(self, send_sem, recv_sem):
        self.send_sem, self.recv_sem, self.count, self.sent = send_sem, recv_sem, 0, []

    def reserve(self, n):
        self.count += n
        return self.count - n

    def copy(self, src, dst, device, sem=None):
        k = self.reserve(1) if sem is None else sem
        return pltpu.make_async_remote_copy(
            src_ref=src, dst_ref=dst, send_sem=self.send_sem.at[k], recv_sem=self.recv_sem.at[k],
            device_id=device, device_id_type=MESH,
        )

    def start(self, copy, cond=None):
        if cond is None:
            copy.start()
        else:
            pl.when(cond)(copy.start)
        self.sent.append((copy, cond))

    def drain(self):
        for copy, cond in self.sent:
            if cond is None:
                copy.wait_send()
            else:
                pl.when(cond)(copy.wait_send)
        self.sent = []


def greet(peers):
    barrier = pltpu.get_barrier_semaphore()
    total = 0
    for device, cond in peers:
        if cond is None:
            pl.semaphore_signal(barrier, inc=1, device_id=device, device_id_type=MESH)
            total = total + 1
        else:

            @pl.when(cond)
            def _(device=device):
                pl.semaphore_signal(barrier, inc=1, device_id=device, device_id_type=MESH)

            total = total + cond.astype(jnp.int32)
    pl.semaphore_wait(barrier, total)


def near_peers():
    z, y, x, g = place()
    return [
        (dev(z, y, 1 - x, g), None), (dev(z, 1 - y, x, g), None), (dev(z, y, x, 1 - g), None),
        (dev(jnp.minimum(z + 1, 3), y, x, g), z < 3), (dev(jnp.maximum(z - 1, 0), y, x, g), z > 0),
    ]


def all_peers():
    z, y, x, g = place()
    me = lax.axis_index("dp")
    return [((lax.rem(me + k, 16), g), None) for k in range(1, 16)] + [(dev(z, y, x, 1 - g), None)]


def gather_steps(links, arrays, low, lag1=2, lag2=4):
    z, y, x, g = place()
    items = []
    nearest = jnp.clip(z, low, low + 1)
    bases = [(links.reserve(2), links.reserve(2)) for _ in PIECES]
    for zz in (nearest, 2 * low + 1 - nearest):
        for (kind, lo, n, half), (b_up, b_down) in zip(PIECES, bases):

            def here(yy, xx, first, count, zz=zz, kind=kind):
                return rows_of(arrays[kind], kind, zz, yy, xx, g, first, count)

            c = {"zz": zz}

            def add(name, ref, device, sem=None, c=c):
                c[name] = links.copy(ref, ref, device, sem)

            own = here(y, x, lo, n)
            add("up", own, dev(jnp.minimum(z + 1, 3), y, x, g), b_up + zz - low)
            add("down", own, dev(jnp.maximum(z - 1, 0), y, x, g), b_down + zz - low)
            add("x", own, dev(z, y, 1 - x, g))
            add("y", own, dev(z, 1 - y, x, g))
            add("p", own, dev(z, y, x, 1 - g))
            add("a", here(y, 1 - x, lo, half), dev(z, 1 - y, x, g))
            add("b", here(1 - y, x, lo + half, n - half), dev(z, y, 1 - x, g))
            add("px", here(y, 1 - x, lo, n), dev(z, y, x, 1 - g))
            add("py", here(1 - y, x, lo, n), dev(z, y, x, 1 - g))
            add("pa", here(1 - y, 1 - x, lo, half), dev(z, y, x, 1 - g))
            add("pb", here(1 - y, 1 - x, lo + half, n - half), dev(z, y, x, 1 - g))
            items.append(c)

    def first(c):
        zz = c["zz"]
        pl.when(z > zz)(c["up"].wait_recv)
        pl.when(z < zz)(c["down"].wait_recv)
        links.start(c["up"], (z >= zz) & (z < 3))
        links.start(c["down"], (z <= zz) & (z > 0))
        for k in ("x", "y", "p"):
            links.start(c[k])

    def second(c):
        c["x"].wait_recv()
        links.start(c["a"])
        links.start(c["px"])
        c["y"].wait_recv()
        links.start(c["b"])
        links.start(c["py"])

    def third(c):
        c["a"].wait_recv()
        links.start(c["pa"])
        c["b"].wait_recv()
        links.start(c["pb"])

    n = len(items)
    steps = []
    for t in range(n + lag2):

        def step(t=t):
            if t < n:
                first(items[t])
            if 0 <= t - lag1 < n:
                second(items[t - lag1])
            if 0 <= t - lag2 < n:
                third(items[t - lag2])

        steps.append(step)

    def end():
        for c in items:
            for k in ("p", "px", "py", "pa", "pb"):
                c[k].wait_recv()

    return steps, end


def gather_kernel(win_sh, wout_sh, tok_s, mem_s, aux_s, win, wout, tok, mem, aux, ss, rs, ls):
    z, y, x, g = place()
    me = lax.axis_index("dp")
    links = Links(ss, rs)
    near = [
        pltpu.make_async_copy(win_sh, rows_of(win, "i", z, y, x, g, 0, 272), ls.at[0]),
        pltpu.make_async_copy(wout_sh, rows_of(wout, "o", z, y, x, g, 0, 112), ls.at[1]),
    ]
    moves = ((tok_s, tok), (aux_s, aux), (mem_s, mem))
    own = [pltpu.make_async_copy(s.at[me], t.at[me], ls.at[2 + k]) for k, (s, t) in enumerate(moves)]
    for c in near + own:
        c.start()
    greet(all_peers())
    for c in near:
        c.wait()
    queue = []
    for s, t in moves:
        for k in range(1, 16):
            to = lax.rem(me + k, 16)
            queue.append(links.copy(s.at[to], t.at[me], (to, g)))
    steps, ends = [], []
    for low in (0, 2):
        more, end = gather_steps(links, {"i": win, "o": wout}, low)
        steps += more
        ends.append(end)
    per = -(-len(queue) // len(steps))
    for k, step in enumerate(steps):
        step()
        for c in queue[k * per : (k + 1) * per]:
            links.start(c)
    for c in queue:
        c.wait_recv()
    for end in ends:
        end()
    for c in own:
        c.wait()
    links.drain()


def sums_kernel(win_g, wout_g, dtok, dmem, part_in, part_out, btok, bmem, own, got, gx, gy, fin, gz, final, ss, rs, ls):
    z, y, x, g = place()
    me = lax.axis_index("dp")
    links = Links(ss, rs)
    moves = ((dmem, bmem), (dtok, btok))
    mine = [pltpu.make_async_copy(s.at[me], t.at[me], ls.at[k]) for k, (s, t) in enumerate(moves)]
    for c in mine:
        c.start()
    greet(all_peers())
    queue = []
    for s, t in moves:
        for k in range(1, 16):
            to = lax.rem(me + k, 16)
            queue.append(links.copy(s.at[to], t.at[me], (to, g)))
    arrays = {"i": win_g, "o": wout_g}
    order = [(zz, k) for zz in (3, 0, 2, 1) for k in range(len(PIECES))]
    cols = ((y, x), (y, 1 - x), (1 - y, x), (1 - y, 1 - x))
    tot = sum(p[2] for p in PIECES)
    items = []
    for zz, k in order:
        kind, lo, n, half = PIECES[k]
        base = zz * tot + sum(p[2] for p in PIECES[:k])
        at = lambda ref, c, off, m, base=base: ref.at[c, pl.ds(base + off, m)]
        it = {"zz": zz, "n": n, "half": half, "base": base, "kind": kind, "lo": lo}
        it["load"], it["pair"] = [], []
        for c, (yy, xx) in enumerate(cols):
            it["load"].append(
                pltpu.make_async_copy(
                    rows_of(arrays[kind], kind, zz, yy, xx, g, lo, n), at(own, c, 0, n), ls.at[2 + 4 * len(items) + c]
                )
            )
            it["pair"].append(
                links.copy(
                    rows_of(arrays[kind], kind, zz, yy, xx, 1 - g, lo, n), at(got, c, 0, n), dev(z, y, x, 1 - g)
                )
            )
        nx, ny = dev(z, y, 1 - x, g), dev(z, 1 - y, x, g)
        it["x1"] = [links.copy(at(own, c, 0, half), at(gx, s, 0, half), nx) for s, c in ((0, 1), (1, 3))]
        it["y1"] = [links.copy(at(own, c, half, n - half), at(gy, s, half, n - half), ny) for s, c in ((0, 2), (1, 3))]
        it["y2"] = links.copy(at(own, 2, 0, half), at(fin, 0, 0, half), ny)
        it["x2"] = links.copy(at(own, 1, half, n - half), at(fin, 0, half, n - half), nx)
        whole = at(own, 0, 0, n)
        it["up"] = links.copy(whole, at(gz, 0, 0, n), dev(jnp.minimum(z + 1, 3), y, x, g))
        it["down"] = links.copy(whole, at(gz, 1, 0, n), dev(jnp.maximum(z - 1, 0), y, x, g))
        items.append(it)

    def add(dst, c, src, s, it, off, m):
        rows = pl.ds(it["base"] + off, m)
        dst[c, rows, :] = (dst[c, rows, :].astype(jnp.float32) + src[s, rows, :].astype(jnp.float32)).astype(jnp.bfloat16)

    def stage0(it):
        for c in it["load"]:
            c.start()
        for c in it["pair"]:
            links.start(c)

    def stage1(it):
        for c in (3, 1, 2, 0):
            it["load"][c].wait()
            it["pair"][c].wait_recv()
            add(own, c, got, c, it, 0, it["n"])
            if c == 3:
                links.start(it["x1"][1])
                links.start(it["y1"][1])
            if c == 1:
                links.start(it["x1"][0])
            if c == 2:
                links.start(it["y1"][0])

    def stage2(it):
        half, rest = it["half"], it["n"] - it["half"]
        it["x1"][1].wait_recv()
        add(own, 2, gx, 1, it, 0, half)
        links.start(it["y2"])
        it["y1"][1].wait_recv()
        add(own, 1, gy, 1, it, half, rest)
        links.start(it["x2"])
        it["x1"][0].wait_recv()
        add(own, 0, gx, 0, it, 0, half)
        it["y1"][0].wait_recv()
        add(own, 0, gy, 0, it, half, rest)

    def stage3(it):
        zz, n, half = it["zz"], it["n"], it["half"]
        it["y2"].wait_recv()
        it["x2"].wait_recv()
        add(own, 0, fin, 0, it, 0, n)

        @pl.when(z < zz)
        def _():
            @pl.when(z > 0)
            def _():
                it["up"].wait_recv()
                add(own, 0, gz, 0, it, 0, n)

            it["up"].start()

        @pl.when(z > zz)
        def _():
            @pl.when(z < 3)
            def _():
                it["down"].wait_recv()
                add(own, 0, gz, 1, it, 0, n)

            it["down"].start()

        links.sent.append((it["up"], z < zz))
        links.sent.append((it["down"], z > zz))

        @pl.when(z == zz)
        def _():
            rows = pl.ds(it["base"], n)
            total = own[0, rows, :].astype(jnp.float32)
            if zz > 0:
                it["up"].wait_recv()
                total += gz[0, rows, :].astype(jnp.float32)
            if zz < 3:
                it["down"].wait_recv()
                total += gz[1, rows, :].astype(jnp.float32)
            into = part_in if it["kind"] == "i" else part_out
            into[it["lo"] : it["lo"] + n, :] = total

    lags = (0, 2, 4, 6)
    stages = (stage0, stage1, stage2, stage3)
    n = len(items)
    per = -(-len(queue) // n)
    for t in range(n + lags[-1]):
        for lag, stage in zip(lags, stages):
            if 0 <= t - lag < n:
                stage(items[t - lag])
        for c in queue[t * per : (t + 1) * per]:
            links.start(c)
    for c in queue:
        c.wait_recv()
    for c in mine:
        c.wait()
    links.drain()


def vmem_call(kernel, out_shape, scratch, **kw):
    return pl.pallas_call(
        kernel,
        out_shape=out_shape,
        scratch_shapes=scratch,
        compiler_params=pltpu.CompilerParams(vmem_limit_bytes=VMEM_BYTES),
        **kw,
    )


def sds(shape, dtype=jnp.bfloat16):
    return jax.ShapeDtypeStruct(shape, dtype)


WEIGHTS = [
    pltpu.VMEM((6 * HEAD_COLS, WIDTH), jnp.bfloat16), pltpu.VMEM((2 * HEAD_COLS, WIDTH), jnp.bfloat16),
    pltpu.SemaphoreType.DMA((2,)),
]


def load_weights(win, wout, win_v, wout_v, sem):
    copies = [
        pltpu.make_async_copy(win.at[0 : 6 * HEAD_COLS], win_v, sem.at[0]),
        pltpu.make_async_copy(wout.at[0 : 2 * HEAD_COLS], wout_v, sem.at[1]),
    ]
    for c in copies:
        c.start()
    return copies


def anywhere():
    return pl.BlockSpec(memory_space=pl.ANY)


def whole():
    return pl.BlockSpec(memory_space=pltpu.VMEM)


def gather_all(win_sh, wout_sh, tok_s, mem_s, aux_s):
    any_ = pl.BlockSpec(memory_space=pl.ANY)
    sems = 45 + 2 * 22 * len(PIECES)
    return pl.pallas_call(
        gather_kernel,
        out_shape=(
            sds((32 * win_sh.shape[0], WIDTH)), sds((32 * wout_sh.shape[0], WIDTH)),
            sds(tok_s.shape), sds(mem_s.shape), sds(aux_s.shape),
        ),
        in_specs=[whole(), whole(), any_, any_, any_],
        out_specs=(any_,) * 5,
        scratch_shapes=[
            pltpu.SemaphoreType.DMA((sems,)), pltpu.SemaphoreType.DMA((sems,)), pltpu.SemaphoreType.DMA((5,)),
        ],
        compiler_params=pltpu.CompilerParams(
            collective_id=1, has_side_effects=True, vmem_limit_bytes=VMEM_BYTES
        ),
    )(win_sh, wout_sh, tok_s, mem_s, aux_s)


def sum_all(g_win, g_wout, d_tok, d_mem):
    any_ = pl.BlockSpec(memory_space=pl.ANY)
    tot = 4 * sum(p[2] for p in PIECES)
    items = 4 * len(PIECES)
    sems = 30 + 12 * items
    vm = lambda k: pltpu.VMEM((k, tot, WIDTH), jnp.bfloat16)
    return pl.pallas_call(
        sums_kernel,
        out_shape=(
            sds((272, WIDTH), jnp.float32), sds((112, WIDTH), jnp.float32), sds(d_tok.shape), sds(d_mem.shape),
        ),
        in_specs=[any_] * 4,
        out_specs=(whole(), whole(), any_, any_),
        scratch_shapes=[
            vm(4), vm(4), vm(2), vm(2), vm(1), vm(2), pltpu.VMEM((8, 128), jnp.float32),
            pltpu.SemaphoreType.DMA((sems,)), pltpu.SemaphoreType.DMA((sems,)),
            pltpu.SemaphoreType.DMA((2 + 4 * items,)),
        ],
        compiler_params=pltpu.CompilerParams(
            collective_id=2, has_side_effects=True, vmem_limit_bytes=VMEM_BYTES
        ),
    )(g_win, g_wout, d_tok, d_mem)


def forward_call(tok, mem, aux, win, wout, gains, table):
    f32 = jnp.float32

    def kernel(tok, mem, aux, win, wout, *refs):
        win_v, wout_v, sem = refs[-3:]
        loads = load_weights(win, wout, win_v, wout_v, sem)
        for c in loads:
            c.wait()
        attention_forward(tok, mem, aux, win_v, wout_v, *refs[:-3], step=lambda name, p: None)

    return vmem_call(
        kernel,
        (
            sds((SEQ, 3 * HEAD_COLS)), sds((SEQ, HEAD_COLS)), sds((SEQ, 128), f32), sds((SEQ, WIDTH), f32),
            sds((SEQ, HEAD_COLS)), sds((SEQ, 2 * HEAD_COLS)), sds((SEQ, HEAD_COLS)), sds((SEQ, 128), f32),
            sds((SEQ, WIDTH), f32),
        ),
        WEIGHTS,
        in_specs=[whole(), whole(), whole(), anywhere(), anywhere(), whole(), whole()],
    )(tok, mem, aux, win, wout, gains, table)


def ff_call(x2, cot, keep, gains, win, wout):
    f32 = jnp.float32
    step = 256
    n = FF // step
    at = lambda block, first: pl.BlockSpec((step, WIDTH), lambda c: (first + c, 0))
    full = lambda rows, cols: pl.BlockSpec((rows, cols), lambda c: (0, 0))
    gate0, down0 = 6 * HEAD_COLS // step, 2 * HEAD_COLS // step
    return vmem_call(
        ff_kernel,
        (
            sds((SEQ, WIDTH)), sds((SEQ, WIDTH), f32), sds((1, WIDTH), f32), sds(win.shape), sds(wout.shape),
        ),
        [
            pltpu.VMEM((SEQ, WIDTH), jnp.bfloat16), pltpu.VMEM((SEQ, WIDTH), jnp.bfloat16),
            pltpu.VMEM((SEQ, WIDTH), f32), pltpu.VMEM((SEQ, WIDTH), f32),
            pltpu.VMEM((2, 3, step, WIDTH), jnp.bfloat16), pltpu.SemaphoreType.DMA((2, 3)),
        ],
        grid=(n,),
        in_specs=[
            full(SEQ, WIDTH), full(SEQ, WIDTH), full(SEQ, 128), full(3, WIDTH),
            at(step, gate0), at(step, gate0 + n), at(step, down0),
        ],
        out_specs=(full(SEQ, WIDTH), full(SEQ, WIDTH), full(1, WIDTH), anywhere(), anywhere()),
    )(x2, cot, keep, gains, win, win, wout)


def backward_call(tok, mem, aux, win, wout, gains, table, kept, g2, g_win, g_wout):
    f32 = jnp.float32

    def kernel(_, __, tok, mem, aux, win, wout, *refs):
        ins, (g_win, g_wout), outs = refs[:11], refs[11:13], refs[13:17]
        scratch, (held, put_sem, win_v, wout_v, sem) = refs[17:21], refs[21:]
        loads = load_weights(win, wout, win_v, wout_v, sem)
        puts = []

        def emit(block, value):
            held[block] = value.astype(jnp.bfloat16)
            into, first = (g_win, block) if block < 6 else (g_wout, block - 6)
            rows = pl.ds(first * HEAD_COLS, HEAD_COLS)
            puts.append(pltpu.make_async_copy(held.at[block], into.at[rows], put_sem.at[block]))
            puts[-1].start()

        for c in loads:
            c.wait()
        attention_backward(
            tok, mem, aux, win_v, wout_v, *ins, *outs, *scratch, emit=emit, step=lambda name, p: None
        )
        for c in puts:
            c.wait()

    return vmem_call(
        kernel,
        (
            sds(g_win.shape), sds(g_wout.shape), sds((SEQ, WIDTH)), sds((SEQ, WIDTH)),
            sds((2, WIDTH), f32), sds((16, 384), f32),
        ),
        [
            pltpu.VMEM((SEQ, HEAD_COLS), jnp.bfloat16), pltpu.VMEM((SEQ, 3 * HEAD_COLS), jnp.bfloat16),
            pltpu.VMEM((2, 128, SEQ), f32), pltpu.VMEM((2, 128, 384), f32),
            pltpu.VMEM((8, HEAD_COLS, WIDTH), jnp.bfloat16), pltpu.SemaphoreType.DMA((8,)),
        ]
        + WEIGHTS,
        in_specs=[anywhere()] * 2 + [whole()] * 3 + [anywhere()] * 2 + [whole()] * 11,
        out_specs=(anywhere(), anywhere()) + (whole(),) * 4,
        input_output_aliases={0: 0, 1: 1},
    )(g_win, g_wout, tok, mem, aux, win, wout, gains, table, *kept, g2)


def body(
    tokens, memory, segments, memory_segments, row_source, denoiser_modes, sentinel, cotangent, w_in, w_out,
    norm_gains, rel_bias, rows_in, cols_in, rows_out, cols_out, sq_gains, sq_rel,
):
    n_index = lax.axis_size("dp")
    n_group = lax.axis_size("group")
    my_group = lax.axis_index("group")
    my_place = lax.axis_index(("dp", "group"))
    half_rows = tokens.shape[0]
    rows_dev = cotangent.shape[0]
    assert rows_dev == 1
    boxed = n_index == 16 and n_group == 2
    slot_table = row_source.reshape(n_index, n_group)
    sources = lax.dynamic_index_in_dim(slot_table, my_group, 1, keepdims=False) - my_group * half_rows
    own_row = lax.dynamic_index_in_dim(row_source, my_place, 0, keepdims=False)
    own_mode = lax.dynamic_index_in_dim(denoiser_modes, own_row, 0, keepdims=False)

    spot = jnp.arange(128) % HSIZE
    both = jnp.where(spot < SEGS, segments[sources][:, :, None], memory_segments[sources][:, :, None])
    aux_s = ((both == spot % SEGS) & (spot < 2 * SEGS)).astype(jnp.bfloat16)
    win_sh = w_in.T.astype(jnp.bfloat16)
    wout_sh = w_out.astype(jnp.bfloat16)
    tok_s, mem_s = tokens[sources], memory[sources]
    if boxed:
        win, wout, tok, mem, aux = gather_all(win_sh, wout_sh, tok_s, mem_s, aux_s)
    else:
        win = lax.all_gather(win_sh, ("dp", "group"), axis=0, tiled=True)
        wout = lax.all_gather(wout_sh, ("dp", "group"), axis=0, tiled=True)
        tok, mem, aux = (
            lax.all_to_all(v, "dp", split_axis=0, concat_axis=0, tiled=True) for v in (tok_s, mem_s, aux_s)
        )
    tok, mem, aux = tok.reshape(SEQ, WIDTH), mem.reshape(SEQ, WIDTH), aux.reshape(SEQ, 128)

    buckets = bucket_table(SEQ, BUCKETS)
    hot = (buckets[:256, None] == np.arange(BUCKETS)[None, :]).astype(np.float32)
    lane = np.arange(256)
    dist_f = np.where(lane <= 128, 128 - lane, 384 - lane)
    hot_f = hot[dist_f]
    rel_row = lax.dynamic_index_in_dim(rel_bias, own_mode, 0, keepdims=False)
    rel_pad = jnp.pad(rel_row.T, ((0, 4), (0, 0)))
    tables = jnp.dot(rel_pad, np.concatenate([hot_f, hot], axis=0).T, precision=PRECISE)
    table_f, table_b = tables[:, :256], tables[:, 256:]

    kept = forward_call(tok, mem, aux, win, wout, norm_gains, table_f)
    x2 = kept[8]
    keep = jnp.broadcast_to((1 - sentinel).astype(jnp.float32).reshape(SEQ, 1), (SEQ, 128))
    mixed, g2, d_gain_three, g_win, g_wout = ff_call(
        x2, cotangent.reshape(SEQ, WIDTH), keep, norm_gains, win, wout
    )
    g_win, g_wout, d_mem, d_tok, d_gains, dist = backward_call(
        tok, mem, aux, win, wout, norm_gains, table_b, kept[:8], g2, g_win, g_wout
    )
    d_tok, d_mem = d_tok.reshape(tok_s.shape), d_mem.reshape(mem_s.shape)
    if boxed:
        part_in_t, part_out, back_tok, back_mem = sum_all(g_win, g_wout, d_tok, d_mem)
    else:
        back_tok, back_mem = (
            lax.all_to_all(v, "dp", split_axis=0, concat_axis=0, tiled=True) for v in (d_tok, d_mem)
        )
        part_in_t, part_out = (
            lax.psum_scatter(v.astype(jnp.float32), ("dp", "group"), scatter_dimension=0, tiled=True)
            for v in (g_win, g_wout)
        )
    part_in = part_in_t.T
    inverse = jnp.argsort(sources)
    merge = lambda v: v.reshape(n_index, SEQ // n_index, WIDTH)[inverse]
    d_tokens_out, d_memory_out = merge(back_tok), merge(back_mem)
    hot_dist = np.concatenate([hot, np.repeat(np.eye(BUCKETS, dtype=np.float32)[-1:], 128, axis=0)], axis=0)
    d_rel_row = jnp.dot(dist[:HEADS], hot_dist, precision=PRECISE).T
    mode_hot = (own_mode == jnp.arange(MODES)).astype(jnp.float32)
    d_rel = mode_hot[:, None, None] * d_rel_row[None]

    col_count = part_in.shape[1]
    col_ids = my_place * col_count + jnp.arange(col_count)
    col_hot = jnp.stack(
        [
            col_ids < 3 * HEAD_COLS,
            (col_ids >= 3 * HEAD_COLS) & (col_ids < 6 * HEAD_COLS),
            col_ids >= 6 * HEAD_COLS,
        ],
        axis=0,
    ).astype(jnp.float32)
    sq_in = part_in * part_in
    row_terms = jnp.einsum("mc,dc->md", col_hot, sq_in, precision=PRECISE)
    row_count = part_out.shape[0]
    row_ids = my_place * row_count + jnp.arange(row_count)
    row_hot = jnp.stack(
        [
            row_ids < HEAD_COLS,
            (row_ids >= HEAD_COLS) & (row_ids < 2 * HEAD_COLS),
            row_ids >= 2 * HEAD_COLS,
        ],
        axis=0,
    ).astype(jnp.float32)
    sq_out = part_out * part_out
    rows_out_new = DECAY_RATE * rows_out + (1 - DECAY_RATE) * jnp.mean(sq_out, axis=1)
    col_terms = jnp.einsum("mr,rd->md", row_hot, sq_out, precision=PRECISE)
    row_totals = jnp.dot(row_hot, rows_out_new, precision=PRECISE)
    gain_grads = jnp.concatenate([d_gains, d_gain_three], axis=0)
    row_sums, col_sums, total_sums, g_gains, g_rel = lax.psum(
        (row_terms, col_terms, row_totals, gain_grads, d_rel), ("dp", "group")
    )
    in_counts = jnp.array([3 * HEAD_COLS, 3 * HEAD_COLS, 2 * FF], jnp.float32)
    out_counts = jnp.array([HEAD_COLS, HEAD_COLS, FF], jnp.float32)
    rows_in_new = DECAY_RATE * rows_in + (1 - DECAY_RATE) * row_sums / in_counts[:, None]
    cols_in_new = DECAY_RATE * cols_in + (1 - DECAY_RATE) * jnp.mean(sq_in, axis=0)
    row_scaled = rows_in_new / jnp.mean(rows_in_new, axis=1, keepdims=True)
    in_scale = jnp.einsum("mc,md->dc", col_hot, row_scaled, precision=PRECISE) * cols_in_new[None, :]
    new_in = w_in - STEP_SIZE * part_in * lax.rsqrt(in_scale)
    cols_out_new = DECAY_RATE * cols_out + (1 - DECAY_RATE) * col_sums / out_counts[:, None]
    row_mean = jnp.dot(row_hot.T, total_sums / out_counts, precision=PRECISE)
    col_pick = jnp.einsum("mr,md->rd", row_hot, cols_out_new, precision=PRECISE)
    new_out = w_out - STEP_SIZE * part_out * lax.rsqrt((rows_out_new / row_mean)[:, None] * col_pick)
    sq_gains_new = DECAY_RATE * sq_gains + (1 - DECAY_RATE) * g_gains * g_gains
    new_gains = norm_gains - PLAIN_STEP * g_gains * lax.rsqrt(sq_gains_new)
    sq_rel_new = DECAY_RATE * sq_rel + (1 - DECAY_RATE) * g_rel * g_rel
    new_rel = rel_bias - PLAIN_STEP * g_rel * lax.rsqrt(sq_rel_new)
    return (
        mixed[None], d_tokens_out, d_memory_out, part_in, part_out, g_gains, g_rel, new_in, new_out, new_gains,
        new_rel, rows_in_new, cols_in_new, rows_out_new, cols_out_new, sq_gains_new, sq_rel_new,
    )


def solution(mesh):
    both = ("dp", "group")
    row_in = P("group", "dp", None)
    seg_in = P("group", "dp")
    return jax.shard_map(
        body,
        mesh=mesh,
        in_specs=(
            row_in, row_in, seg_in, seg_in, P(), P(), P(both, None), P(both, None, None), P(None, both),
            P(both, None), P(), P(), P(), P(both), P(both), P(), P(), P(),
        ),
        out_specs=(
            P(both, None, None), row_in, row_in, P(None, both), P(both, None), P(), P(), P(None, both),
            P(both, None), P(), P(), P(), P(both), P(both), P(), P(), P(),
        ),
        check_vma=False,
    )
```

time: 954 us -> 499 us (0.52)
  local copies, waits for them, and re-layouts: 425 us -> 19 us
  Pallas kernels: 0 us -> 401 us
  waiting for transfers between devices: 172 us -> 0 us
  matrix products: 152 us -> 9.14 us
  other arithmetic: 97.5 us -> 11.4 us
  starting transfers between devices: 35.7 us -> 0 us
  between operations: 18.1 us -> 5.18 us
    pallas_call x0 -> x5, Pallas kernels: none -> 401 us  [the longest x1 140 us: gather_all(): pl.pallas_call(gather_kernel, out_shape=(sds((32 * win_sh.shape[0], WIDTH...]
    unnamed x208 -> x52, local copies, waits for them, and re-layouts: 211 us -> 1.78 us
    dot_general x36 -> x2, matrix products: 145 us -> 1.24 us  [the longest x1 1 us: body(): jnp.dot(rel_pad, np.concatenate([hot_f, hot], axis=0).T, precision=PRECISE)]
    reshape x4 -> x1, local copies, waits for them, and re-layouts: 119 us -> 0.73 us  [body(): slot_table = row_source.reshape(n_index, n_group)]
    reduce_scatter x2 -> x0, waiting for transfers between devices: 93.5 us -> none  [the longest x1 93.5 us: body(): lax.psum_scatter(part_in, 'dp', scatter_dimension=1, tiled=True)]
    unnamed x6 -> x0, waiting for transfers between devices: 64.1 us -> none
    slice x4 -> x1, local copies, waits for them, and re-layouts: 37.1 us -> 0.62 us  [body(): table_f, table_b = (tables[:, :256], tables[:, 256:])]
    all_to_all x6 -> x0, starting transfers between devices: 35.5 us -> none  [the longest x1 8.31 us: body(): lax.all_to_all(sending[2], 'dp', split_axis=0, concat_axis=1, tiled=True)]
  transfers between devices with their start and end apart: 11 -> 0, of which waited for: 5 -> 0; matrix products, arithmetic and copies ran while one was open for 50% -> 0% of each run, Pallas kernels for 0% -> 0%
where the time goes in v1:
time: 499 us; the launch traced here: 494 us
  Pallas kernels  401 us (80%)
  blocking collectives  48.3 us (10%)
  local copies, waits for them, and re-layouts  19 us (4%)
  other arithmetic  11.4 us (2%)
  matrix products  9.14 us (2%)
  between operations  5.18 us (1%)
    pallas_call x1, Pallas kernels, gather_all(): pl.pallas_call(gather_kernel, out_shape=(sds((32 * win_sh.shape[0], WIDTH...  140 us
    pallas_call x1, Pallas kernels, sum_all(): pl.pallas_call(sums_kernel, out_shape=(sds((272, WIDTH), jnp.float32), sd...  129 us
    pallas_call x1, Pallas kernels, backward_call(): vmem_call(kernel, (sds(g_win.shape), sds(g_wout.shape), sds((SEQ, WIDTH))...  64.4 us
    psum x1, blocking collectives, body(): lax.psum((row_terms, col_terms, row_totals, gain_grads, d_rel), ('dp', 'g...  48.3 us
    pallas_call x1, Pallas kernels, forward_call(): vmem_call(kernel, (sds((SEQ, 3 * HEAD_COLS)), sds((SEQ, HEAD_COLS)), sds(...  42.6 us
    pallas_call x1, Pallas kernels, ff_call(): vmem_call(ff_kernel, (sds((SEQ, WIDTH)), sds((SEQ, WIDTH), f32), sds((1,...  24.7 us

profile of v1, /device:TPU:0, one launch (start us, length us, event | category | flops | bytes accessed | tf_op | source)
XLA Modules:
  0.0 493.7 jit_solution(2567269041372278931)
XLA Ops:
  0.7 0.0 copy-start
  0.7 1.3 dynamic_slice.16
  3.9 1.2 dynamic_slice.17
  7.1 0.7 dynamic-slice_bitcast_fusion
  7.8 1.0 fusion.19
  8.8 0.6 fusion.34
  9.4 0.7 reshape.146
  10.2 0.2 fusion.21
  10.4 1.3 gather_fusion.2
  11.7 1.3 gather_fusion.3
  12.9 0.9 fusion.12.aux_s
  13.8 1.5 gather_fusion
  15.3 2.6 gather_fusion.1
  17.9 1.9 convert_bitcast_fusion.win_sh
  19.8 1.7 convert_element_type.27.wout_sh
  21.5 139.6 %shard_map.341 = (bf16[8704,768]{1,0:T(8,128)(2,1)}, bf16[3584,768]{1,0:T(8,128)(2,1)}, bf16[16,32,768]{2,1,0:T(8,128)(2,1)}, bf16[16,32,768]{2,1,0:T(8,128)(2,1)}, bf16[16,32,128]{2,1,0:T(8,128)(2,1)}) custom-call(bf16[272,768]{1,0:T(8,128)(2,1)} %convert_bitcast_fusion.win_sh, bf16[112,768]{1,0:T(8,128)(2,1)} %convert_element_type.27.wout_sh, ...), custom_call_target="tpu_custom_call" | custom-call | tf_op jit(solution)/shard_map/pallas_call | solution.py:786
  161.1 42.6 %shard_map.342 = (bf16[512,2304]{1,0:T(8,128)(2,1)}, bf16[512,768]{1,0:T(8,128)(2,1)}, f32[512,128]{1,0:T(8,128)}, f32[512,768]{1,0:T(8,128)}, bf16[512,768]{1,0...) custom-call(bf16[512,768]{1,0:T(8,128)(2,1)} %bitcast.42, ...), custom_call_target="tpu_custom_call" | custom-call | tf_op jit(solution)/shard_map/pallas_call | solution.py:837
  203.7 0.8 broadcast_in_dim.32.keep
  204.6 24.7 %shard_map.343 = (bf16[512,768]{1,0:T(8,128)(2,1)}, f32[512,768]{1,0:T(8,128)}, f32[1,768]{1,0:T(1,128)}, bf16[8704,768]{1,0:T(8,128)(2,1)}, bf16[3584,768]{1,0:T(8,128)(2,1)}) custom-call(f32[512,768]{1,0:T(8,128)} %get-tuple-element.52.x2, bf16[512,768]{1,0:T(8,128)(2,1)} %bitcast.48, f32[512,128]{1,0:T(8,128)} %broadcast_in_dim.32.keep, ...), custom_call_target="tpu_custom_call" | custom-call | tf_op jit(solution)/shard_map/pallas_call | solution.py:856
  229.3 64.4 %shard_map.344 = (bf16[8704,768]{1,0:T(8,128)(2,1)}, bf16[3584,768]{1,0:T(8,128)(2,1)}, bf16[512,768]{1,0:T(8,128)(2,1)}, bf16[512,768]{1,0:T(8,128)(2,1)}, f32[2,768]{1,0:T(2,128)}, /*index=5*/f32[16,384]{1,0:T(8,128)}) custom-call(bf16[8704,768]{1,0:T(8,128)(2,1)} %get-tuple-element.54._, ...), custom_call_target="tpu_custom_call", output_to_operand_aliasing={{0}: (0, {}), {1}: (1, {})} | custom-call | tf_op jit(solution)/shard_map/pallas_call | solution.py:899
  293.7 0.7 pad_maximum_fusion
  294.5 0.0 copy-start.6
  294.5 0.0 copy-start.22
  294.5 0.0 copy-start.21
  294.6 129.3 %shard_map.345 = (f32[272,768]{1,0:T(8,128)}, f32[112,768]{1,0:T(8,128)}, bf16[16,32,768]{2,1,0:T(8,128)(2,1)}, bf16[16,32,768]{2,1,0:T(8,128)(2,1)}) custom-call(bf16[8704,768]{1,0:T(8,128)(2,1)} %get-tuple-element.65.win_g, bf16[3584,768]{1,0:T(8,128)(2,1)} %get-tuple-element.66.wout_g, bf16[16,32,768]{2,1,0:T(8,128)(2,1)} %bitcast.47, ...), custom_call_target="tpu_custom_call" | custom-call | tf_op jit(solution)/shard_map/pallas_call | solution.py:809
  424.0 1.6 fusion.7
  425.7 1.3 fusion.9
  426.9 1.1 multiply_reduce_fusion.1
  428.1 0.1 convolution_bitcast_fusion.1
  428.2 0.2 fusion.14
  428.5 0.7 compare_convert_fusion
  429.1 0.1 broadcast_multiply_fusion
  429.2 48.3 %all-reduce.1 = (f32[3,768]{1,0:T(4,128)S(1)}, f32[3,32,12]{1,2,0:T(8,128)S(1)}, f32[3,768]{1,0:T(4,128)S(1)}, f32[3,768]{1,0:T(4,128)S(1)}, f32[3]{0:T(128)S(1)}) all-reduce(f32[3,768]{1,0:T(4,128)S(1)} %pad_maximum_fusion, f32[3,32,12]{1,2,0:T(8,128)S(1)} %broadcast_multiply_fusion, ...), channel_id=1, replica_groups=mesh['dp'=16,'group'=2] {'dp','group'}, use_global_device_ids=true, to_apply=%region_1.2 | all-reduce | flops 8067 | bytes 64536 | tf_op jit(solution)/shard_map/psum | solution.py:1016
  477.5 0.0 copy-start.12
  477.5 0.0 copy-start.16
  477.5 0.1 fusion.6
  477.6 0.1 multiply_add_fusion
  477.7 2.1 fusion.5
  479.8 0.2 fusion.33
  480.0 1.3 multiply_reduce_fusion
  481.4 2.7 fusion.2
  484.1 0.6 multiply_subtract_fusion
  484.7 0.6 multiply_subtract_fusion.1
  485.3 1.2 sort.17
  486.6 2.6 gather_fusion.5
  489.2 2.6 gather_fusion.4
  491.8 0.9 copy.45
  492.7 0.7 copy.46
  (59 shorter events, 0.2 us)
Async XLA Ops:
  0.7 13.2 %copy-start = (bf16[16,32,768]{2,1,0:T(8,128)(2,1)S(1)}, bf16[16,32,768]{2,1,0:T(8,128)(2,1)}, u32[]{:S(2)}) copy-start(bf16[16,32,768]{2,1,0:T(8,128)(2,1)} %param.22) | copy-start | bytes 2359300
  161.1 42.6 %copy-start.20 = (s32[1,512]{1,0:T(1,128)S(1)}, s32[1,512]{1,0:T(1,128)}, u32[]{:S(2)}) copy-start(s32[1,512]{1,0:T(1,128)} %param.28) | copy-start | bytes 6148
  229.3 64.4 %copy-start.18 = (f32[1,768]{1,0:T(1,128)S(1)}, f32[1,768]{1,0:T(1,128)}, u32[]{:S(2)}) copy-start(f32[1,768]{1,0:T(1,128)} %get-tuple-element.75) | copy-start | bytes 9220
  294.4 133.6 %copy-start.23 = (f32[112]{0:T(128)S(1)}, f32[112]{0:T(128)}, u32[]{:S(2)}) copy-start(f32[112]{0:T(128)} %param.36) | copy-start | bytes 1348
  294.5 133.7 %copy-start.6 = (f32[384,32]{1,0:T(8,128)S(1)}, f32[384,32]{1,0:T(8,128)}, u32[]{:S(2)}) copy-start(f32[384,32]{1,0:T(8,128)} %constant.115.clone) | copy-start | bytes 147460
  294.5 133.7 %copy-start.10 = (f32[16,384]{1,0:T(8,128)S(1)}, f32[16,384]{1,0:T(8,128)}, u32[]{:S(2)}) copy-start(f32[16,384]{1,0:T(8,128)} %get-tuple-element.76) | copy-start | bytes 73732
  294.5 183.0 %copy-start.22 = (f32[3]{0:T(128)S(1)}, f32[3]{0:T(128)}, u32[]{:S(2)}) copy-start(f32[3]{0:T(128)} %constant.127) | copy-start | bytes 40
  294.5 183.1 %copy-start.13 = (f32[3,768]{1,0:T(4,128)S(1)}, f32[3,768]{1,0:T(4,128)}, u32[]{:S(2)}) copy-start(f32[3,768]{1,0:T(4,128)} %param.37) | copy-start | bytes 27652
  294.5 183.2 %copy-start.4 = (f32[112,768]{1,0:T(8,128)S(1)}, f32[112,768]{1,0:T(8,128)}, u32[]{:S(2)}) copy-start(f32[112,768]{1,0:T(8,128)} %param.31) | copy-start | bytes 1032196
  294.5 185.3 %copy-start.14 = (f32[3,768]{1,0:T(4,128)S(1)}, f32[3,768]{1,0:T(4,128)}, u32[]{:S(2)}) copy-start(f32[3,768]{1,0:T(4,128)} %param.34) | copy-start | bytes 27652
  294.5 185.3 %copy-start.21 = (f32[3]{0:T(128)S(1)}, f32[3]{0:T(128)}, u32[]{:S(2)}) copy-start(f32[3]{0:T(128)} %constant.126) | copy-start | bytes 40
  294.5 186.8 %copy-start.19 = (f32[272]{0:T(512)S(1)}, f32[272]{0:T(512)}, u32[]{:S(2)}) copy-start(f32[272]{0:T(512)} %param.35) | copy-start | bytes 3268
  294.6 186.8 %copy-start.3 = (f32[768,272]{0,1:T(8,128)S(1)}, f32[768,272]{0,1:T(8,128)}, u32[]{:S(2)}) copy-start(f32[768,272]{0,1:T(8,128)} %param.30) | copy-start | bytes 2506756
  423.9 60.2 %copy-start.9 = (f32[3,32,12]{1,2,0:T(8,128)S(1)}, f32[3,32,12]{1,2,0:T(8,128)}, u32[]{:S(2)}) copy-start(f32[3,32,12]{1,2,0:T(8,128)} %param.33) | copy-start | bytes 13828
  423.9 60.2 %copy-start.11 = (f32[3,32,12]{1,2,0:T(8,128)S(1)}, f32[3,32,12]{1,2,0:T(8,128)}, u32[]{:S(2)}) copy-start(f32[3,32,12]{1,2,0:T(8,128)} %param.39) | copy-start | bytes 13828
  423.9 60.8 %copy-start.5 = (f32[3,768]{1,0:T(4,128)S(1)}, f32[3,768]{1,0:T(4,128)}, u32[]{:S(2)}) copy-start(f32[3,768]{1,0:T(4,128)} %refs_0_.3) | copy-start | bytes 27652
  423.9 60.8 %copy-start.15 = (f32[3,768]{1,0:T(4,128)S(1)}, f32[3,768]{1,0:T(4,128)}, u32[]{:S(2)}) copy-start(f32[3,768]{1,0:T(4,128)} %param.38) | copy-start | bytes 27652
  423.9 67.8 %copy-start.1 = (f32[272,768]{1,0:T(8,128)S(1)}, f32[272,768]{1,0:T(8,128)}, u32[]{:S(2)}) copy-start(f32[272,768]{1,0:T(8,128)} %get-tuple-element.72) | copy-start | bytes 2506756
  425.6 67.1 %copy-start.2 = (f32[112,768]{1,0:T(8,128)S(1)}, f32[112,768]{1,0:T(8,128)}, u32[]{:S(2)}) copy-start(f32[112,768]{1,0:T(8,128)} %get-tuple-element.119) | copy-start | bytes 1032196
  428.1 65.3 %copy-start.24 = (f32[112]{0:T(128)}, f32[112]{0:T(128)S(1)}, u32[]{:S(2)}) copy-start(f32[112]{0:T(128)S(1)} %multiply_add_fusion.3) | copy-start | bytes 1348
  477.5 15.9 %copy-start.12 = (f32[3,32,12]{1,2,0:T(8,128)}, f32[3,32,12]{1,2,0:T(8,128)S(1)}, u32[]{:S(2)}) copy-start(f32[3,32,12]{1,2,0:T(8,128)S(1)} %get-tuple-element.121) | copy-start | bytes 13828
  477.5 15.9 %copy-start.16 = (f32[3,768]{1,0:T(4,128)}, f32[3,768]{1,0:T(4,128)S(1)}, u32[]{:S(2)}) copy-start(f32[3,768]{1,0:T(4,128)S(1)} %get-tuple-element.120) | copy-start | bytes 27652
  477.7 15.7 %copy-start.7 = (f32[3,768]{1,0:T(4,128)}, f32[3,768]{1,0:T(4,128)S(1)}, u32[]{:S(2)}) copy-start(f32[3,768]{1,0:T(4,128)S(1)} %multiply_add_fusion) | copy-start | bytes 27652
  480.0 13.4 %copy-start.8 = (f32[3,768]{1,0:T(4,128)}, f32[3,768]{1,0:T(4,128)S(1)}, u32[]{:S(2)}) copy-start(f32[3,768]{1,0:T(4,128)S(1)} %get-tuple-element.126) | copy-start | bytes 27652
  481.4 12.1 %copy-start.17 = (f32[272]{0:T(512)}, f32[272]{0:T(512)S(1)}, u32[]{:S(2)}) copy-start(f32[272]{0:T(512)S(1)} %multiply_add_fusion.2) | copy-start | bytes 3268

commit v2 on v1

--- a/solution.py
+++ b/solution.py
@@ -413,6 +413,9 @@
 )
 
 
+REGION = 400
+
+
 def place():
     dp = lax.axis_index("dp")
     return dp // 4, (dp // 2) % 2, dp % 2, lax.axis_index("group")
@@ -428,8 +431,8 @@
 
 
 class Links:
-    def __init__(self, send_sem, recv_sem):
-        self.send_sem, self.recv_sem, self.count, self.sent = send_sem, recv_sem, 0, []
+    def __init__(self, send_sem, recv_sem, count=0):
+        self.send_sem, self.recv_sem, self.count, self.sent = send_sem, recv_sem, count, []
 
     def reserve(self, n):
         self.count += n
@@ -500,7 +503,8 @@
             def here(yy, xx, first, count, zz=zz, kind=kind):
                 return rows_of(arrays[kind], kind, zz, yy, xx, g, first, count)
 
-            c = {"zz": zz}
+            c = {"zz": zz, "go_up": (z >= zz) & (z < 3), "go_down": (z <= zz) & (z > 0)}
+            c["from_below"], c["from_above"] = z > zz, z < zz
 
             def add(name, ref, device, sem=None, c=c):
                 c[name] = links.copy(ref, ref, device, sem)
@@ -520,11 +524,10 @@
             items.append(c)
 
     def first(c):
-        zz = c["zz"]
-        pl.when(z > zz)(c["up"].wait_recv)
-        pl.when(z < zz)(c["down"].wait_recv)
-        links.start(c["up"], (z >= zz) & (z < 3))
-        links.start(c["down"], (z <= zz) & (z > 0))
+        pl.when(c["from_below"])(c["up"].wait_recv)
+        pl.when(c["from_above"])(c["down"].wait_recv)
+        links.start(c["up"], c["go_up"])
+        links.start(c["down"], c["go_down"])
         for k in ("x", "y", "p"):
             links.start(c[k])
 
@@ -603,143 +606,188 @@
     links.drain()
 
 
-def sums_kernel(win_g, wout_g, dtok, dmem, part_in, part_out, btok, bmem, own, got, gx, gy, fin, gz, final, ss, rs, ls):
-    z, y, x, g = place()
-    me = lax.axis_index("dp")
-    links = Links(ss, rs)
-    moves = ((dmem, bmem), (dtok, btok))
-    mine = [pltpu.make_async_copy(s.at[me], t.at[me], ls.at[k]) for k, (s, t) in enumerate(moves)]
-    for c in mine:
-        c.start()
-    greet(all_peers())
-    queue = []
-    for s, t in moves:
-        for k in range(1, 16):
-            to = lax.rem(me + k, 16)
-            queue.append(links.copy(s.at[to], t.at[me], (to, g)))
-    arrays = {"i": win_g, "o": wout_g}
-    order = [(zz, k) for zz in (3, 0, 2, 1) for k in range(len(PIECES))]
-    cols = ((y, x), (y, 1 - x), (1 - y, x), (1 - y, 1 - x))
-    tot = sum(p[2] for p in PIECES)
-    items = []
-    for zz, k in order:
-        kind, lo, n, half = PIECES[k]
-        base = zz * tot + sum(p[2] for p in PIECES[:k])
-        at = lambda ref, c, off, m, base=base: ref.at[c, pl.ds(base + off, m)]
-        it = {"zz": zz, "n": n, "half": half, "base": base, "kind": kind, "lo": lo}
-        it["load"], it["pair"] = [], []
-        for c, (yy, xx) in enumerate(cols):
-            it["load"].append(
-                pltpu.make_async_copy(
-                    rows_of(arrays[kind], kind, zz, yy, xx, g, lo, n), at(own, c, 0, n), ls.at[2 + 4 * len(items) + c]
+class Sums:
+    def __init__(self, win_g, wout_g, own, got, plane, fin, line, part_in, part_out, load_sem):
+        self.arrays = {"i": win_g, "o": wout_g}
+        self.own, self.got, self.plane, self.fin, self.line = own, got, plane, fin, line
+        self.part_in, self.part_out, self.load_sem = part_in, part_out, load_sem
+        self.loads, self.line_rows = 0, 0
+
+    def batch(self, links, region, members):
+        z, y, x, g = place()
+        base = region * REGION
+        items = []
+        for zz, k in members:
+            kind, lo, n, half = PIECES[k]
+            at = lambda ref, c, off, m, base=base: ref.at[c, pl.ds(base + off, m)]
+            it = {"zz": zz, "n": n, "half": half, "base": base, "kind": kind, "lo": lo, "line": self.line_rows}
+            it["links"] = links
+            it["below"], it["above"], it["z"] = z < zz, z > zz, z
+            it["load"], it["pair"] = [], []
+            for c, (yy, xx) in enumerate(((y, x), (y, 1 - x), (1 - y, x), (1 - y, 1 - x))):
+                ref = self.arrays[kind]
+                it["load"].append(
+                    pltpu.make_async_copy(
+                        rows_of(ref, kind, zz, yy, xx, g, lo, n), at(self.own, c, 0, n), self.load_sem.at[self.loads]
+                    )
                 )
-            )
-            it["pair"].append(
-                links.copy(
-                    rows_of(arrays[kind], kind, zz, yy, xx, 1 - g, lo, n), at(got, c, 0, n), dev(z, y, x, 1 - g)
+                self.loads += 1
+                it["pair"].append(
+                    links.copy(
+                        rows_of(ref, kind, zz, yy, xx, 1 - g, lo, n), at(self.got, c, 0, n), dev(z, y, x, 1 - g)
+                    )
                 )
-            )
-        nx, ny = dev(z, y, 1 - x, g), dev(z, 1 - y, x, g)
-        it["x1"] = [links.copy(at(own, c, 0, half), at(gx, s, 0, half), nx) for s, c in ((0, 1), (1, 3))]
-        it["y1"] = [links.copy(at(own, c, half, n - half), at(gy, s, half, n - half), ny) for s, c in ((0, 2), (1, 3))]
-        it["y2"] = links.copy(at(own, 2, 0, half), at(fin, 0, 0, half), ny)
-        it["x2"] = links.copy(at(own, 1, half, n - half), at(fin, 0, half, n - half), nx)
-        whole = at(own, 0, 0, n)
-        it["up"] = links.copy(whole, at(gz, 0, 0, n), dev(jnp.minimum(z + 1, 3), y, x, g))
-        it["down"] = links.copy(whole, at(gz, 1, 0, n), dev(jnp.maximum(z - 1, 0), y, x, g))
-        items.append(it)
-
-    def add(dst, c, src, s, it, off, m):
-        rows = pl.ds(it["base"] + off, m)
-        dst[c, rows, :] = (dst[c, rows, :].astype(jnp.float32) + src[s, rows, :].astype(jnp.float32)).astype(jnp.bfloat16)
-
-    def stage0(it):
-        for c in it["load"]:
-            c.start()
-        for c in it["pair"]:
-            links.start(c)
-
-    def stage1(it):
+            nx, ny, rest = dev(z, y, 1 - x, g), dev(z, 1 - y, x, g), n - half
+            own, plane, fin = self.own, self.plane, self.fin
+            it["x1"] = [links.copy(at(own, c, 0, half), at(plane, s, 0, half), nx) for s, c in ((0, 1), (1, 3))]
+            it["y1"] = [links.copy(at(own, c, half, rest), at(plane, s, half, rest), ny) for s, c in ((0, 2), (1, 3))]
+            it["y2"] = links.copy(at(own, 2, 0, half), at(fin, 0, 0, half), ny)
+            it["x2"] = links.copy(at(own, 1, half, rest), at(fin, 0, half, rest), nx)
+            there = lambda s: self.line.at[s, pl.ds(it["line"], n)]
+            it["up"] = links.copy(at(own, 0, 0, n), there(0), dev(jnp.minimum(z + 1, 3), y, x, g))
+            it["down"] = links.copy(at(own, 0, 0, n), there(1), dev(jnp.maximum(z - 1, 0), y, x, g))
+            items.append(it)
+            base += n
+            self.line_rows += n
+        assert base <= (region + 1) * REGION
+        n = len(items)
+        lag2, lag3 = 2, 4
+        steps = []
+
+        def begin():
+            for it in items:
+                for c in it["load"]:
+                    c.start()
+                for c in (3, 1, 2, 0):
+                    links.start(it["pair"][c])
+
+        steps.append(begin)
+        for t in range(n + lag3):
+
+            def step(t=t):
+                if t < n:
+                    self.to_core(items[t])
+                if 0 <= t - lag2 < n:
+                    self.to_plane(items[t - lag2])
+                if 0 <= t - lag3 < n:
+                    self.to_line(items[t - lag3])
+
+            steps.append(step)
+        return steps
+
+    @staticmethod
+    def add(dst, c, first, src, s, start, m):
+        rows = pl.ds(first, m)
+        more = src[s, pl.ds(start, m), :].astype(jnp.float32)
+        dst[c, rows, :] = (dst[c, rows, :].astype(jnp.float32) + more).astype(jnp.bfloat16)
+
+    def to_core(self, it):
         for c in (3, 1, 2, 0):
             it["load"][c].wait()
             it["pair"][c].wait_recv()
-            add(own, c, got, c, it, 0, it["n"])
+            self.add(self.own, c, it["base"], self.got, c, it["base"], it["n"])
             if c == 3:
-                links.start(it["x1"][1])
-                links.start(it["y1"][1])
+                it["links"].start(it["x1"][1])
+                it["links"].start(it["y1"][1])
             if c == 1:
-                links.start(it["x1"][0])
+                it["links"].start(it["x1"][0])
             if c == 2:
-                links.start(it["y1"][0])
-
-    def stage2(it):
-        half, rest = it["half"], it["n"] - it["half"]
+                it["links"].start(it["y1"][0])
+
+    def to_plane(self, it):
+        half, rest, base = it["half"], it["n"] - it["half"], it["base"]
+        low = base + half
         it["x1"][1].wait_recv()
-        add(own, 2, gx, 1, it, 0, half)
-        links.start(it["y2"])
+        self.add(self.own, 2, base, self.plane, 1, base, half)
+        it["links"].start(it["y2"])
         it["y1"][1].wait_recv()
-        add(own, 1, gy, 1, it, half, rest)
-        links.start(it["x2"])
+        self.add(self.own, 1, low, self.plane, 1, low, rest)
+        it["links"].start(it["x2"])
         it["x1"][0].wait_recv()
-        add(own, 0, gx, 0, it, 0, half)
+        self.add(self.own, 0, base, self.plane, 0, base, half)
         it["y1"][0].wait_recv()
-        add(own, 0, gy, 0, it, half, rest)
-
-    def stage3(it):
-        zz, n, half = it["zz"], it["n"], it["half"]
+        self.add(self.own, 0, low, self.plane, 0, low, rest)
+
+    def to_line(self, it):
+        z, below, above = it["z"], it["below"], it["above"]
+        zz, n, base, line = it["zz"], it["n"], it["base"], it["line"]
         it["y2"].wait_recv()
         it["x2"].wait_recv()
-        add(own, 0, fin, 0, it, 0, n)
-
-        @pl.when(z < zz)
-        def _():
-            @pl.when(z > 0)
+        self.add(self.own, 0, base, self.fin, 0, base, n)
+        up, down = it["up"], it["down"]
+        if zz > 0:
+
+            @pl.when(below)
             def _():
-                it["up"].wait_recv()
-                add(own, 0, gz, 0, it, 0, n)
-
-            it["up"].start()
-
-        @pl.when(z > zz)
-        def _():
-            @pl.when(z < 3)
+                @pl.when(z > 0)
+                def _():
+                    up.wait_recv()
+                    self.add(self.own, 0, base, self.line, 0, line, n)
+
+                up.start()
+
+            it["links"].sent.append((up, below))
+        if zz < 3:
+
+            @pl.when(above)
             def _():
-                it["down"].wait_recv()
-                add(own, 0, gz, 1, it, 0, n)
-
-            it["down"].start()
-
-        links.sent.append((it["up"], z < zz))
-        links.sent.append((it["down"], z > zz))
+                @pl.when(z < 3)
+                def _():
+                    down.wait_recv()
+                    self.add(self.own, 0, base, self.line, 1, line, n)
+
+                down.start()
+
+            it["links"].sent.append((down, above))
 
         @pl.when(z == zz)
         def _():
-            rows = pl.ds(it["base"], n)
-            total = own[0, rows, :].astype(jnp.float32)
+            total = self.own[0, pl.ds(base, n), :].astype(jnp.float32)
             if zz > 0:
-                it["up"].wait_recv()
-                total += gz[0, rows, :].astype(jnp.float32)
+                up.wait_recv()
+                total += self.line[0, pl.ds(line, n), :].astype(jnp.float32)
             if zz < 3:
-                it["down"].wait_recv()
-                total += gz[1, rows, :].astype(jnp.float32)
-            into = part_in if it["kind"] == "i" else part_out
+                down.wait_recv()
+                total += self.line[1, pl.ds(line, n), :].astype(jnp.float32)
+            into = self.part_in if it["kind"] == "i" else self.part_out
             into[it["lo"] : it["lo"] + n, :] = total
 
-    lags = (0, 2, 4, 6)
-    stages = (stage0, stage1, stage2, stage3)
-    n = len(items)
-    per = -(-len(queue) // n)
-    for t in range(n + lags[-1]):
-        for lag, stage in zip(lags, stages):
-            if 0 <= t - lag < n:
-                stage(items[t - lag])
-        for c in queue[t * per : (t + 1) * per]:
-            links.start(c)
-    for c in queue:
-        c.wait_recv()
-    for c in mine:
-        c.wait()
-    links.drain()
+
+def total_steps(links, ref, room):
+    z, y, x, g = place()
+    hops = [dev(z, y, x, 1 - g), dev(z, y, 1 - x, g), dev(z, 1 - y, x, g)]
+    copies = [links.copy(ref, room.at[k], to) for k, to in enumerate(hops)]
+    over = [links.copy(ref, room.at[2 + k], dev(lax.rem(z + k, 4), y, x, g)) for k in (1, 2, 3)]
+
+    def hop(k):
+        def step():
+            if k > 0:
+                copies[k - 1].wait()
+                ref[...] = ref[...] + room[k - 1]
+            copies[k].start()
+
+        return step
+
+    def spread():
+        copies[2].wait()
+        ref[...] = ref[...] + room[2]
+        for c in over:
+            c.start()
+
+    def finish():
+        for c in over:
+            c.wait()
+        mine = ref[...]
+        total = jnp.zeros_like(mine)
+        for plane in range(4):
+            back = lax.rem(z - plane + 4, 4)
+            term = jnp.where(back == 0, mine, jnp.zeros_like(mine))
+            for k in (1, 2, 3):
+                term = jnp.where(back == k, room[2 + k], term)
+            total = total + term
+        ref[...] = total
+
+    return [hop(0), hop(1), hop(2), spread, finish]
 
 
 def vmem_call(kernel, out_shape, scratch, **kw):
@@ -800,28 +848,168 @@
     )(win_sh, wout_sh, tok_s, mem_s, aux_s)
 
 
-def sum_all(g_win, g_wout, d_tok, d_mem):
-    any_ = pl.BlockSpec(memory_space=pl.ANY)
-    tot = 4 * sum(p[2] for p in PIECES)
-    items = 4 * len(PIECES)
-    sems = 30 + 12 * items
-    vm = lambda k: pltpu.VMEM((k, tot, WIDTH), jnp.bfloat16)
-    return pl.pallas_call(
-        sums_kernel,
-        out_shape=(
-            sds((272, WIDTH), jnp.float32), sds((112, WIDTH), jnp.float32), sds(d_tok.shape), sds(d_mem.shape),
+def spread_steps(calls, steps):
+    out, done = [], 0
+    for k in range(calls):
+        upto = -(-len(steps) * (k + 1) // calls)
+        out.append(steps[done:upto])
+        done = upto
+    return out
+
+
+def run(steps):
+    for s in steps:
+        s()
+
+
+def block_of(ids, edges):
+    return (ids >= edges[0]).astype(jnp.int32) + (ids >= edges[1]).astype(jnp.int32)
+
+
+IN_EDGES = (3 * HEAD_COLS, 6 * HEAD_COLS)
+OUT_EDGES = (HEAD_COLS, 2 * HEAD_COLS)
+
+
+def block_sums(part_in_t, part_out, rows_out, first_in, first_out):
+    sq_in, sq_out = part_in_t * part_in_t, part_out * part_out
+    block_in = block_of(first_in + lax.broadcasted_iota(jnp.int32, (sq_in.shape[0], 1), 0), IN_EDGES)
+    block_out = block_of(first_out + lax.broadcasted_iota(jnp.int32, (sq_out.shape[0], 1), 0), OUT_EDGES)
+    rows_new = DECAY_RATE * rows_out + (1 - DECAY_RATE) * jnp.mean(sq_out, axis=1, keepdims=True)
+    lane = lax.broadcasted_iota(jnp.int32, (1, WIDTH), 1)
+    lines = [jnp.sum(jnp.where(block_in == k, sq_in, 0.0), axis=0, keepdims=True) for k in range(3)]
+    lines += [jnp.sum(jnp.where(block_out == k, sq_out, 0.0), axis=0, keepdims=True) for k in range(3)]
+    totals = jnp.zeros((1, WIDTH), jnp.float32)
+    for k in range(3):
+        total = jnp.sum(jnp.where(block_out == k, rows_new, 0.0), axis=0, keepdims=True)
+        totals = jnp.where(lane == k, total, totals)
+    return jnp.concatenate(lines + [totals, jnp.zeros((1, WIDTH), jnp.float32)], axis=0)
+
+
+def prep_kernel(
+    ids, row_source, modes, tokens, memory, segments, msegments, w_in, w_out, rel_bias, hot, sentinel,
+    tok_s, mem_s, aux_s, win_sh, wout_sh, tables, keep, flip, seg_t, mseg_t,
+):
+    half_rows, length = tokens.shape[0], tokens.shape[1]
+    groups, group, where = ids[0], ids[1], ids[2]
+    flip[:, 0 : w_in.shape[1]] = w_in[...]
+    win_sh[...] = flip[...].T[0 : w_in.shape[1], :].astype(jnp.bfloat16)
+    wout_sh[...] = w_out[...].astype(jnp.bfloat16)
+    for source, out in ((segments, seg_t), (msegments, mseg_t)):
+        out[0:half_rows, 0:length] = source[...].astype(jnp.float32)
+        out[...] = out[...].T
+    lane = lax.broadcasted_iota(jnp.int32, (length, 128), 1)
+    spot = (lane & (HSIZE - 1)).astype(jnp.float32)
+
+    @pl.loop(0, half_rows)
+    def _(i):
+        source = row_source[i * groups + group] - group * half_rows
+        tok_s[i] = tokens[source]
+        mem_s[i] = memory[source]
+        col = jnp.sum(jnp.where(lane == source, seg_t[0:length, :], 0.0), axis=1, keepdims=True)
+        mcol = jnp.sum(jnp.where(lane == source, mseg_t[0:length, :], 0.0), axis=1, keepdims=True)
+        same = ((spot < SEGS) & (spot == col)) | ((spot >= SEGS) & (spot < 2 * SEGS) & (spot - SEGS == mcol))
+        aux_s[i] = jnp.where(same, 1.0, 0.0).astype(jnp.bfloat16)
+
+    mode = modes[row_source[where]]
+    tables[...] = jnp.zeros_like(tables)
+    tables[0:HEADS, :] = lax.dot_general(
+        rel_bias[mode], hot[...], (((0,), (0,)), ((), ())), precision=PRECISE, preferred_element_type=jnp.float32
+    )
+    kept = (1 - sentinel[...]).astype(jnp.float32)
+    keep[...] = jnp.broadcast_to(kept, (128, SEQ)).T
+
+
+def prep_call(ids, row_source, modes, tokens, memory, segments, msegments, w_in, w_out, rel_bias, hot, sentinel):
+    f32 = jnp.float32
+    scalars = pl.BlockSpec(memory_space=pltpu.SMEM)
+    half_rows, length = tokens.shape[0], tokens.shape[1]
+    padded = -(-w_in.shape[1] // 128) * 128
+    return vmem_call(
+        prep_kernel,
+        (
+            sds(tokens.shape), sds(memory.shape), sds((half_rows, length, 128)), sds((w_in.shape[1], WIDTH)),
+            sds(w_out.shape), sds((16, 512), f32), sds((SEQ, 128), f32),
         ),
-        in_specs=[any_] * 4,
-        out_specs=(whole(), whole(), any_, any_),
-        scratch_shapes=[
-            vm(4), vm(4), vm(2), vm(2), vm(1), vm(2), pltpu.VMEM((8, 128), jnp.float32),
-            pltpu.SemaphoreType.DMA((sems,)), pltpu.SemaphoreType.DMA((sems,)),
-            pltpu.SemaphoreType.DMA((2 + 4 * items,)),
-        ],
-        compiler_params=pltpu.CompilerParams(
-            collective_id=2, has_side_effects=True, vmem_limit_bytes=VMEM_BYTES
+        [pltpu.VMEM((WIDTH, padded), f32), pltpu.VMEM((128, 128), f32), pltpu.VMEM((128, 128), f32)],
+        in_specs=[scalars] * 3 + [whole()] * 9,
+    )(ids, row_source, modes, tokens, memory, segments, msegments, w_in, w_out, rel_bias, hot, sentinel)
+
+
+def update_kernel(
+    ids, row_source, part_in_t, part_out, sums, early, back_tok, back_mem, w_in, w_out, gains, rel_bias, rows_in,
+    cols_in, rows_out, cols_out, sq_gains, sq_rel,
+    d_tokens, d_memory, grad_in, grad_out, grad_gains, grad_rel, new_in, new_out, new_gains, new_rel, rows_in_new,
+    cols_in_new, rows_out_new, cols_out_new, sq_gains_new, sq_rel_new, flip,
+):
+    half_rows = back_tok.shape[0]
+    groups, group, where = ids[0], ids[1], ids[2]
+
+    @pl.loop(0, half_rows)
+    def _(i):
+        source = row_source[i * groups + group] - group * half_rows
+        d_tokens[source] = back_tok[i]
+        d_memory[source] = back_mem[i]
+
+    n_in, n_out = w_in.shape[1], w_out.shape[0]
+    flip[0:n_in, :] = part_in_t[...]
+    part_in = flip[...].T[:, 0:n_in]
+    grad_in[...] = part_in
+    cols_new = DECAY_RATE * cols_in[...] + (1 - DECAY_RATE) * jnp.mean(part_in * part_in, axis=0, keepdims=True)
+    cols_in_new[...] = cols_new
+    rows_new, scaled = [], []
+    for k, count in enumerate((3 * HEAD_COLS, 3 * HEAD_COLS, 2 * FF)):
+        row = DECAY_RATE * rows_in[k : k + 1, :] + (1 - DECAY_RATE) * (sums[k : k + 1, :] / count)
+        rows_in_new[k : k + 1, :] = row
+        scaled.append(row / jnp.mean(row, axis=1, keepdims=True))
+    upright = jnp.concatenate(scaled + [jnp.zeros((128 - 3, WIDTH), jnp.float32)], axis=0).T
+    block_in = block_of(where * n_in + lax.broadcasted_iota(jnp.int32, (1, n_in), 1), IN_EDGES)
+    spread = jnp.where(block_in == 0, upright[:, 0:1], jnp.where(block_in == 1, upright[:, 1:2], upright[:, 2:3]))
+    new_in[...] = w_in[...] - STEP_SIZE * part_in * lax.rsqrt(spread * cols_new)
+
+    p_out = part_out[...]
+    grad_out[...] = p_out
+    out_rows = DECAY_RATE * rows_out[...] + (1 - DECAY_RATE) * jnp.mean(p_out * p_out, axis=1, keepdims=True)
+    rows_out_new[...] = out_rows
+    block_out = block_of(where * n_out + lax.broadcasted_iota(jnp.int32, (n_out, 1), 0), OUT_EDGES)
+    scale = jnp.zeros((n_out, WIDTH), jnp.float32)
+    for k, count in enumerate((HEAD_COLS, HEAD_COLS, FF)):
+        col = DECAY_RATE * cols_out[k : k + 1, :] + (1 - DECAY_RATE) * (sums[3 + k : 4 + k, :] / count)
+        cols_out_new[k : k + 1, :] = col
+        mean = sums[6:7, k : k + 1] / count
+        scale = jnp.where(block_out == k, (out_rows / mean) * col, scale)
+    new_out[...] = w_out[...] - STEP_SIZE * p_out * lax.rsqrt(scale)
+
+    g = early[0:3, :]
+    grad_gains[...] = g
+    sq = DECAY_RATE * sq_gains[...] + (1 - DECAY_RATE) * g * g
+    sq_gains_new[...] = sq
+    new_gains[...] = gains[...] - PLAIN_STEP * g * lax.rsqrt(sq)
+    for k in range(MODES):
+        both = jnp.concatenate([early[8:24, k * 128 : (k + 1) * 128], jnp.zeros((112, 128), jnp.float32)], axis=0)
+        g = both.T[0:BUCKETS, 0:HEADS]
+        grad_rel[k] = g
+        sq = DECAY_RATE * sq_rel[k] + (1 - DECAY_RATE) * g * g
+        sq_rel_new[k] = sq
+        new_rel[k] = rel_bias[k] - PLAIN_STEP * g * lax.rsqrt(sq)
+
+
+def update_call(ids, row_source, *arrays):
+    f32 = jnp.float32
+    scalars = pl.BlockSpec(memory_space=pltpu.SMEM)
+    (part_in_t, part_out, sums, early, back_tok, back_mem, w_in, w_out, gains, rel_bias) = arrays[:10]
+    n_in, n_out = w_in.shape[1], w_out.shape[0]
+    three = sds((3, WIDTH), f32)
+    rel = sds(rel_bias.shape, f32)
+    return vmem_call(
+        update_kernel,
+        (
+            sds(back_tok.shape), sds(back_mem.shape), sds(w_in.shape, f32), sds(w_out.shape, f32), three, rel,
+            sds(w_in.shape, f32), sds(w_out.shape, f32), three, rel, three, sds((1, n_in), f32), sds((n_out, 1), f32),
+            three, three, rel,
         ),
-    )(g_win, g_wout, d_tok, d_mem)
+        [pltpu.VMEM((-(-n_in // 128) * 128, WIDTH), f32)],
+        in_specs=[scalars] * 2 + [whole()] * len(arrays),
+    )(ids, row_source, *arrays)
 
 
 def forward_call(tok, mem, aux, win, wout, gains, table):
@@ -872,46 +1060,172 @@
     )(x2, cot, keep, gains, win, win, wout)
 
 
-def backward_call(tok, mem, aux, win, wout, gains, table, kept, g2, g_win, g_wout):
-    f32 = jnp.float32
-
-    def kernel(_, __, tok, mem, aux, win, wout, *refs):
-        ins, (g_win, g_wout), outs = refs[:11], refs[11:13], refs[13:17]
-        scratch, (held, put_sem, win_v, wout_v, sem) = refs[17:21], refs[21:]
-        loads = load_weights(win, wout, win_v, wout_v, sem)
-        puts = []
-
-        def emit(block, value):
-            held[block] = value.astype(jnp.bfloat16)
-            into, first = (g_win, block) if block < 6 else (g_wout, block - 6)
-            rows = pl.ds(first * HEAD_COLS, HEAD_COLS)
-            puts.append(pltpu.make_async_copy(held.at[block], into.at[rows], put_sem.at[block]))
-            puts[-1].start()
-
-        for c in loads:
-            c.wait()
-        attention_backward(
-            tok, mem, aux, win_v, wout_v, *ins, *outs, *scratch, emit=emit, step=lambda name, p: None
+def rel_sums(dist, hot_dist, mode_rows):
+    by_bucket = jnp.dot(dist, hot_dist, precision=PRECISE, preferred_element_type=jnp.float32)
+    return jnp.concatenate([by_bucket * mode_rows[k : k + 1, :] for k in range(MODES)], axis=1)
+
+
+def backward_kernel(boxed, _, __, tok, mem, aux, win, wout, *refs):
+    ins, (hot_dist, mode_rows, gain_three, rows_out) = refs[:11], refs[11:15]
+    refs = refs[15:]
+    if boxed:
+        (g_win, g_wout, part_in, part_out, sums, early, btok, bmem), refs = refs[:8], refs[8:]
+        (d_mem, d_tok, d_gains, dist), refs = refs[:4], refs[4:]
+    else:
+        (g_win, g_wout, d_mem, d_tok, early), refs = refs[:5], refs[5:]
+        (d_gains, dist), refs = refs[:2], refs[2:]
+    scratch, (held, put_sem, win_v, wout_v, sem), refs = refs[:4], refs[4:9], refs[9:]
+    loads = load_weights(win, wout, win_v, wout_v, sem)
+    puts, settled = [], []
+
+    def settle(upto):
+        while len(settled) < upto:
+            puts[len(settled)].wait()
+            settled.append(True)
+
+    def emit(block, value):
+        k = len(puts)
+        settle(k - 2)
+        held[k % 3] = value.astype(jnp.bfloat16)
+        into, first = (g_win, block) if block < 6 else (g_wout, block - 6)
+        puts.append(
+            pltpu.make_async_copy(
+                held.at[k % 3], into.at[pl.ds(first * HEAD_COLS, HEAD_COLS)], put_sem.at[k]
+            )
         )
-        for c in puts:
-            c.wait()
-
-    return vmem_call(
-        kernel,
-        (
-            sds(g_win.shape), sds(g_wout.shape), sds((SEQ, WIDTH)), sds((SEQ, WIDTH)),
-            sds((2, WIDTH), f32), sds((16, 384), f32),
-        ),
-        [
-            pltpu.VMEM((SEQ, HEAD_COLS), jnp.bfloat16), pltpu.VMEM((SEQ, 3 * HEAD_COLS), jnp.bfloat16),
-            pltpu.VMEM((2, 128, SEQ), f32), pltpu.VMEM((2, 128, 384), f32),
-            pltpu.VMEM((8, HEAD_COLS, WIDTH), jnp.bfloat16), pltpu.SemaphoreType.DMA((8,)),
+        puts[k].start()
+
+    dist[...] = jnp.zeros_like(dist)
+    step = lambda name, p: None
+    if boxed:
+        own, got, plane, fin, line, room, early_room, ss, rs, load_sem = refs
+        z, y, x, g = place()
+        me = lax.axis_index("dp")
+        pos = SEQ // 16
+        greet(all_peers())
+        work = Sums(g_win, g_wout, own, got, plane, fin, line, part_in, part_out, load_sem)
+        n = len(PIECES)
+        groups = (
+            (0, [(3, k) for k in range(n)]),
+            (1, [(2, k) for k in range(n)]),
+            (0, [(1, k) for k in range(2, n)] + [(0, k) for k in range(4, n)]),
+            (1, [(0, k) for k in range(4)] + [(1, k) for k in range(2)]),
+        )
+        links, batches = [Links(ss, rs)], []
+        for region, members in groups:
+            batches.append(work.batch(links[-1], region, members))
+            links.append(Links(ss, rs, links[-1].count))
+        back = links[-1]
+
+        def row_copies(src, dst):
+            copies = []
+            for k in range(1, 16):
+                to = lax.rem(me + k, 16)
+                here = src.at[pl.ds(pl.multiple_of(to * pos, 16), pos)]
+                copies.append(back.copy(here, dst.at[me], (to, g)))
+            return copies
+
+        def keep_rows(src, dst, k):
+            return pltpu.make_async_copy(src.at[pl.ds(pl.multiple_of(me * pos, 16), pos)], dst.at[me], sem.at[2 + k])
+
+        mem_copies, tok_copies = row_copies(d_mem, bmem), row_copies(d_tok, btok)
+        kept_mem, kept_tok = keep_rows(d_mem, bmem, 0), keep_rows(d_tok, btok, 1)
+
+        def begin_third():
+            links[0].drain()
+            batches[2][0]()
+
+        first = spread_steps(6, batches[0][1:])
+        second = spread_steps(6, batches[1][1:] + [begin_third] + batches[2][1:6])
+        rest = batches[2][6:]
+        batches[0][0]()
+
+        def step(name, p):
+            if name == "middle":
+                kept_mem.start()
+                settle(len(puts))
+                batches[1][0]()
+                return
+            for k, part in enumerate(first if name == "cross" else second):
+
+                @pl.when(p == k)
+                def _(part=part, k=k):
+                    if name == "self":
+                        for c in mem_copies[3 * k : 3 * k + 3]:
+                            back.start(c)
+                    run(part)
+
+    for c in loads:
+        c.wait()
+    attention_backward(
+        tok, mem, aux, win_v, wout_v, *ins, d_mem, d_tok, d_gains, dist, *scratch, emit=emit, step=step
+    )
+    early[...] = jnp.zeros_like(early)
+    early[0:2, :] = d_gains[0:2, :]
+    early[2:3, :] = gain_three[...]
+    early[8:24, 0:384] = rel_sums(dist[...], hot_dist[...], mode_rows[...])
+    settle(len(puts))
+    if not boxed:
+        return
+    kept_tok.start()
+    links[1].drain()
+    batches[3][0]()
+    run(rest)
+    turns = total_steps(back, early, early_room)
+    last = batches[3][1:]
+    for k, part in enumerate(last):
+        part()
+        if k < len(turns):
+            turns[k]()
+        for c in tok_copies[3 * k : 3 * k + 3]:
+            back.start(c)
+    where = me * 2 + g
+    sums[...] = block_sums(part_in[...], part_out[...], rows_out[...], where * 272, where * 112)
+    run(total_steps(back, sums, room))
+    for c in mem_copies + tok_copies:
+        c.wait_recv()
+    kept_mem.wait()
+    kept_tok.wait()
+    for k in range(2, 5):
+        links[k].drain()
+
+
+def backward_call(boxed, tok, mem, aux, win, wout, gains, table, kept, g2, g_win, g_wout, *more):
+    f32, bf16 = jnp.float32, jnp.bfloat16
+    vm, dma = pltpu.VMEM, pltpu.SemaphoreType.DMA
+    row = sds((SEQ, WIDTH))
+    rows = [vm((SEQ, WIDTH), bf16), vm((SEQ, WIDTH), bf16)]
+    scratch = [vm((8, WIDTH), f32), vm((16, 384), f32)]
+    scratch += [
+        vm((SEQ, HEAD_COLS), bf16), vm((SEQ, 3 * HEAD_COLS), bf16), vm((2, 128, SEQ), f32), vm((2, 128, 384), f32),
+        vm((3, HEAD_COLS, WIDTH), bf16), dma((8,)),
+    ]
+    scratch += WEIGHTS[:2] + [dma((4,))]
+    outs = [sds(g_win.shape), sds(g_wout.shape)]
+    if boxed:
+        items, both = 4 * len(PIECES), 2 * REGION
+        chunks = sds((16, SEQ // 16, WIDTH))
+        outs += [sds((272, WIDTH), f32), sds((112, WIDTH), f32), sds((8, WIDTH), f32), sds((24, WIDTH), f32), chunks, chunks]
+        specs = (anywhere(),) * 2 + (whole(),) * 4 + (anywhere(),) * 2
+        scratch = rows + scratch
+        scratch += [
+            vm((4, both, WIDTH), bf16), vm((4, both, WIDTH), bf16), vm((2, both, WIDTH), bf16),
+            vm((1, both, WIDTH), bf16), vm((2, 4 * 384, WIDTH), bf16), vm((6, 8, WIDTH), f32), vm((6, 24, WIDTH), f32),
+            dma((12 * items + 48,)), dma((12 * items + 48,)), dma((4 * items,)),
         ]
-        + WEIGHTS,
-        in_specs=[anywhere()] * 2 + [whole()] * 3 + [anywhere()] * 2 + [whole()] * 11,
-        out_specs=(anywhere(), anywhere()) + (whole(),) * 4,
+    else:
+        outs += [row, row, sds((24, WIDTH), f32)]
+        specs = (anywhere(),) * 2 + (whole(),) * 3
+    extra = dict(collective_id=2, has_side_effects=True) if boxed else {}
+    return pl.pallas_call(
+        functools.partial(backward_kernel, boxed),
+        out_shape=tuple(outs),
+        scratch_shapes=scratch,
+        in_specs=[anywhere()] * 2 + [whole()] * 3 + [anywhere()] * 2 + [whole()] * 15,
+        out_specs=specs,
         input_output_aliases={0: 0, 1: 1},
-    )(g_win, g_wout, tok, mem, aux, win, wout, gains, table, *kept, g2)
+        compiler_params=pltpu.CompilerParams(vmem_limit_bytes=VMEM_BYTES, **extra),
+    )(g_win, g_wout, tok, mem, aux, win, wout, gains, table, *kept, g2, *more)
 
 
 def body(
@@ -926,17 +1240,15 @@
     rows_dev = cotangent.shape[0]
     assert rows_dev == 1
     boxed = n_index == 16 and n_group == 2
-    slot_table = row_source.reshape(n_index, n_group)
-    sources = lax.dynamic_index_in_dim(slot_table, my_group, 1, keepdims=False) - my_group * half_rows
-    own_row = lax.dynamic_index_in_dim(row_source, my_place, 0, keepdims=False)
-    own_mode = lax.dynamic_index_in_dim(denoiser_modes, own_row, 0, keepdims=False)
-
-    spot = jnp.arange(128) % HSIZE
-    both = jnp.where(spot < SEGS, segments[sources][:, :, None], memory_segments[sources][:, :, None])
-    aux_s = ((both == spot % SEGS) & (spot < 2 * SEGS)).astype(jnp.bfloat16)
-    win_sh = w_in.T.astype(jnp.bfloat16)
-    wout_sh = w_out.astype(jnp.bfloat16)
-    tok_s, mem_s = tokens[sources], memory[sources]
+    ids = jnp.stack([jnp.int32(n_group), my_group, my_place])
+    buckets = bucket_table(SEQ, BUCKETS)
+    hot = (buckets[:256, None] == np.arange(BUCKETS)[None, :]).astype(np.float32)
+    lane = np.arange(256)
+    dist_f = np.where(lane <= 128, 128 - lane, 384 - lane)
+    hot_t = jnp.asarray(np.concatenate([hot[dist_f], hot], axis=0).T)
+    tok_s, mem_s, aux_s, win_sh, wout_sh, tables, keep = prep_call(
+        ids, row_source, denoiser_modes, tokens, memory, segments, memory_segments, w_in, w_out, rel_bias, hot_t, sentinel
+    )
     if boxed:
         win, wout, tok, mem, aux = gather_all(win_sh, wout_sh, tok_s, mem_s, aux_s)
     else:
@@ -947,93 +1259,48 @@
         )
     tok, mem, aux = tok.reshape(SEQ, WIDTH), mem.reshape(SEQ, WIDTH), aux.reshape(SEQ, 128)
 
-    buckets = bucket_table(SEQ, BUCKETS)
-    hot = (buckets[:256, None] == np.arange(BUCKETS)[None, :]).astype(np.float32)
-    lane = np.arange(256)
-    dist_f = np.where(lane <= 128, 128 - lane, 384 - lane)
-    hot_f = hot[dist_f]
-    rel_row = lax.dynamic_index_in_dim(rel_bias, own_mode, 0, keepdims=False)
-    rel_pad = jnp.pad(rel_row.T, ((0, 4), (0, 0)))
-    tables = jnp.dot(rel_pad, np.concatenate([hot_f, hot], axis=0).T, precision=PRECISE)
     table_f, table_b = tables[:, :256], tables[:, 256:]
-
     kept = forward_call(tok, mem, aux, win, wout, norm_gains, table_f)
     x2 = kept[8]
-    keep = jnp.broadcast_to((1 - sentinel).astype(jnp.float32).reshape(SEQ, 1), (SEQ, 128))
     mixed, g2, d_gain_three, g_win, g_wout = ff_call(
         x2, cotangent.reshape(SEQ, WIDTH), keep, norm_gains, win, wout
     )
-    g_win, g_wout, d_mem, d_tok, d_gains, dist = backward_call(
-        tok, mem, aux, win, wout, norm_gains, table_b, kept[:8], g2, g_win, g_wout
+    hot_dist = np.concatenate([hot, np.repeat(np.eye(BUCKETS, dtype=np.float32)[-1:], 128, axis=0)], axis=0)
+    hot_dist = jnp.asarray(np.pad(hot_dist, ((0, 0), (0, 128 - BUCKETS))))
+    own_mode = denoiser_modes[row_source[my_place]]
+    mode_rows = jnp.broadcast_to((own_mode == jnp.arange(8)).astype(jnp.float32)[:, None], (8, 128))
+    rows_out_up = rows_out.reshape(-1, 1)
+    result = backward_call(
+        boxed, tok, mem, aux, win, wout, norm_gains, table_b, kept[:8], g2, g_win, g_wout,
+        hot_dist, mode_rows, d_gain_three, rows_out_up,
     )
-    d_tok, d_mem = d_tok.reshape(tok_s.shape), d_mem.reshape(mem_s.shape)
     if boxed:
-        part_in_t, part_out, back_tok, back_mem = sum_all(g_win, g_wout, d_tok, d_mem)
+        _, _, part_in_t, part_out, sums, early, back_tok, back_mem = result
     else:
+        g_win, g_wout, d_mem, d_tok, early = result
         back_tok, back_mem = (
-            lax.all_to_all(v, "dp", split_axis=0, concat_axis=0, tiled=True) for v in (d_tok, d_mem)
+            lax.all_to_all(v.reshape(tok_s.shape), "dp", split_axis=0, concat_axis=0, tiled=True)
+            for v in (d_tok, d_mem)
         )
         part_in_t, part_out = (
             lax.psum_scatter(v.astype(jnp.float32), ("dp", "group"), scatter_dimension=0, tiled=True)
             for v in (g_win, g_wout)
         )
-    part_in = part_in_t.T
-    inverse = jnp.argsort(sources)
-    merge = lambda v: v.reshape(n_index, SEQ // n_index, WIDTH)[inverse]
-    d_tokens_out, d_memory_out = merge(back_tok), merge(back_mem)
-    hot_dist = np.concatenate([hot, np.repeat(np.eye(BUCKETS, dtype=np.float32)[-1:], 128, axis=0)], axis=0)
-    d_rel_row = jnp.dot(dist[:HEADS], hot_dist, precision=PRECISE).T
-    mode_hot = (own_mode == jnp.arange(MODES)).astype(jnp.float32)
-    d_rel = mode_hot[:, None, None] * d_rel_row[None]
-
-    col_count = part_in.shape[1]
-    col_ids = my_place * col_count + jnp.arange(col_count)
-    col_hot = jnp.stack(
-        [
-            col_ids < 3 * HEAD_COLS,
-            (col_ids >= 3 * HEAD_COLS) & (col_ids < 6 * HEAD_COLS),
-            col_ids >= 6 * HEAD_COLS,
-        ],
-        axis=0,
-    ).astype(jnp.float32)
-    sq_in = part_in * part_in
-    row_terms = jnp.einsum("mc,dc->md", col_hot, sq_in, precision=PRECISE)
-    row_count = part_out.shape[0]
-    row_ids = my_place * row_count + jnp.arange(row_count)
-    row_hot = jnp.stack(
-        [
-            row_ids < HEAD_COLS,
-            (row_ids >= HEAD_COLS) & (row_ids < 2 * HEAD_COLS),
-            row_ids >= 2 * HEAD_COLS,
-        ],
-        axis=0,
-    ).astype(jnp.float32)
-    sq_out = part_out * part_out
-    rows_out_new = DECAY_RATE * rows_out + (1 - DECAY_RATE) * jnp.mean(sq_out, axis=1)
-    col_terms = jnp.einsum("mr,rd->md", row_hot, sq_out, precision=PRECISE)
-    row_totals = jnp.dot(row_hot, rows_out_new, precision=PRECISE)
-    gain_grads = jnp.concatenate([d_gains, d_gain_three], axis=0)
-    row_sums, col_sums, total_sums, g_gains, g_rel = lax.psum(
-        (row_terms, col_terms, row_totals, gain_grads, d_rel), ("dp", "group")
+        sums = block_sums(
+            part_in_t, part_out, rows_out_up, my_place * part_in_t.shape[0], my_place * part_out.shape[0]
+        )
+        sums, early = lax.psum((sums, early), ("dp", "group"))
+    (
+        d_tokens, d_memory, grad_in, grad_out, grad_gains, grad_rel, new_in, new_out, new_gains, new_rel,
+        rows_in_new, cols_in_new, rows_out_new, cols_out_new, sq_gains_new, sq_rel_new,
+    ) = update_call(
+        ids, row_source, part_in_t, part_out, sums, early, back_tok, back_mem, w_in, w_out, norm_gains, rel_bias,
+        rows_in, cols_in.reshape(1, -1), rows_out_up, cols_out, sq_gains, sq_rel,
     )
-    in_counts = jnp.array([3 * HEAD_COLS, 3 * HEAD_COLS, 2 * FF], jnp.float32)
-    out_counts = jnp.array([HEAD_COLS, HEAD_COLS, FF], jnp.float32)
-    rows_in_new = DECAY_RATE * rows_in + (1 - DECAY_RATE) * row_sums / in_counts[:, None]
-    cols_in_new = DECAY_RATE * cols_in + (1 - DECAY_RATE) * jnp.mean(sq_in, axis=0)
-    row_scaled = rows_in_new / jnp.mean(rows_in_new, axis=1, keepdims=True)
-    in_scale = jnp.einsum("mc,md->dc", col_hot, row_scaled, precision=PRECISE) * cols_in_new[None, :]
-    new_in = w_in - STEP_SIZE * part_in * lax.rsqrt(in_scale)
-    cols_out_new = DECAY_RATE * cols_out + (1 - DECAY_RATE) * col_sums / out_counts[:, None]
-    row_mean = jnp.dot(row_hot.T, total_sums / out_counts, precision=PRECISE)
-    col_pick = jnp.einsum("mr,md->rd", row_hot, cols_out_new, precision=PRECISE)
-    new_out = w_out - STEP_SIZE * part_out * lax.rsqrt((rows_out_new / row_mean)[:, None] * col_pick)
-    sq_gains_new = DECAY_RATE * sq_gains + (1 - DECAY_RATE) * g_gains * g_gains
-    new_gains = norm_gains - PLAIN_STEP * g_gains * lax.rsqrt(sq_gains_new)
-    sq_rel_new = DECAY_RATE * sq_rel + (1 - DECAY_RATE) * g_rel * g_rel
-    new_rel = rel_bias - PLAIN_STEP * g_rel * lax.rsqrt(sq_rel_new)
     return (
-        mixed[None], d_tokens_out, d_memory_out, part_in, part_out, g_gains, g_rel, new_in, new_out, new_gains,
-        new_rel, rows_in_new, cols_in_new, rows_out_new, cols_out_new, sq_gains_new, sq_rel_new,
+        mixed[None], d_tokens, d_memory, grad_in, grad_out, grad_gains, grad_rel, new_in, new_out, new_gains,
+        new_rel, rows_in_new, cols_in_new.reshape(-1), rows_out_new.reshape(-1), cols_out_new, sq_gains_new,
+        sq_rel_new,
     )
 
 

time: 499 us -> 462 us (0.926)
  blocking collectives: 48.3 us -> 0 us
  Pallas kernels: 401 us -> 432 us
  matrix products: 9.14 us -> 0 us
  other arithmetic: 11.4 us -> 2.46 us
    psum x1 -> x0, blocking collectives: 48.3 us -> none  [body(): lax.psum((row_terms, col_terms, row_totals, gain_grads, d_rel), ('dp', 'g...]
    pallas_call x2 -> x3, Pallas kernels: 194 us -> 225 us  [the longest x1 215 us: backward_call(): pl.pallas_call(functools.partial(backward_kernel, boxed), out_shape=tuple...]
    gather x6 -> x0, local copies, waits for them, and re-layouts: 11.8 us -> none  [the longest x2 5.21 us: body(): merge = lambda v: v.reshape(n_index, SEQ // n_index, WIDTH)[inverse]]
    unnamed x52 -> x28, local copies, waits for them, and re-layouts: 1.78 us -> 11.5 us
    dot_general x8 -> x0, matrix products: 9.14 us -> none  [the longest x1 2.68 us: body(): jnp.einsum('mc,md->dc', col_hot, row_scaled, precision=PRECISE)]
where the time goes in v2:
time: 462 us; the launch traced here: 454 us
  Pallas kernels  432 us (94%)
  local copies, waits for them, and re-layouts  15.9 us (3%)
    pallas_call x1, Pallas kernels, backward_call(): pl.pallas_call(functools.partial(backward_kernel, boxed), out_shape=tuple...  215 us
    pallas_call x1, Pallas kernels, gather_all(): pl.pallas_call(gather_kernel, out_shape=(sds((32 * win_sh.shape[0], WIDTH...  140 us
    pallas_call x1, Pallas kernels, forward_call(): vmem_call(kernel, (sds((SEQ, 3 * HEAD_COLS)), sds((SEQ, HEAD_COLS)), sds(...  42.4 us
    pallas_call x1, Pallas kernels, ff_call(): vmem_call(ff_kernel, (sds((SEQ, WIDTH)), sds((SEQ, WIDTH), f32), sds((1,...  25 us
    unnamed x28, local copies, waits for them, and re-layouts  11.5 us

profile of v2, /device:TPU:0, one launch (start us, length us, event | category | flops | bytes accessed | tf_op | source)
XLA Modules:
  0.0 453.8 jit_solution(10411586160093611927)
XLA Ops:
  0.7 0.6 pad_add_fusion.ids
  1.2 2.5 copy.51.w_in
  3.8 1.4 copy.52.rel_bias
  5.2 5.0 %shard_map.323 = (bf16[16,32,768]{2,1,0:T(8,128)(2,1)}, bf16[16,32,768]{2,1,0:T(8,128)(2,1)}, bf16[16,32,128]{2,1,0:T(8,128)(2,1)}, bf16[272,768]{1,0:T(8,128)(2...) custom-call(s32[3]{0:T(128)} %pad_add_fusion.ids, s32[32]{0:T(128)} %row_source.3, s32[32]{0:T(128)} %modes.1, ...), custom_call_target="tpu_custom_call" | custom-call | tf_op jit(solution)/shard_map/pallas_call | solution.py:927
  10.2 139.6 %shard_map.324 = (bf16[8704,768]{1,0:T(8,128)(2,1)}, bf16[3584,768]{1,0:T(8,128)(2,1)}, bf16[16,32,768]{2,1,0:T(8,128)(2,1)}, bf16[16,32,768]{2,1,0:T(8,128)(2,1)}, bf16[16,32,128]{2,1,0:T(8,128)(2,1)}) custom-call(bf16[272,768]{1,0:T(8,128)(2,1)} %get-tuple-element.65.win_sh, bf16[112,768]{1,0:T(8,128)(2,1)} %get-tuple-element.66.wout_sh, ...), custom_call_target="tpu_custom_call" | custom-call | tf_op jit(solution)/shard_map/pallas_call | solution.py:834
  149.8 1.4 fusion
  151.2 42.4 %shard_map.325 = (bf16[512,2304]{1,0:T(8,128)(2,1)}, bf16[512,768]{1,0:T(8,128)(2,1)}, f32[512,128]{1,0:T(8,128)}, f32[512,768]{1,0:T(8,128)}, bf16[512,768]{1,0...) custom-call(bf16[512,768]{1,0:T(8,128)(2,1)} %bitcast.10, ...), custom_call_target="tpu_custom_call" | custom-call | tf_op jit(solution)/shard_map/pallas_call | solution.py:1025
  193.6 0.0 copy-start.5
  193.6 0.0 copy-start.8
  193.6 0.0 copy-start.9
  193.6 25.0 %shard_map.326 = (bf16[512,768]{1,0:T(8,128)(2,1)}, f32[512,768]{1,0:T(8,128)}, f32[1,768]{1,0:T(1,128)}, bf16[8704,768]{1,0:T(8,128)(2,1)}, bf16[3584,768]{1,0:T(8,128)(2,1)}) custom-call(f32[512,768]{1,0:T(8,128)} %get-tuple-element.76.x2, bf16[512,768]{1,0:T(8,128)(2,1)} %bitcast.14, f32[512,128]{1,0:T(8,128)} %get-tuple-element.77.keep, f32[3,768]{1,0:T(4,128)} %gains.3, ...), custom_call_target="tpu_custom_call" | custom-call | tf_op jit(solution)/shard_map/pallas_call | solution.py:1044
  218.6 0.0 copy-done.5
  218.6 0.6 dynamic_slice.6
  221.1 0.0 copy-done.8
  221.1 0.6 dynamic_slice.7
  221.7 0.6 compare_convert_fusion
  222.4 0.7 broadcast_in_dim.10.refs_12_
  223.1 0.0 copy-done.9
  223.1 0.7 copy.53.refs_14_.rows_out
  223.8 0.0 copy-start.6
  223.8 0.0 copy-start.4
  223.8 215.3 %shard_map.327 = (bf16[8704,768]{1,0:T(8,128)(2,1)}, bf16[3584,768]{1,0:T(8,128)(2,1)}, f32[272,768]{1,0:T(8,128)}, f32[112,768]{1,0:T(8,128)}, f32[8,768]{1,0:T...) custom-call(bf16[8704,768]{1,0:T(8,128)(2,1)} %get-tuple-element.79., ...), custom_call_target="tpu_custom_call", output_to_operand_aliasing={{0}: (0, {}), {1}: (1, {})} | custom-call | tf_op jit(solution)/shard_map/pallas_call | solution.py:1220
  439.1 0.0 copy-done.6
  439.1 0.6 reshape.68.cols_in
  439.7 0.0 copy-done.4
  439.7 0.7 copy.57.sq_rel
  440.4 5.0 %shard_map.328 = (bf16[16,32,768]{2,1,0:T(8,128)(2,1)}, bf16[16,32,768]{2,1,0:T(8,128)(2,1)}, f32[768,272]{1,0:T(8,128)}, f32[112,768]{1,0:T(8,128)}, f32[3,768]...) custom-call(s32[3]{0:T(128)} %pad_add_fusion.ids, ...), custom_call_target="tpu_custom_call" | custom-call | tf_op jit(solution)/shard_map/pallas_call | solution.py:1003
  445.4 0.0 copy-start
  445.4 0.0 copy-start.3
  445.4 0.0 copy-start.7
  445.4 0.0 copy-start.1
  445.4 0.0 copy-start.2
  445.4 2.6 copy.58
  448.0 1.5 copy.59
  449.5 0.0 copy-done
  449.5 1.2 copy.60
  450.7 0.0 copy-done.3
  450.7 0.7 copy.61
  451.4 0.0 copy-done.7
  451.4 0.6 reduce
  452.0 0.0 copy-done.1
  452.0 0.6 reduce.1
  452.7 0.0 copy-done.2
  452.7 0.7 copy.62
Async XLA Ops:
  193.6 25.0 %copy-start.5 = (s32[32]{0:T(128)S(1)}, s32[32]{0:T(128)}, u32[]{:S(2)}) copy-start(s32[32]{0:T(128)} %row_source.3) | copy-start | bytes 388
  193.6 27.5 %copy-start.8 = (s32[32]{0:T(128)S(1)}, s32[32]{0:T(128)}, u32[]{:S(2)}) copy-start(s32[32]{0:T(128)} %modes.1) | copy-start | bytes 388
  193.6 29.4 %copy-start.9 = (f32[112]{0:T(128)S(1)}, f32[112]{0:T(128)}, u32[]{:S(2)}) copy-start(f32[112]{0:T(128)} %param.34) | copy-start | bytes 1348
  223.8 215.3 %copy-start.6 = (f32[272]{0:T(512)S(1)}, f32[272]{0:T(512)}, u32[]{:S(2)}) copy-start(f32[272]{0:T(512)} %param.33) | copy-start | bytes 3268
  223.8 215.9 %copy-start.4 = (f32[3,32,12]{1,2,0:T(8,128)S(1)}, f32[3,32,12]{1,2,0:T(8,128)}, u32[]{:S(2)}) copy-start(f32[3,32,12]{1,2,0:T(8,128)} %param.37) | copy-start | bytes 13828
  445.4 4.1 copy-start
  445.4 5.4 %copy-start.3 = (f32[3,32,12]{2,1,0:T(8,128)S(1)}, f32[3,32,12]{2,1,0:T(8,128)}, u32[]{:S(2)}) copy-start(f32[3,32,12]{2,1,0:T(8,128)} %get-tuple-element.140) | copy-start | bytes 13828
  445.4 6.1 %copy-start.7 = (f32[1,272]{1,0:T(1,128)S(1)}, f32[1,272]{1,0:T(1,128)}, u32[]{:S(2)}) copy-start(f32[1,272]{1,0:T(1,128)} %get-tuple-element.108) | copy-start | bytes 3268
  445.4 6.6 %copy-start.1 = (f32[112,1]{1,0:T(8,128)S(1)}, f32[112,1]{1,0:T(8,128)}, u32[]{:S(2)}) copy-start(f32[112,1]{1,0:T(8,128)} %get-tuple-element.109) | copy-start | bytes 1348
  445.4 7.3 %copy-start.2 = (f32[3,32,12]{2,1,0:T(8,128)S(1)}, f32[3,32,12]{2,1,0:T(8,128)}, u32[]{:S(2)}) copy-start(f32[3,32,12]{2,1,0:T(8,128)} %get-tuple-element.146) | copy-start | bytes 13828

commit v3 on v2

--- a/solution.py
+++ b/solution.py
@@ -257,6 +257,7 @@
         if k == 0:
             got = got.astype(jnp.bfloat16).astype(jnp.float32) * HSIZE**-0.5
         qkv[:, cols] = got.astype(jnp.bfloat16)
+    step("projected", 0)
     lse1[...] = jnp.zeros_like(lse1)
     lse2[...] = jnp.zeros_like(lse2)
 
@@ -270,6 +271,7 @@
         step("self", p)
 
     x1[...] = tok[...].astype(jnp.float32) + nn(att1[...], wout[0:HEAD_COLS, :])
+    step("middle", 0)
     a2 = (x1[...] * inv_rms(x1[...]) * gains[1:2, :]).astype(jnp.bfloat16)
     got = nt(a2, win[3 * HEAD_COLS : 4 * HEAD_COLS, :])
     qc[...] = (got.astype(jnp.bfloat16).astype(jnp.float32) * HSIZE**-0.5).astype(jnp.bfloat16)
@@ -277,6 +279,7 @@
         kvc[:, k * HEAD_COLS : (k + 1) * HEAD_COLS] = nt(
             mem[...], win[(4 + k) * HEAD_COLS : (5 + k) * HEAD_COLS, :]
         ).astype(jnp.bfloat16)
+    step("crossed", 0)
 
     @pl.loop(0, HEADS // 2)
     def _(p):
@@ -288,7 +291,9 @@
         )
         step("cross", p)
 
+    step("attended", 0)
     x2[...] = x1[...] + nn(att2[...], wout[HEAD_COLS : 2 * HEAD_COLS, :])
+    step("end", 0)
 
 
 def ff_kernel(
@@ -346,42 +351,57 @@
                 pltpu.make_async_copy(held.at[other, k], g_wout.at[0:rows], sem.at[other, k]).wait()
 
 
+LATE = 4
+
+
+BACK_BLOCKS = (("o", 1), ("i", 4), ("i", 5), ("i", 3), ("o", 0), ("i", 0), ("i", 1), ("i", 2))
+
+
 def attention_backward(
-    tok, mem, aux, win, wout, gains, table, qkv, att1, lse1, x1, qc, kvc, att2, lse2, g2,
-    d_mem, d_tok, d_gains, dist, do, dqkv, dq_acc, rel_acc, emit, step,
+    tok, mem, aux, gains, table, qkv, att1, lse1, x1, qc, kvc, att2, lse2, g2,
+    d_mem, d_tok, d_gains, dist, do, dqkv, dq_acc, rel_acc, weight, need, emit, step,
 ):
+    need(1)
     e2 = g2[...].astype(jnp.bfloat16)
-    do[...] = nt(e2, wout[HEAD_COLS : 2 * HEAD_COLS, :]).astype(jnp.bfloat16)
-    emit(7, tn(att2[...], e2))
-
-    @pl.loop(0, HEADS // 2)
-    def _(p):
-        _, against = ext_masks(aux[...], 0)
-        hot = pltpu.roll(ext_masks(aux[...], SEGS)[0], 128 - SEGS, 1)
-        dq, dk, dv = back_pair(
-            p, qc[:, tile_cols(p)], kvc[:, tile_cols(p)], kvc[:, tile_cols(p, HEAD_COLS)], do[:, tile_cols(p)],
-            att2[:, tile_cols(p)], lse2[...], hot, against, None, dq_acc, rel_acc, dist,
-        )
-        dqkv[:, tile_cols(p)] = dq.astype(jnp.bfloat16)
-        dqkv[:, tile_cols(p, HEAD_COLS)] = dk.astype(jnp.bfloat16)
-        dqkv[:, tile_cols(p, 2 * HEAD_COLS)] = dv.astype(jnp.bfloat16)
-        step("cross", p)
-
+    do[...] = weight(0, lambda w: nt(e2, w)).astype(jnp.bfloat16)
+    need(8)
+
+    def cross_pairs(first, last):
+        @pl.loop(first, last)
+        def _(p):
+            _, against = ext_masks(aux[...], 0)
+            hot = pltpu.roll(ext_masks(aux[...], SEGS)[0], 128 - SEGS, 1)
+            dq, dk, dv = back_pair(
+                p, qc[:, tile_cols(p)], kvc[:, tile_cols(p)], kvc[:, tile_cols(p, HEAD_COLS)], do[:, tile_cols(p)],
+                att2[:, tile_cols(p)], lse2[...], hot, against, None, dq_acc, rel_acc, dist,
+            )
+            dqkv[:, tile_cols(p)] = dq.astype(jnp.bfloat16)
+            dqkv[:, tile_cols(p, HEAD_COLS)] = dk.astype(jnp.bfloat16)
+            dqkv[:, tile_cols(p, 2 * HEAD_COLS)] = dv.astype(jnp.bfloat16)
+            step("cross", p, first, last)
+
+    late = 2 * HEAD_COLS + LATE * 128
+    cross_pairs(LATE, HEADS // 2)
+    emit("i", 3 * HEAD_COLS + late, tn(dqkv[:, late:], mem[...]))
+    step("late", None, 0, 0)
+    cross_pairs(0, LATE)
+    need(12)
     a2 = (x1[...] * inv_rms(x1[...]) * gains[1:2, :]).astype(jnp.bfloat16)
-    for k in range(3):
-        cols = slice(k * HEAD_COLS, (k + 1) * HEAD_COLS)
-        emit(3 + k, tn(dqkv[:, cols], a2 if k == 0 else mem[...]))
-    d_mem[...] = nn(
-        dqkv[:, HEAD_COLS : 3 * HEAD_COLS], win[4 * HEAD_COLS : 6 * HEAD_COLS, :]
-    ).astype(jnp.bfloat16)
-    da2 = nn(dqkv[:, 0:HEAD_COLS], win[3 * HEAD_COLS : 4 * HEAD_COLS, :])
+    emit("o", HEAD_COLS, tn(att2[...], e2))
+    emit("i", 3 * HEAD_COLS, tn(dqkv[:, 0:HEAD_COLS], a2))
+    emit("i", 4 * HEAD_COLS, tn(dqkv[:, HEAD_COLS : 2 * HEAD_COLS], mem[...]))
+    emit("i", 5 * HEAD_COLS, tn(dqkv[:, 2 * HEAD_COLS : late], mem[...]))
+    d_rows = weight(1, lambda w: nn(dqkv[:, HEAD_COLS : 2 * HEAD_COLS], w))
+    d_rows += weight(2, lambda w: nn(dqkv[:, 2 * HEAD_COLS : 3 * HEAD_COLS], w))
+    d_mem[...] = d_rows.astype(jnp.bfloat16)
+    da2 = weight(3, lambda w: nn(dqkv[:, 0:HEAD_COLS], w))
     part, gain = rms_back(x1[...], gains[1:2, :], da2)
     d_gains[1:2, :] = gain
     g2[...] += part
     e1 = g2[...].astype(jnp.bfloat16)
-    do[...] = nt(e1, wout[0:HEAD_COLS, :]).astype(jnp.bfloat16)
-    emit(6, tn(att1[...], e1))
-    step("middle", 0)
+    do[...] = weight(4, lambda w: nt(e1, w)).astype(jnp.bfloat16)
+    emit("o", 0, tn(att1[...], e1))
+    step("middle", None, 0, 0)
 
     @pl.loop(0, HEADS // 2)
     def _(p):
@@ -393,14 +413,16 @@
         dqkv[:, tile_cols(p)] = dq.astype(jnp.bfloat16)
         dqkv[:, tile_cols(p, HEAD_COLS)] = dk.astype(jnp.bfloat16)
         dqkv[:, tile_cols(p, 2 * HEAD_COLS)] = dv.astype(jnp.bfloat16)
-        step("self", p)
+        step("self", p, 0, HEADS // 2)
 
     x0 = tok[...].astype(jnp.float32)
     a1 = (x0 * inv_rms(x0) * gains[0:1, :]).astype(jnp.bfloat16)
     for k in range(3):
-        cols = slice(k * HEAD_COLS, (k + 1) * HEAD_COLS)
-        emit(k, tn(dqkv[:, cols], a1))
-    da1 = nn(dqkv[...], win[0 : 3 * HEAD_COLS, :])
+        emit("i", k * HEAD_COLS, tn(dqkv[:, k * HEAD_COLS : (k + 1) * HEAD_COLS], a1))
+    step("last", None, 0, 0)
+    da1 = weight(5, lambda w: nn(dqkv[:, 0:HEAD_COLS], w))
+    for k in (1, 2):
+        da1 += weight(5 + k, lambda w: nn(dqkv[:, k * HEAD_COLS : (k + 1) * HEAD_COLS], w))
     part, gain = rms_back(x0, gains[0:1, :], da1)
     d_gains[0:1, :] = gain
     d_tok[...] = (g2[...] + part).astype(jnp.bfloat16)
@@ -411,9 +433,6 @@
     ("i", 0, 64, 32), ("i", 64, 64, 32), ("i", 128, 64, 32), ("i", 192, 80, 48),
     ("o", 0, 64, 32), ("o", 64, 48, 16),
 )
-
-
-REGION = 400
 
 
 def place():
@@ -492,118 +511,111 @@
     return [((lax.rem(me + k, 16), g), None) for k in range(1, 16)] + [(dev(z, y, x, 1 - g), None)]
 
 
-def gather_steps(links, arrays, low, lag1=2, lag2=4):
-    z, y, x, g = place()
-    items = []
-    nearest = jnp.clip(z, low, low + 1)
-    bases = [(links.reserve(2), links.reserve(2)) for _ in PIECES]
-    for zz in (nearest, 2 * low + 1 - nearest):
-        for (kind, lo, n, half), (b_up, b_down) in zip(PIECES, bases):
-
-            def here(yy, xx, first, count, zz=zz, kind=kind):
-                return rows_of(arrays[kind], kind, zz, yy, xx, g, first, count)
-
-            c = {"zz": zz, "go_up": (z >= zz) & (z < 3), "go_down": (z <= zz) & (z > 0)}
-            c["from_below"], c["from_above"] = z > zz, z < zz
-
-            def add(name, ref, device, sem=None, c=c):
-                c[name] = links.copy(ref, ref, device, sem)
-
-            own = here(y, x, lo, n)
-            add("up", own, dev(jnp.minimum(z + 1, 3), y, x, g), b_up + zz - low)
-            add("down", own, dev(jnp.maximum(z - 1, 0), y, x, g), b_down + zz - low)
-            add("x", own, dev(z, y, 1 - x, g))
-            add("y", own, dev(z, 1 - y, x, g))
-            add("p", own, dev(z, y, x, 1 - g))
-            add("a", here(y, 1 - x, lo, half), dev(z, 1 - y, x, g))
-            add("b", here(1 - y, x, lo + half, n - half), dev(z, y, 1 - x, g))
-            add("px", here(y, 1 - x, lo, n), dev(z, y, x, 1 - g))
-            add("py", here(1 - y, x, lo, n), dev(z, y, x, 1 - g))
-            add("pa", here(1 - y, 1 - x, lo, half), dev(z, y, x, 1 - g))
-            add("pb", here(1 - y, 1 - x, lo + half, n - half), dev(z, y, x, 1 - g))
-            items.append(c)
-
-    def first(c):
+class Gather:
+    def __init__(self, links, arrays):
+        z, y, x, g = place()
+        self.links, self.items = links, []
+        for low in (0, 2):
+            nearest = jnp.clip(z, 0, 1) if low == 0 else low
+            bases = [(links.reserve(2), links.reserve(2)) for _ in PIECES]
+            for zz in (nearest, 2 * low + 1 - nearest):
+                for (kind, lo, n, half), (b_up, b_down) in zip(PIECES, bases):
+
+                    def here(yy, xx, first, count, zz=zz, kind=kind):
+                        return rows_of(arrays[kind], kind, zz, yy, xx, g, first, count)
+
+                    c = {"go_up": (z >= zz) & (z < 3), "go_down": (z <= zz) & (z > 0)}
+                    c["from_below"], c["from_above"] = z > zz, z < zz
+                    c["hops"] = jnp.abs(z - zz)
+
+                    def add(name, ref, device, sem=None, c=c):
+                        c[name] = links.copy(ref, ref, device, sem)
+
+                    own = here(y, x, lo, n)
+                    add("up", own, dev(jnp.minimum(z + 1, 3), y, x, g), b_up + zz - low)
+                    add("down", own, dev(jnp.maximum(z - 1, 0), y, x, g), b_down + zz - low)
+                    add("x", own, dev(z, y, 1 - x, g))
+                    add("y", own, dev(z, 1 - y, x, g))
+                    add("p", own, dev(z, y, x, 1 - g))
+                    add("a", here(y, 1 - x, lo, half), dev(z, 1 - y, x, g))
+                    add("b", here(1 - y, x, lo + half, n - half), dev(z, y, 1 - x, g))
+                    add("px", here(y, 1 - x, lo, n), dev(z, y, x, 1 - g))
+                    add("py", here(1 - y, x, lo, n), dev(z, y, x, 1 - g))
+                    add("pa", here(1 - y, 1 - x, lo, half), dev(z, y, x, 1 - g))
+                    add("pb", here(1 - y, 1 - x, lo + half, n - half), dev(z, y, x, 1 - g))
+                    self.items.append(c)
+
+    def along(self, c):
         pl.when(c["from_below"])(c["up"].wait_recv)
         pl.when(c["from_above"])(c["down"].wait_recv)
-        links.start(c["up"], c["go_up"])
-        links.start(c["down"], c["go_down"])
+        self.links.start(c["up"], c["go_up"])
+        self.links.start(c["down"], c["go_down"])
+
+    def near(self, c):
         for k in ("x", "y", "p"):
-            links.start(c[k])
-
-    def second(c):
+            self.links.start(c[k])
+
+    def second(self, c):
         c["x"].wait_recv()
-        links.start(c["a"])
-        links.start(c["px"])
+        self.links.start(c["a"])
+        self.links.start(c["px"])
         c["y"].wait_recv()
-        links.start(c["b"])
-        links.start(c["py"])
-
-    def third(c):
+        self.links.start(c["b"])
+        self.links.start(c["py"])
+
+    def third(self, c):
         c["a"].wait_recv()
-        links.start(c["pa"])
+        self.links.start(c["pa"])
         c["b"].wait_recv()
-        links.start(c["pb"])
-
-    n = len(items)
-    steps = []
-    for t in range(n + lag2):
-
-        def step(t=t):
-            if t < n:
-                first(items[t])
-            if 0 <= t - lag1 < n:
-                second(items[t - lag1])
-            if 0 <= t - lag2 < n:
-                third(items[t - lag2])
-
-        steps.append(step)
-
-    def end():
-        for c in items:
+        self.links.start(c["pb"])
+
+    def arrived(self, first, last):
+        for c in self.items[first:last]:
             for k in ("p", "px", "py", "pa", "pb"):
                 c[k].wait_recv()
 
-    return steps, end
-
-
-def gather_kernel(win_sh, wout_sh, tok_s, mem_s, aux_s, win, wout, tok, mem, aux, ss, rs, ls):
-    z, y, x, g = place()
-    me = lax.axis_index("dp")
-    links = Links(ss, rs)
-    near = [
-        pltpu.make_async_copy(win_sh, rows_of(win, "i", z, y, x, g, 0, 272), ls.at[0]),
-        pltpu.make_async_copy(wout_sh, rows_of(wout, "o", z, y, x, g, 0, 112), ls.at[1]),
-    ]
-    moves = ((tok_s, tok), (aux_s, aux), (mem_s, mem))
-    own = [pltpu.make_async_copy(s.at[me], t.at[me], ls.at[2 + k]) for k, (s, t) in enumerate(moves)]
-    for c in near + own:
-        c.start()
-    greet(all_peers())
-    for c in near:
-        c.wait()
-    queue = []
-    for s, t in moves:
+    def slots(self):
+        n = len(self.items)
+        half = n // 2
+        lead = half // 2
+        out = [[] for _ in range(n + 6)]
+        for t, c in enumerate(self.items):
+            if t < half:
+                out[t].append(functools.partial(self.along, c))
+            else:
+                for h in range(4):
+
+                    def hop(c=c, h=h):
+                        @pl.when(c["hops"] == h)
+                        def _():
+                            pl.when(c["from_below"])(c["up"].wait_recv)
+                            pl.when(c["from_above"])(c["down"].wait_recv)
+                            pl.when(c["go_up"])(c["up"].start)
+                            pl.when(c["go_down"])(c["down"].start)
+
+                    out[t - lead + h].append(hop)
+                self.links.sent += [(c["up"], c["go_up"]), (c["down"], c["go_down"])]
+        for t, c in enumerate(self.items):
+            out[t].append(functools.partial(self.near, c))
+            out[t + 3].append(functools.partial(self.second, c))
+            out[t + 6].append(functools.partial(self.third, c))
+        return out
+
+
+def row_exchange(links, sources, targets, rows):
+    me, g = lax.axis_index("dp"), lax.axis_index("group")
+    copies = []
+    for src, dst in zip(sources, targets):
         for k in range(1, 16):
             to = lax.rem(me + k, 16)
-            queue.append(links.copy(s.at[to], t.at[me], (to, g)))
-    steps, ends = [], []
-    for low in (0, 2):
-        more, end = gather_steps(links, {"i": win, "o": wout}, low)
-        steps += more
-        ends.append(end)
-    per = -(-len(queue) // len(steps))
-    for k, step in enumerate(steps):
-        step()
-        for c in queue[k * per : (k + 1) * per]:
-            links.start(c)
-    for c in queue:
-        c.wait_recv()
-    for end in ends:
-        end()
-    for c in own:
-        c.wait()
-    links.drain()
+            there = dst.at[pl.ds(pl.multiple_of(me * rows, 16), rows)]
+            copies.append(links.copy(src.at[pl.ds(pl.multiple_of(to * rows, 16), rows)], there, (to, g)))
+    return copies
+
+
+def own_rows(src, dst, rows, sem):
+    here = pl.ds(pl.multiple_of(lax.axis_index("dp") * rows, 16), rows)
+    return pltpu.make_async_copy(src.at[here], dst.at[here], sem)
 
 
 class Sums:
@@ -611,16 +623,16 @@
         self.arrays = {"i": win_g, "o": wout_g}
         self.own, self.got, self.plane, self.fin, self.line = own, got, plane, fin, line
         self.part_in, self.part_out, self.load_sem = part_in, part_out, load_sem
-        self.loads, self.line_rows = 0, 0
-
-    def batch(self, links, region, members):
+        self.loads, self.rows, self.line_rows = 0, 0, 0
+
+    def batch(self, links, members):
         z, y, x, g = place()
-        base = region * REGION
         items = []
         for zz, k in members:
             kind, lo, n, half = PIECES[k]
+            base = self.rows
             at = lambda ref, c, off, m, base=base: ref.at[c, pl.ds(base + off, m)]
-            it = {"zz": zz, "n": n, "half": half, "base": base, "kind": kind, "lo": lo, "line": self.line_rows}
+            it = {"zz": zz, "n": n, "half": half, "base": base, "kind": kind, "lo": lo}
             it["links"] = links
             it["below"], it["above"], it["z"] = z < zz, z > zz, z
             it["load"], it["pair"] = [], []
@@ -643,43 +655,44 @@
             it["y1"] = [links.copy(at(own, c, half, rest), at(plane, s, half, rest), ny) for s, c in ((0, 2), (1, 3))]
             it["y2"] = links.copy(at(own, 2, 0, half), at(fin, 0, 0, half), ny)
             it["x2"] = links.copy(at(own, 1, half, rest), at(fin, 0, half, rest), nx)
-            there = lambda s: self.line.at[s, pl.ds(it["line"], n)]
-            it["up"] = links.copy(at(own, 0, 0, n), there(0), dev(jnp.minimum(z + 1, 3), y, x, g))
-            it["down"] = links.copy(at(own, 0, 0, n), there(1), dev(jnp.maximum(z - 1, 0), y, x, g))
+            for way, needed in (("from_below", zz > 0), ("from_above", zz < 3)):
+                if needed:
+                    it[way] = pl.ds(self.line_rows, n)
+                    self.line_rows += n
+            if zz > 0:
+                it["up"] = links.copy(at(own, 0, 0, n), self.line.at[it["from_below"]], dev(jnp.minimum(z + 1, 3), y, x, g))
+            if zz < 3:
+                it["down"] = links.copy(at(own, 0, 0, n), self.line.at[it["from_above"]], dev(jnp.maximum(z - 1, 0), y, x, g))
             items.append(it)
-            base += n
-            self.line_rows += n
-        assert base <= (region + 1) * REGION
-        n = len(items)
-        lag2, lag3 = 2, 4
-        steps = []
-
-        def begin():
-            for it in items:
-                for c in it["load"]:
-                    c.start()
-                for c in (3, 1, 2, 0):
-                    links.start(it["pair"][c])
-
-        steps.append(begin)
-        for t in range(n + lag3):
-
-            def step(t=t):
-                if t < n:
-                    self.to_core(items[t])
-                if 0 <= t - lag2 < n:
-                    self.to_plane(items[t - lag2])
-                if 0 <= t - lag3 < n:
-                    self.to_line(items[t - lag3])
-
-            steps.append(step)
-        return steps
+            self.rows += n
+        return items
+
+    def begin(self, items):
+        for it in items:
+            for c in it["load"]:
+                c.start()
+            for c in (3, 1, 2, 0):
+                it["links"].start(it["pair"][c])
+
+    def place_in(self, slots, first, items):
+        for k, it in enumerate(items):
+            t = first + k
+            slots[t].append((2, self.to_core, it))
+            slots[t + 3].append((1, self.to_plane, it))
+            slots[t + 6].append((0, self.to_line, it))
+            for h in range(1, max(it["zz"], 3 - it["zz"]) + 1):
+                slots[t + 6 + 2 * h].append((-h, functools.partial(self.hop, h), it))
 
     @staticmethod
     def add(dst, c, first, src, s, start, m):
         rows = pl.ds(first, m)
         more = src[s, pl.ds(start, m), :].astype(jnp.float32)
         dst[c, rows, :] = (dst[c, rows, :].astype(jnp.float32) + more).astype(jnp.bfloat16)
+
+    def add_line(self, it, way):
+        rows = pl.ds(it["base"], it["n"])
+        more = self.line[it[way], :].astype(jnp.float32)
+        self.own[0, rows, :] = (self.own[0, rows, :].astype(jnp.float32) + more).astype(jnp.bfloat16)
 
     def to_core(self, it):
         for c in (3, 1, 2, 0):
@@ -709,48 +722,53 @@
         self.add(self.own, 0, low, self.plane, 0, low, rest)
 
     def to_line(self, it):
-        z, below, above = it["z"], it["below"], it["above"]
-        zz, n, base, line = it["zz"], it["n"], it["base"], it["line"]
         it["y2"].wait_recv()
         it["x2"].wait_recv()
-        self.add(self.own, 0, base, self.fin, 0, base, n)
-        up, down = it["up"], it["down"]
+        self.add(self.own, 0, it["base"], self.fin, 0, it["base"], it["n"])
+        z, zz = it["z"], it["zz"]
         if zz > 0:
-
-            @pl.when(below)
+            pl.when(z == 0)(it["up"].start)
+            it["links"].sent.append((it["up"], it["below"]))
+        if zz < 3:
+            pl.when(z == 3)(it["down"].start)
+            it["links"].sent.append((it["down"], it["above"]))
+
+    def hop(self, h, it):
+        z, zz, n, base = it["z"], it["zz"], it["n"], it["base"]
+        if h < zz:
+
+            @pl.when(z == h)
             def _():
-                @pl.when(z > 0)
-                def _():
-                    up.wait_recv()
-                    self.add(self.own, 0, base, self.line, 0, line, n)
-
-                up.start()
-
-            it["links"].sent.append((up, below))
-        if zz < 3:
-
-            @pl.when(above)
+                it["up"].wait_recv()
+                self.add_line(it, "from_below")
+                it["up"].start()
+
+        if h < 3 - zz:
+
+            @pl.when(z == 3 - h)
             def _():
-                @pl.when(z < 3)
-                def _():
-                    down.wait_recv()
-                    self.add(self.own, 0, base, self.line, 1, line, n)
-
-                down.start()
-
-            it["links"].sent.append((down, above))
-
-        @pl.when(z == zz)
-        def _():
-            total = self.own[0, pl.ds(base, n), :].astype(jnp.float32)
-            if zz > 0:
-                up.wait_recv()
-                total += self.line[0, pl.ds(line, n), :].astype(jnp.float32)
-            if zz < 3:
-                down.wait_recv()
-                total += self.line[1, pl.ds(line, n), :].astype(jnp.float32)
-            into = self.part_in if it["kind"] == "i" else self.part_out
-            into[it["lo"] : it["lo"] + n, :] = total
+                it["down"].wait_recv()
+                self.add_line(it, "from_above")
+                it["down"].start()
+
+        if h == max(zz, 3 - zz):
+
+            @pl.when(z == zz)
+            def _():
+                total = self.own[0, pl.ds(base, n), :].astype(jnp.float32)
+                if zz > 0:
+                    it["up"].wait_recv()
+                    total += self.line[it["from_below"], :].astype(jnp.float32)
+                if zz < 3:
+                    it["down"].wait_recv()
+                    total += self.line[it["from_above"], :].astype(jnp.float32)
+                into = self.part_in if it["kind"] == "i" else self.part_out
+                into[it["lo"] : it["lo"] + n, :] = total
+
+
+def run_slot(slot):
+    for _, step, it in sorted(slot, key=lambda entry: entry[0]):
+        step(it)
 
 
 def total_steps(links, ref, room):
@@ -804,20 +822,13 @@
     return jax.ShapeDtypeStruct(shape, dtype)
 
 
-WEIGHTS = [
-    pltpu.VMEM((6 * HEAD_COLS, WIDTH), jnp.bfloat16), pltpu.VMEM((2 * HEAD_COLS, WIDTH), jnp.bfloat16),
-    pltpu.SemaphoreType.DMA((2,)),
-]
-
-
-def load_weights(win, wout, win_v, wout_v, sem):
-    copies = [
-        pltpu.make_async_copy(win.at[0 : 6 * HEAD_COLS], win_v, sem.at[0]),
-        pltpu.make_async_copy(wout.at[0 : 2 * HEAD_COLS], wout_v, sem.at[1]),
-    ]
-    for c in copies:
-        c.start()
-    return copies
+WEIGHTS = [pltpu.VMEM((6 * HEAD_COLS, WIDTH), jnp.bfloat16), pltpu.VMEM((2 * HEAD_COLS, WIDTH), jnp.bfloat16)]
+
+
+def load_rows(src, dst, first, last, sem):
+    copy = pltpu.make_async_copy(src.at[first:last], dst.at[first:last], sem)
+    copy.start()
+    return copy
 
 
 def anywhere():
@@ -826,35 +837,6 @@
 
 def whole():
     return pl.BlockSpec(memory_space=pltpu.VMEM)
-
-
-def gather_all(win_sh, wout_sh, tok_s, mem_s, aux_s):
-    any_ = pl.BlockSpec(memory_space=pl.ANY)
-    sems = 45 + 2 * 22 * len(PIECES)
-    return pl.pallas_call(
-        gather_kernel,
-        out_shape=(
-            sds((32 * win_sh.shape[0], WIDTH)), sds((32 * wout_sh.shape[0], WIDTH)),
-            sds(tok_s.shape), sds(mem_s.shape), sds(aux_s.shape),
-        ),
-        in_specs=[whole(), whole(), any_, any_, any_],
-        out_specs=(any_,) * 5,
-        scratch_shapes=[
-            pltpu.SemaphoreType.DMA((sems,)), pltpu.SemaphoreType.DMA((sems,)), pltpu.SemaphoreType.DMA((5,)),
-        ],
-        compiler_params=pltpu.CompilerParams(
-            collective_id=1, has_side_effects=True, vmem_limit_bytes=VMEM_BYTES
-        ),
-    )(win_sh, wout_sh, tok_s, mem_s, aux_s)
-
-
-def spread_steps(calls, steps):
-    out, done = [], 0
-    for k in range(calls):
-        upto = -(-len(steps) * (k + 1) // calls)
-        out.append(steps[done:upto])
-        done = upto
-    return out
 
 
 def run(steps):
@@ -887,12 +869,11 @@
 
 def prep_kernel(
     ids, row_source, modes, tokens, memory, segments, msegments, w_in, w_out, rel_bias, hot, sentinel,
-    tok_s, mem_s, aux_s, win_sh, wout_sh, tables, keep, flip, seg_t, mseg_t,
+    tok_s, mem_s, aux_s, win_sh, wout_sh, table_f, table_b, keep, mode_rows, seg_t, mseg_t,
 ):
     half_rows, length = tokens.shape[0], tokens.shape[1]
     groups, group, where = ids[0], ids[1], ids[2]
-    flip[:, 0 : w_in.shape[1]] = w_in[...]
-    win_sh[...] = flip[...].T[0 : w_in.shape[1], :].astype(jnp.bfloat16)
+    win_sh[...] = w_in[...].astype(jnp.bfloat16)
     wout_sh[...] = w_out[...].astype(jnp.bfloat16)
     for source, out in ((segments, seg_t), (msegments, mseg_t)):
         out[0:half_rows, 0:length] = source[...].astype(jnp.float32)
@@ -911,10 +892,11 @@
         aux_s[i] = jnp.where(same, 1.0, 0.0).astype(jnp.bfloat16)
 
     mode = modes[row_source[where]]
-    tables[...] = jnp.zeros_like(tables)
-    tables[0:HEADS, :] = lax.dot_general(
-        rel_bias[mode], hot[...], (((0,), (0,)), ((), ())), precision=PRECISE, preferred_element_type=jnp.float32
-    )
+    tables = jnp.dot(rel_bias[mode], hot[...], precision=PRECISE, preferred_element_type=jnp.float32)
+    for k, table in enumerate((table_f, table_b)):
+        table[...] = jnp.zeros_like(table)
+        table[0:HEADS, :] = tables[:, k * 256 : (k + 1) * 256]
+    mode_rows[...] = jnp.where(lax.broadcasted_iota(jnp.int32, (8, 128), 0) == mode, 1.0, 0.0)
     kept = (1 - sentinel[...]).astype(jnp.float32)
     keep[...] = jnp.broadcast_to(kept, (128, SEQ)).T
 
@@ -923,14 +905,13 @@
     f32 = jnp.float32
     scalars = pl.BlockSpec(memory_space=pltpu.SMEM)
     half_rows, length = tokens.shape[0], tokens.shape[1]
-    padded = -(-w_in.shape[1] // 128) * 128
     return vmem_call(
         prep_kernel,
         (
-            sds(tokens.shape), sds(memory.shape), sds((half_rows, length, 128)), sds((w_in.shape[1], WIDTH)),
-            sds(w_out.shape), sds((16, 512), f32), sds((SEQ, 128), f32),
+            sds(tokens.shape), sds(memory.shape), sds((half_rows, length, 128)), sds(w_in.shape),
+            sds(w_out.shape), sds((16, 256), f32), sds((16, 256), f32), sds((SEQ, 128), f32), sds((8, 128), f32),
         ),
-        [pltpu.VMEM((WIDTH, padded), f32), pltpu.VMEM((128, 128), f32), pltpu.VMEM((128, 128), f32)],
+        [pltpu.VMEM((128, 128), f32), pltpu.VMEM((128, 128), f32)],
         in_specs=[scalars] * 3 + [whole()] * 9,
     )(ids, row_source, modes, tokens, memory, segments, msegments, w_in, w_out, rel_bias, hot, sentinel)
 
@@ -939,7 +920,7 @@
     ids, row_source, part_in_t, part_out, sums, early, back_tok, back_mem, w_in, w_out, gains, rel_bias, rows_in,
     cols_in, rows_out, cols_out, sq_gains, sq_rel,
     d_tokens, d_memory, grad_in, grad_out, grad_gains, grad_rel, new_in, new_out, new_gains, new_rel, rows_in_new,
-    cols_in_new, rows_out_new, cols_out_new, sq_gains_new, sq_rel_new, flip,
+    cols_in_new, rows_out_new, cols_out_new, sq_gains_new, sq_rel_new,
 ):
     half_rows = back_tok.shape[0]
     groups, group, where = ids[0], ids[1], ids[2]
@@ -950,21 +931,18 @@
         d_tokens[source] = back_tok[i]
         d_memory[source] = back_mem[i]
 
-    n_in, n_out = w_in.shape[1], w_out.shape[0]
-    flip[0:n_in, :] = part_in_t[...]
-    part_in = flip[...].T[:, 0:n_in]
-    grad_in[...] = part_in
-    cols_new = DECAY_RATE * cols_in[...] + (1 - DECAY_RATE) * jnp.mean(part_in * part_in, axis=0, keepdims=True)
-    cols_in_new[...] = cols_new
-    rows_new, scaled = [], []
+    n_in, n_out = w_in.shape[0], w_out.shape[0]
+    p_in = part_in_t[...]
+    grad_in[...] = p_in
+    in_cols = DECAY_RATE * cols_in[...] + (1 - DECAY_RATE) * jnp.mean(p_in * p_in, axis=1, keepdims=True)
+    cols_in_new[...] = in_cols
+    block_in = block_of(where * n_in + lax.broadcasted_iota(jnp.int32, (n_in, 1), 0), IN_EDGES)
+    scale = jnp.zeros((n_in, WIDTH), jnp.float32)
     for k, count in enumerate((3 * HEAD_COLS, 3 * HEAD_COLS, 2 * FF)):
         row = DECAY_RATE * rows_in[k : k + 1, :] + (1 - DECAY_RATE) * (sums[k : k + 1, :] / count)
         rows_in_new[k : k + 1, :] = row
-        scaled.append(row / jnp.mean(row, axis=1, keepdims=True))
-    upright = jnp.concatenate(scaled + [jnp.zeros((128 - 3, WIDTH), jnp.float32)], axis=0).T
-    block_in = block_of(where * n_in + lax.broadcasted_iota(jnp.int32, (1, n_in), 1), IN_EDGES)
-    spread = jnp.where(block_in == 0, upright[:, 0:1], jnp.where(block_in == 1, upright[:, 1:2], upright[:, 2:3]))
-    new_in[...] = w_in[...] - STEP_SIZE * part_in * lax.rsqrt(spread * cols_new)
+        scale = jnp.where(block_in == k, in_cols * (row / jnp.mean(row, axis=1, keepdims=True)), scale)
+    new_in[...] = w_in[...] - STEP_SIZE * p_in * lax.rsqrt(scale)
 
     p_out = part_out[...]
     grad_out[...] = p_out
@@ -985,8 +963,7 @@
     sq_gains_new[...] = sq
     new_gains[...] = gains[...] - PLAIN_STEP * g * lax.rsqrt(sq)
     for k in range(MODES):
-        both = jnp.concatenate([early[8:24, k * 128 : (k + 1) * 128], jnp.zeros((112, 128), jnp.float32)], axis=0)
-        g = both.T[0:BUCKETS, 0:HEADS]
+        g = early[8 : 8 + HEADS, k * 128 : k * 128 + BUCKETS]
         grad_rel[k] = g
         sq = DECAY_RATE * sq_rel[k] + (1 - DECAY_RATE) * g * g
         sq_rel_new[k] = sq
@@ -997,41 +974,164 @@
     f32 = jnp.float32
     scalars = pl.BlockSpec(memory_space=pltpu.SMEM)
     (part_in_t, part_out, sums, early, back_tok, back_mem, w_in, w_out, gains, rel_bias) = arrays[:10]
-    n_in, n_out = w_in.shape[1], w_out.shape[0]
+    n_in, n_out = w_in.shape[0], w_out.shape[0]
     three = sds((3, WIDTH), f32)
     rel = sds(rel_bias.shape, f32)
     return vmem_call(
         update_kernel,
         (
             sds(back_tok.shape), sds(back_mem.shape), sds(w_in.shape, f32), sds(w_out.shape, f32), three, rel,
-            sds(w_in.shape, f32), sds(w_out.shape, f32), three, rel, three, sds((1, n_in), f32), sds((n_out, 1), f32),
+            sds(w_in.shape, f32), sds(w_out.shape, f32), three, rel, three, sds((n_in, 1), f32), sds((n_out, 1), f32),
             three, three, rel,
         ),
-        [pltpu.VMEM((-(-n_in // 128) * 128, WIDTH), f32)],
+        [],
         in_specs=[scalars] * 2 + [whole()] * len(arrays),
     )(ids, row_source, *arrays)
 
 
-def forward_call(tok, mem, aux, win, wout, gains, table):
-    f32 = jnp.float32
-
-    def kernel(tok, mem, aux, win, wout, *refs):
-        win_v, wout_v, sem = refs[-3:]
-        loads = load_weights(win, wout, win_v, wout_v, sem)
+def forward_kernel(boxed, *refs):
+    n_in = 5
+    ins, refs = refs[:n_in], refs[n_in:]
+    (gains, table), refs = refs[:2], refs[2:]
+    if boxed:
+        win_sh, wout_sh, tok_s, mem_s, aux_s = ins
+        (win, wout), rows_out, refs = refs[:2], refs[2:5], refs[5:]
+    else:
+        tok_s, mem_s, aux_s, win, wout = ins
+        rows_out = None
+    kept_out, kept, (tok, mem, aux), refs = refs[:9], refs[9:18], refs[18:21], refs[21:]
+    (win_v, wout_v, sem, put_sem, ls), refs = refs[:5], refs[5:]
+    puts = []
+
+    def keep(src, dst):
+        puts.append(pltpu.make_async_copy(src, dst, put_sem.at[len(puts)]))
+        puts[-1].start()
+
+    def hand_on(name):
+        names = {"projected": (0,), "middle": (1, 2, 3), "crossed": (4, 5), "attended": (6, 7), "end": (8,)}
+        for k in names.get(name, ()):
+            keep(kept[k], kept_out[k])
+        if boxed and name == "projected":
+            keep(tok, rows_out[0])
+            keep(aux, rows_out[2])
+        if boxed and name == "crossed":
+            keep(mem, rows_out[1])
+
+    if not boxed:
+        loads = [load_rows(win, win_v, 0, 6 * HEAD_COLS, sem.at[0]), load_rows(wout, wout_v, 0, 2 * HEAD_COLS, sem.at[1])]
+        for k, (s, t) in enumerate(((tok_s, tok), (mem_s, mem), (aux_s, aux))):
+            loads.append(pltpu.make_async_copy(s, t, ls.at[k]))
+            loads[-1].start()
         for c in loads:
             c.wait()
-        attention_forward(tok, mem, aux, win_v, wout_v, *refs[:-3], step=lambda name, p: None)
-
-    return vmem_call(
-        kernel,
-        (
-            sds((SEQ, 3 * HEAD_COLS)), sds((SEQ, HEAD_COLS)), sds((SEQ, 128), f32), sds((SEQ, WIDTH), f32),
-            sds((SEQ, HEAD_COLS)), sds((SEQ, 2 * HEAD_COLS)), sds((SEQ, HEAD_COLS)), sds((SEQ, 128), f32),
-            sds((SEQ, WIDTH), f32),
-        ),
-        WEIGHTS,
-        in_specs=[whole(), whole(), whole(), anywhere(), anywhere(), whole(), whole()],
-    )(tok, mem, aux, win, wout, gains, table)
+        attention_forward(
+            tok, mem, aux, win_v, wout_v, gains, table, *kept, step=lambda name, p: hand_on(name)
+        )
+        for c in puts:
+            c.wait()
+        return
+    ss, rs = refs
+    z, y, x, g = place()
+    pos = SEQ // 16
+    links = Links(ss, rs)
+    near = [
+        pltpu.make_async_copy(win_sh, rows_of(win, "i", z, y, x, g, 0, 272), ls.at[0]),
+        pltpu.make_async_copy(wout_sh, rows_of(wout, "o", z, y, x, g, 0, 112), ls.at[1]),
+    ]
+    own = [own_rows(s, t, pos, ls.at[2 + k]) for k, (s, t) in enumerate(((tok_s, tok), (mem_s, mem), (aux_s, aux)))]
+    for c in near + own:
+        c.start()
+    greet(all_peers())
+    for c in near:
+        c.wait()
+    gather = Gather(links, {"i": win, "o": wout})
+    slots = gather.slots()
+    first_rows = row_exchange(links, (tok_s, aux_s), (tok, aux), pos)
+    mem_rows = row_exchange(links, (mem_s,), (mem,), pos)
+    half = len(gather.items) // 2
+    now = half + 6
+    queue = [[] for _ in range(len(slots))]
+    for k, c in enumerate(first_rows):
+        queue[8 + k // 4].append(c)
+    for k, c in enumerate(mem_rows):
+        queue[16 + k // 3].append(c)
+
+    def run_gather(t):
+        run(slots[t])
+        for c in queue[t]:
+            links.start(c)
+
+    for t in range(now):
+        run_gather(t)
+    gather.arrived(0, half)
+    loads = [
+        load_rows(win, win_v, 0, 3 * HEAD_COLS, sem.at[0]), load_rows(wout, wout_v, 0, 2 * HEAD_COLS, sem.at[1]),
+        load_rows(win, win_v, 3 * HEAD_COLS, 16 * 272, sem.at[2]),
+    ]
+    for c in first_rows:
+        c.wait_recv()
+    for c in own:
+        c.wait()
+    loads[0].wait()
+    calls = HEADS // 2
+    shares = [range(now + k, now + k + 1) for k in range(calls)]
+    shares += [range(now + calls + k, now + calls + k + 1) for k in range(calls)]
+
+    def step(name, p):
+        hand_on(name)
+        if name == "middle":
+            gather.arrived(half, half + 4)
+            more = load_rows(win, win_v, 16 * 272, 6 * HEAD_COLS, sem.at[3])
+            for c in mem_rows:
+                c.wait_recv()
+            loads[2].wait()
+            more.wait()
+        if name not in ("self", "cross"):
+            return
+        for k in range(calls):
+
+            @pl.when(p == k)
+            def _(k=k):
+                for t in shares[k + (0 if name == "self" else calls)]:
+                    run_gather(t)
+                if name == "self" and k == calls - 1:
+                    loads[1].wait()
+
+    attention_forward(tok, mem, aux, win_v, wout_v, gains, table, *kept, step=step)
+    for t in range(now + 2 * calls, len(slots)):
+        run_gather(t)
+    gather.arrived(half + 4, 2 * half)
+    for c in puts:
+        c.wait()
+    links.drain()
+
+
+def forward_call(boxed, *arrays):
+    f32 = jnp.float32
+    dma = pltpu.SemaphoreType.DMA
+    outs = (
+        sds((SEQ, 3 * HEAD_COLS)), sds((SEQ, HEAD_COLS)), sds((SEQ, 128), f32), sds((SEQ, WIDTH), f32),
+        sds((SEQ, HEAD_COLS)), sds((SEQ, 2 * HEAD_COLS)), sds((SEQ, HEAD_COLS)), sds((SEQ, 128), f32),
+        sds((SEQ, WIDTH), f32),
+    )
+    rows = (sds((SEQ, WIDTH)), sds((SEQ, WIDTH)), sds((SEQ, 128)))
+    scratch = [pltpu.VMEM(v.shape, v.dtype) for v in outs + rows] + WEIGHTS + [dma((4,)), dma((12,)), dma((5,))]
+    specs = [anywhere()] * 5
+    extra = {}
+    if boxed:
+        sems = 45 + 4 * 22 * len(PIECES)
+        scratch = scratch + [dma((sems,)), dma((sems,))]
+        outs = (sds((6 * HEAD_COLS + 2 * FF, WIDTH)), sds((2 * HEAD_COLS + FF, WIDTH))) + rows + outs
+        specs = [whole()] * 2 + [anywhere()] * 3
+        extra = dict(collective_id=1, has_side_effects=True)
+    return pl.pallas_call(
+        functools.partial(forward_kernel, boxed),
+        out_shape=outs,
+        scratch_shapes=scratch,
+        in_specs=specs + [whole()] * 2,
+        out_specs=(anywhere(),) * len(outs),
+        compiler_params=pltpu.CompilerParams(vmem_limit_bytes=VMEM_BYTES, **extra),
+    )(*arrays)
 
 
 def ff_call(x2, cot, keep, gains, win, wout):
@@ -1065,17 +1165,46 @@
     return jnp.concatenate([by_bucket * mode_rows[k : k + 1, :] for k in range(MODES)], axis=1)
 
 
-def backward_kernel(boxed, _, __, tok, mem, aux, win, wout, *refs):
-    ins, (hot_dist, mode_rows, gain_three, rows_out) = refs[:11], refs[11:15]
-    refs = refs[15:]
+def backward_kernel(boxed, _, __, win, wout, *refs):
+    lazy, refs = refs[:12], refs[12:]
+    (gains, table, hot_dist, mode_rows, gain_three, rows_out), refs = refs[:6], refs[6:]
     if boxed:
         (g_win, g_wout, part_in, part_out, sums, early, btok, bmem), refs = refs[:8], refs[8:]
-        (d_mem, d_tok, d_gains, dist), refs = refs[:4], refs[4:]
+        (d_mem, d_tok), refs = refs[:2], refs[2:]
     else:
         (g_win, g_wout, d_mem, d_tok, early), refs = refs[:5], refs[5:]
-        (d_gains, dist), refs = refs[:2], refs[2:]
-    scratch, (held, put_sem, win_v, wout_v, sem), refs = refs[:4], refs[4:9], refs[9:]
-    loads = load_weights(win, wout, win_v, wout_v, sem)
+    (d_gains, dist), refs = refs[:2], refs[2:]
+    scratch, (held, put_sem, blocks, block_sem, lazy_sem, sem), refs = refs[:4], refs[4:10], refs[10:]
+    lazy_v, refs = refs[:12], refs[12:]
+    fetched = []
+
+    def fetch(k):
+        array, block = BACK_BLOCKS[k]
+        src = (win if array == "i" else wout).at[block * HEAD_COLS : (block + 1) * HEAD_COLS]
+        fetched.append(pltpu.make_async_copy(src, blocks.at[k % 3], block_sem.at[k]))
+        fetched[k].start()
+
+    def weight(k, fn):
+        fetched[k].wait()
+        value = fn(blocks[k % 3])
+        if k + 3 < len(BACK_BLOCKS):
+            fetch(k + 3)
+        return value
+
+    loads = [pltpu.make_async_copy(s, t, lazy_sem.at[k]) for k, (s, t) in enumerate(zip(lazy, lazy_v))]
+    loads[0].start()
+    fetch(0)
+    for c in loads[1:]:
+        c.start()
+    fetch(1)
+    fetch(2)
+    loaded = []
+
+    def need(n):
+        while len(loaded) < n:
+            loads[len(loaded)].wait()
+            loaded.append(True)
+
     puts, settled = [], []
 
     def settle(upto):
@@ -1083,20 +1212,17 @@
             puts[len(settled)].wait()
             settled.append(True)
 
-    def emit(block, value):
+    def emit(array, first, value):
         k = len(puts)
-        settle(k - 2)
-        held[k % 3] = value.astype(jnp.bfloat16)
-        into, first = (g_win, block) if block < 6 else (g_wout, block - 6)
-        puts.append(
-            pltpu.make_async_copy(
-                held.at[k % 3], into.at[pl.ds(first * HEAD_COLS, HEAD_COLS)], put_sem.at[k]
-            )
-        )
+        settle(k - 1)
+        rows = value.shape[0]
+        held[k % 2, 0:rows] = value.astype(jnp.bfloat16)
+        into = g_win if array == "i" else g_wout
+        puts.append(pltpu.make_async_copy(held.at[k % 2, 0:rows], into.at[first : first + rows], put_sem.at[k]))
         puts[k].start()
 
     dist[...] = jnp.zeros_like(dist)
-    step = lambda name, p: None
+    step = lambda *a: None
     if boxed:
         own, got, plane, fin, line, room, early_room, ss, rs, load_sem = refs
         z, y, x, g = place()
@@ -1107,78 +1233,61 @@
         n = len(PIECES)
         groups = (
             (0, [(3, k) for k in range(n)]),
-            (1, [(2, k) for k in range(n)]),
-            (0, [(1, k) for k in range(2, n)] + [(0, k) for k in range(4, n)]),
-            (1, [(0, k) for k in range(4)] + [(1, k) for k in range(2)]),
+            (6, [(2, k) for k in range(n)]),
+            (12, [(1, k) for k in range(2, n)] + [(0, k) for k in range(4, n)]),
+            (20, [(0, k) for k in range(4)] + [(1, k) for k in range(2)]),
         )
+        slots = [[] for _ in range(20 + n + 14)]
         links, batches = [Links(ss, rs)], []
-        for region, members in groups:
-            batches.append(work.batch(links[-1], region, members))
+        for first, members in groups:
+            batches.append(work.batch(links[-1], members))
+            work.place_in(slots, first, batches[-1])
             links.append(Links(ss, rs, links[-1].count))
         back = links[-1]
-
-        def row_copies(src, dst):
-            copies = []
-            for k in range(1, 16):
-                to = lax.rem(me + k, 16)
-                here = src.at[pl.ds(pl.multiple_of(to * pos, 16), pos)]
-                copies.append(back.copy(here, dst.at[me], (to, g)))
-            return copies
-
-        def keep_rows(src, dst, k):
-            return pltpu.make_async_copy(src.at[pl.ds(pl.multiple_of(me * pos, 16), pos)], dst.at[me], sem.at[2 + k])
-
-        mem_copies, tok_copies = row_copies(d_mem, bmem), row_copies(d_tok, btok)
-        kept_mem, kept_tok = keep_rows(d_mem, bmem, 0), keep_rows(d_tok, btok, 1)
-
-        def begin_third():
-            links[0].drain()
-            batches[2][0]()
-
-        first = spread_steps(6, batches[0][1:])
-        second = spread_steps(6, batches[1][1:] + [begin_third] + batches[2][1:6])
-        rest = batches[2][6:]
-        batches[0][0]()
-
-        def step(name, p):
-            if name == "middle":
-                kept_mem.start()
+        mem_copies = row_exchange(back, (d_mem,), (bmem,), pos)
+        tok_copies = row_exchange(back, (d_tok,), (btok,), pos)
+        kept_mem, kept_tok = own_rows(d_mem, bmem, pos, sem.at[2]), own_rows(d_tok, btok, pos, sem.at[3])
+        work.begin(batches[0])
+        shares = {("cross", LATE): ((0, 1), (2, 3)), ("cross", 0): ((4, 5), (6, 7), (8, 9), (10, 11))}
+        shares["self", 0] = ((12, 13), (14, 15), (16,), (17,), (18,), (19,))
+
+        def step(name, p, first, last):
+            if name in ("late", "middle", "last"):
                 settle(len(puts))
-                batches[1][0]()
+                if name == "middle":
+                    kept_mem.start()
+                work.begin(batches[("late", "middle", "last").index(name) + 1])
                 return
-            for k, part in enumerate(first if name == "cross" else second):
-
-                @pl.when(p == k)
-                def _(part=part, k=k):
+            for k, share in enumerate(shares[name, first]):
+
+                @pl.when(p == first + k)
+                def _(share=share, k=k):
                     if name == "self":
                         for c in mem_copies[3 * k : 3 * k + 3]:
                             back.start(c)
-                    run(part)
-
-    for c in loads:
-        c.wait()
+                    for t in share:
+                        run_slot(slots[t])
+
+    g2, aux, qc, kvc, att2, lse2, mem, x1, att1, qkv, lse1, tok = lazy_v
     attention_backward(
-        tok, mem, aux, win_v, wout_v, *ins, d_mem, d_tok, d_gains, dist, *scratch, emit=emit, step=step
+        tok, mem, aux, gains, table, qkv, att1, lse1, x1, qc, kvc, att2, lse2, g2,
+        d_mem, d_tok, d_gains, dist, *scratch, weight=weight, need=need, emit=emit, step=step,
     )
     early[...] = jnp.zeros_like(early)
     early[0:2, :] = d_gains[0:2, :]
     early[2:3, :] = gain_three[...]
     early[8:24, 0:384] = rel_sums(dist[...], hot_dist[...], mode_rows[...])
-    settle(len(puts))
     if not boxed:
+        settle(len(puts))
         return
     kept_tok.start()
-    links[1].drain()
-    batches[3][0]()
-    run(rest)
     turns = total_steps(back, early, early_room)
-    last = batches[3][1:]
-    for k, part in enumerate(last):
-        part()
+    for k, slot in enumerate(slots[20:]):
+        run_slot(slot)
+        for c in tok_copies[3 * k : 3 * k + 3]:
+            back.start(c)
         if k < len(turns):
             turns[k]()
-        for c in tok_copies[3 * k : 3 * k + 3]:
-            back.start(c)
     where = me * 2 + g
     sums[...] = block_sums(part_in[...], part_out[...], rows_out[...], where * 272, where * 112)
     run(total_steps(back, sums, room))
@@ -1186,31 +1295,30 @@
         c.wait_recv()
     kept_mem.wait()
     kept_tok.wait()
-    for k in range(2, 5):
-        links[k].drain()
-
-
-def backward_call(boxed, tok, mem, aux, win, wout, gains, table, kept, g2, g_win, g_wout, *more):
+    for each in links:
+        each.drain()
+
+
+def backward_call(boxed, g_win, g_wout, win, wout, lazy, *more):
     f32, bf16 = jnp.float32, jnp.bfloat16
     vm, dma = pltpu.VMEM, pltpu.SemaphoreType.DMA
     row = sds((SEQ, WIDTH))
-    rows = [vm((SEQ, WIDTH), bf16), vm((SEQ, WIDTH), bf16)]
     scratch = [vm((8, WIDTH), f32), vm((16, 384), f32)]
     scratch += [
         vm((SEQ, HEAD_COLS), bf16), vm((SEQ, 3 * HEAD_COLS), bf16), vm((2, 128, SEQ), f32), vm((2, 128, 384), f32),
-        vm((3, HEAD_COLS, WIDTH), bf16), dma((8,)),
+        vm((2, HEAD_COLS, WIDTH), bf16), dma((9,)), vm((3, HEAD_COLS, WIDTH), bf16), dma((len(BACK_BLOCKS),)),
+        dma((len(lazy),)), dma((4,)),
     ]
-    scratch += WEIGHTS[:2] + [dma((4,))]
+    scratch += [vm(v.shape, v.dtype) for v in lazy]
     outs = [sds(g_win.shape), sds(g_wout.shape)]
     if boxed:
-        items, both = 4 * len(PIECES), 2 * REGION
-        chunks = sds((16, SEQ // 16, WIDTH))
-        outs += [sds((272, WIDTH), f32), sds((112, WIDTH), f32), sds((8, WIDTH), f32), sds((24, WIDTH), f32), chunks, chunks]
+        items, both = 4 * len(PIECES), 4 * 384
+        outs += [sds((272, WIDTH), f32), sds((112, WIDTH), f32), sds((8, WIDTH), f32), sds((24, WIDTH), f32), row, row]
         specs = (anywhere(),) * 2 + (whole(),) * 4 + (anywhere(),) * 2
-        scratch = rows + scratch
+        scratch = [vm((SEQ, WIDTH), bf16), vm((SEQ, WIDTH), bf16)] + scratch
         scratch += [
             vm((4, both, WIDTH), bf16), vm((4, both, WIDTH), bf16), vm((2, both, WIDTH), bf16),
-            vm((1, both, WIDTH), bf16), vm((2, 4 * 384, WIDTH), bf16), vm((6, 8, WIDTH), f32), vm((6, 24, WIDTH), f32),
+            vm((1, both, WIDTH), bf16), vm((6 * 384, WIDTH), bf16), vm((6, 8, WIDTH), f32), vm((6, 24, WIDTH), f32),
             dma((12 * items + 48,)), dma((12 * items + 48,)), dma((4 * items,)),
         ]
     else:
@@ -1221,11 +1329,11 @@
         functools.partial(backward_kernel, boxed),
         out_shape=tuple(outs),
         scratch_shapes=scratch,
-        in_specs=[anywhere()] * 2 + [whole()] * 3 + [anywhere()] * 2 + [whole()] * 15,
+        in_specs=[anywhere()] * (4 + len(lazy)) + [whole()] * len(more),
         out_specs=specs,
         input_output_aliases={0: 0, 1: 1},
         compiler_params=pltpu.CompilerParams(vmem_limit_bytes=VMEM_BYTES, **extra),
-    )(g_win, g_wout, tok, mem, aux, win, wout, gains, table, *kept, g2, *more)
+    )(g_win, g_wout, win, wout, *lazy, *more)
 
 
 def body(
@@ -1246,36 +1354,38 @@
     lane = np.arange(256)
     dist_f = np.where(lane <= 128, 128 - lane, 384 - lane)
     hot_t = jnp.asarray(np.concatenate([hot[dist_f], hot], axis=0).T)
-    tok_s, mem_s, aux_s, win_sh, wout_sh, tables, keep = prep_call(
-        ids, row_source, denoiser_modes, tokens, memory, segments, memory_segments, w_in, w_out, rel_bias, hot_t, sentinel
+    w_in_t, rel_t = w_in.T, jnp.swapaxes(rel_bias, 1, 2)
+    tok_s, mem_s, aux_s, win_sh, wout_sh, table_f, table_b, keep, mode_rows = prep_call(
+        ids, row_source, denoiser_modes, tokens, memory, segments, memory_segments, w_in_t, w_out, rel_t, hot_t, sentinel
     )
     if boxed:
-        win, wout, tok, mem, aux = gather_all(win_sh, wout_sh, tok_s, mem_s, aux_s)
+        flat = lambda v: v.reshape(SEQ, v.shape[-1])
+        win, wout, tok, mem, aux, *kept = forward_call(
+            True, win_sh, wout_sh, flat(tok_s), flat(mem_s), flat(aux_s), norm_gains, table_f
+        )
     else:
         win = lax.all_gather(win_sh, ("dp", "group"), axis=0, tiled=True)
         wout = lax.all_gather(wout_sh, ("dp", "group"), axis=0, tiled=True)
         tok, mem, aux = (
-            lax.all_to_all(v, "dp", split_axis=0, concat_axis=0, tiled=True) for v in (tok_s, mem_s, aux_s)
+            lax.all_to_all(v, "dp", split_axis=0, concat_axis=0, tiled=True).reshape(SEQ, v.shape[-1])
+            for v in (tok_s, mem_s, aux_s)
         )
-    tok, mem, aux = tok.reshape(SEQ, WIDTH), mem.reshape(SEQ, WIDTH), aux.reshape(SEQ, 128)
-
-    table_f, table_b = tables[:, :256], tables[:, 256:]
-    kept = forward_call(tok, mem, aux, win, wout, norm_gains, table_f)
+        kept = forward_call(False, tok, mem, aux, win, wout, norm_gains, table_f)
     x2 = kept[8]
     mixed, g2, d_gain_three, g_win, g_wout = ff_call(
         x2, cotangent.reshape(SEQ, WIDTH), keep, norm_gains, win, wout
     )
     hot_dist = np.concatenate([hot, np.repeat(np.eye(BUCKETS, dtype=np.float32)[-1:], 128, axis=0)], axis=0)
     hot_dist = jnp.asarray(np.pad(hot_dist, ((0, 0), (0, 128 - BUCKETS))))
-    own_mode = denoiser_modes[row_source[my_place]]
-    mode_rows = jnp.broadcast_to((own_mode == jnp.arange(8)).astype(jnp.float32)[:, None], (8, 128))
     rows_out_up = rows_out.reshape(-1, 1)
+    qkv, att1, lse1, x1, qc, kvc, att2, lse2, _ = kept
+    lazy = (g2, aux, qc, kvc, att2, lse2, mem, x1, att1, qkv, lse1, tok)
     result = backward_call(
-        boxed, tok, mem, aux, win, wout, norm_gains, table_b, kept[:8], g2, g_win, g_wout,
-        hot_dist, mode_rows, d_gain_three, rows_out_up,
+        boxed, g_win, g_wout, win, wout, lazy, norm_gains, table_b, hot_dist, mode_rows, d_gain_three, rows_out_up
     )
     if boxed:
         _, _, part_in_t, part_out, sums, early, back_tok, back_mem = result
+        back_tok, back_mem = back_tok.reshape(tok_s.shape), back_mem.reshape(mem_s.shape)
     else:
         g_win, g_wout, d_mem, d_tok, early = result
         back_tok, back_mem = (
@@ -1294,11 +1404,12 @@
         d_tokens, d_memory, grad_in, grad_out, grad_gains, grad_rel, new_in, new_out, new_gains, new_rel,
         rows_in_new, cols_in_new, rows_out_new, cols_out_new, sq_gains_new, sq_rel_new,
     ) = update_call(
-        ids, row_source, part_in_t, part_out, sums, early, back_tok, back_mem, w_in, w_out, norm_gains, rel_bias,
-        rows_in, cols_in.reshape(1, -1), rows_out_up, cols_out, sq_gains, sq_rel,
+        ids, row_source, part_in_t, part_out, sums, early, back_tok, back_mem, w_in_t, w_out, norm_gains, rel_t,
+        rows_in, cols_in.reshape(-1, 1), rows_out_up, cols_out, sq_gains, jnp.swapaxes(sq_rel, 1, 2),
     )
+    grad_rel, new_rel, sq_rel_new = (jnp.swapaxes(v, 1, 2) for v in (grad_rel, new_rel, sq_rel_new))
     return (
-        mixed[None], d_tokens, d_memory, grad_in, grad_out, grad_gains, grad_rel, new_in, new_out, new_gains,
+        mixed[None], d_tokens, d_memory, grad_in.T, grad_out, grad_gains, grad_rel, new_in.T, new_out, new_gains,
         new_rel, rows_in_new, cols_in_new.reshape(-1), rows_out_new.reshape(-1), cols_out_new, sq_gains_new,
         sq_rel_new,
     )

time: 462 us -> 349 us (0.76)
  Pallas kernels: 432 us -> 336 us
  local copies, waits for them, and re-layouts: 15.9 us -> 1.49 us
    pallas_call x1, Pallas kernels: 215 us -> 156 us  [backward_call(): pl.pallas_call(functools.partial(backward_kernel, boxed), out_shape=tuple...]
    pallas_call x2 -> x1, Pallas kernels: 182 us -> 146 us  [forward_call(): pl.pallas_call(functools.partial(forward_kernel, boxed), out_shape=outs,...]
    unnamed x28 -> x4, local copies, waits for them, and re-layouts: 11.5 us -> 0.01 us
where the time goes in v3:
time: 349 us; the launch traced here: 342 us
  Pallas kernels  336 us (96%)
  other arithmetic  3.75 us (1%)
    pallas_call x1, Pallas kernels, backward_call(): pl.pallas_call(functools.partial(backward_kernel, boxed), out_shape=tuple...  156 us
    pallas_call x1, Pallas kernels, forward_call(): pl.pallas_call(functools.partial(forward_kernel, boxed), out_shape=outs,...  146 us
    pallas_call x1, Pallas kernels, ff_call(): vmem_call(ff_kernel, (sds((SEQ, WIDTH)), sds((SEQ, WIDTH), f32), sds((1,...  24.8 us

profile of v3, /device:TPU:0, one launch (start us, length us, event | category | flops | bytes accessed | tf_op | source)
XLA Modules:
  0.0 342.4 jit_solution(4735769460102968952)
XLA Ops:
  0.7 0.7 pad_add_fusion.ids
  1.3 4.7 %shard_map.323 = (bf16[16,32,768]{2,1,0:T(8,128)(2,1)}, bf16[16,32,768]{2,1,0:T(8,128)(2,1)}, bf16[16,32,128]{2,1,0:T(8,128)(2,1)}, bf16[272,768]{1,0:T(8,128)(2...) custom-call(s32[3]{0:T(128)} %pad_add_fusion.ids, ...), custom_call_target="tpu_custom_call" | custom-call | tf_op jit(solution)/shard_map/pallas_call | solution.py:908
  6.0 146.1 %shard_map.324 = (bf16[8704,768]{1,0:T(8,128)(2,1)}, bf16[3584,768]{1,0:T(8,128)(2,1)}, bf16[512,768]{1,0:T(8,128)(2,1)}, bf16[512,768]{1,0:T(8,128)(2,1)}, bf16...) custom-call(bf16[272,768]{1,0:T(8,128)(2,1)} %get-tuple-element.67.r, ...), custom_call_target="tpu_custom_call" | custom-call | tf_op jit(solution)/shard_map/pallas_call | solution.py:1127
  152.1 0.0 copy-start.1
  152.1 24.8 %shard_map.325 = (bf16[512,768]{1,0:T(8,128)(2,1)}, f32[512,768]{1,0:T(8,128)}, f32[1,768]{1,0:T(1,128)}, bf16[8704,768]{1,0:T(8,128)(2,1)}, bf16[3584,768]{1,0:T(8,128)(2,1)}) custom-call(f32[512,768]{1,0:T(8,128)} %get-tuple-element.73.x2, bf16[512,768]{1,0:T(8,128)(2,1)} %bitcast.24, f32[512,128]{1,0:T(8,128)} %get-tuple-element.74.keep, f32[3,768]{1,0:T(4,128)} %gains.3, ...), custom_call_target="tpu_custom_call" | custom-call | tf_op jit(solution)/shard_map/pallas_call | solution.py:1144
  176.9 0.0 copy-done.1
  176.9 0.7 copy.41.refs_17_.rows_out
  177.6 0.0 copy-start
  177.6 156.1 %shard_map.326 = (bf16[8704,768]{1,0:T(8,128)(2,1)}, bf16[3584,768]{1,0:T(8,128)(2,1)}, f32[272,768]{1,0:T(8,128)}, f32[112,768]{1,0:T(8,128)}, f32[8,768]{1,0:T...) custom-call(bf16[8704,768]{1,0:T(8,128)(2,1)} %get-tuple-element.78., ...), custom_call_target="tpu_custom_call", output_to_operand_aliasing={{0}: (0, {}), {1}: (1, {})} | custom-call | tf_op jit(solution)/shard_map/pallas_call | solution.py:1328
  333.8 0.0 copy-done
  333.8 0.8 reshape.74.cols_in
  334.6 4.5 %shard_map.327 = (bf16[16,32,768]{2,1,0:T(8,128)(2,1)}, bf16[16,32,768]{2,1,0:T(8,128)(2,1)}, f32[272,768]{1,0:T(8,128)}, f32[112,768]{1,0:T(8,128)}, f32[3,768]...) custom-call(s32[3]{0:T(128)} %pad_add_fusion.ids, ...), custom_call_target="tpu_custom_call" | custom-call | tf_op jit(solution)/shard_map/pallas_call | solution.py:980
  339.1 1.6 reduce
  340.7 1.4 reduce.1
Async XLA Ops:
  152.1 24.8 %copy-start.1 = (f32[112]{0:T(128)S(1)}, f32[112]{0:T(128)}, u32[]{:S(2)}) copy-start(f32[112]{0:T(128)} %param.34) | copy-start | bytes 1348
  177.6 156.2 %copy-start = (f32[272]{0:T(512)S(1)}, f32[272]{0:T(512)}, u32[]{:S(2)}) copy-start(f32[272]{0:T(512)} %param.33) | copy-start | bytes 3268
